TPU v7x, 512 devices: a whole 4x4x16 slice. The times are simulated.
512 devices in a mesh: client: 32 (over z_hi, x, core), tensor: 16 (over z_lo, y).
Axes of the slice: x: 4, y: 4, z: 16 (z_hi: 4, z_lo: 4; z = z_hi * 4 + z_lo), core: 2. Of those that a mesh axis runs over, the one named last changes fastest.
Arguments:
- tokens: bfloat16 [8192, 8192], P('client', 'tensor'), may hold values from -40 to 40, as said below
- norm_gain: float32 [8192], replicated, may hold values from 0.25 to 1.75
- base_weight: bfloat16 [8192, 8192], P('client', 'tensor'), may hold values from -0.0625 to 0.0625
- factor_a: bfloat16 [2048, 8192], P(('client', 'tensor')), may hold values from -0.0625 to 0.0625
- factor_b: bfloat16 [8192, 2048], P('tensor', 'client'), may hold values from -0.0625 to 0.0625
Outputs:
- query: bfloat16 [8192, 8192], P('client', 'tensor')
Inputs may be any that keep to these rules, and one draw needn't show every extreme that they name: tokens: real-valued hidden states.
All inputs are finite; a program needn't handle non-finite values.
Results may differ from a plain program's by a relative error of at most 0.014.
Values may be sent and summed in bfloat16 or wider, within the bound.
No kernel may reach another device: no remote copies, remote signals or barrier semaphores. Data moves between devices by JAX's collectives and lax.ppermute only.
A program may use at most 64 MiB of HBM per device.

v0:
```python
import jax
import jax.numpy as jnp
from jax import lax
from jax.sharding import PartitionSpec as P

adapter_scale = 2.0
norm_epsilon = 1e-05


def local(tokens, norm_gain, base_weight, factor_a, factor_b):
    up_stack = lax.all_gather(factor_b, "client", axis=1, tiled=True)
    client_rows = lax.all_gather(factor_a, "tensor", axis=0, tiled=True)
    columns = lax.all_to_all(client_rows, "client", split_axis=1, concat_axis=0, tiled=True)
    factor_product = lax.dot_general(
        columns, up_stack, (((0,), (1,)), ((), ())), preferred_element_type=jnp.float32
    )
    update_rows = (adapter_scale * factor_product).astype(jnp.bfloat16)
    shard_merged = (base_weight.astype(jnp.float32) + update_rows.astype(jnp.float32)).astype(
        jnp.bfloat16
    )
    merged = lax.all_gather(shard_merged, "client", axis=0, tiled=True)
    whole = lax.all_gather(tokens, "tensor", axis=1, tiled=True)
    values = whole.astype(jnp.float32)
    mean_square = jnp.mean(values * values, axis=-1, keepdims=True)
    normed = (values * lax.rsqrt(mean_square + norm_epsilon) * norm_gain).astype(jnp.bfloat16)
    query = jnp.dot(normed, merged, preferred_element_type=jnp.float32)
    return query.astype(jnp.bfloat16)


def solution(mesh):
    return jax.shard_map(
        local,
        mesh=mesh,
        in_specs=(
            P("client", "tensor"),
            P(),
            P("client", "tensor"),
            P(("client", "tensor"), None),
            P("tensor", "client"),
        ),
        out_specs=P("client", "tensor"),
        check_vma=False,
    )
```

profile of v0, /device:TPU:1, one launch (start us, length us, event | category | flops | bytes accessed | tf_op | source)
XLA Modules:
  0.0 458.9 jit_solution(7723586876464009440)
XLA Ops:
  6.5 0.0 copy-start
  6.5 0.0 all-gather.12.cloned.1.call-start
  6.5 0.7 all-gather.12.cloned.1.call-update
  7.3 0.0 all-gather.8.cloned.1.call-start
  7.3 0.7 all-gather.8.cloned.1.call-update
  8.0 0.0 all-gather.6.cloned.1.call-start
  8.1 0.7 all-gather.6.cloned.1.call-update
  8.7 82.4 %all-gather.12.cloned.1.call-done = bf16[16,4,8192]{2,1,0:T(4,128)(2,1)} async-done(((bf16[1,4,8192]{2,1,0:T(4,128)(2,1)}), bf16[16,4,8192]{2,1,0:T(4,128)(2,1)}) %all-gather.12.cloned.1.call-update) | async-done | bytes 1048592 | tf_op jit(solution)/shard_map/all_gather | solution.py:12
  91.1 1.8 all_to_all.14
  92.9 1.6 copy.7
  94.5 24.4 %all-to-all-start = ((bf16[64,32,256]{2,0,1:T(8,128)(2,1)}), bf16[64,32,256]{2,0,1:T(8,128)(2,1)S(1)}, u32[]{:S(2)}, u32[]{:S(2)}) async-start(bf16[64,32,256]{2,0,1:T(8,128)(2,1)} %copy.7), calls=%async_computation | async-start | bytes 2097152 | tf_op jit(solution)/shard_map/all_to_all | solution.py:13
  118.9 0.0 all-gather.10.cloned.1.call-start
  118.9 98.7 %all-gather.8.cloned.1.call-done = bf16[512,2048]{0,1:T(8,128)(2,1)} async-done(((bf16[512,64]{0,1:T(8,128)(2,1)}), bf16[512,2048]{0,1:T(8,128)(2,1)}) %all-gather.8.cloned.1.call-update) | async-done | bytes 2097168 | tf_op jit(solution)/shard_map/all_gather | solution.py:11
  217.7 0.0 all-to-all-done
  217.7 3.0 fusion.13
  220.7 0.0 all-gather.10.cloned.1.call-update
  220.7 77.8 %all-gather.6.cloned.1.call-done = bf16[256,8192]{1,0:T(8,128)(2,1)} async-done(((bf16[256,512]{1,0:T(8,128)(2,1)}), bf16[256,8192]{1,0:T(8,128)(2,1)}) %all-gather.6.cloned.1.call-update) | async-done | bytes 4194320 | tf_op jit(solution)/shard_map/all_gather | solution.py:22
  298.5 3.1 fusion
  301.6 143.0 %all-gather.10.cloned.1.call-done = bf16[8192,512]{1,0:T(8,128)(2,1)} async-done(((bf16[256,512]{1,0:T(8,128)(2,1)}), bf16[8192,512]{1,0:T(8,128)(2,1)}) %all-gather.10.cloned.1.call-update) | async-done | bytes 8388624 | tf_op jit(solution)/shard_map/all_gather | solution.py:21
  444.6 0.0 copy-done
  444.6 7.7 %fusion.7 = bf16[256,512]{1,0:T(8,128)(2,1)} fusion(bf16[8192,512]{1,0:T(8,128)(2,1)} %all-gather.10.cloned.1.call-done, bf16[256,8192]{1,0:T(8,128)(2,1)} %all-gather.6.cloned.1.call-done, f32[8192]{0:T(1024)S(1)} %copy-done, f32[256]{0:T(256)S(1)} %add_rsqrt_fusion), kind=kOutput, calls=%fused_computation.9 | convolution fusion | flops 2156003328 | bytes 12878848 | tf_op jit(solution)/shard_map/dot_general | solution.py:26
  (1 shorter events, 0.0 us)
Async XLA Ops:
  6.5 438.0 %copy-start = (f32[8192]{0:T(1024)S(1)}, f32[8192]{0:T(1024)}, u32[]{:S(2)}) copy-start(f32[8192]{0:T(1024)} %param.6) | copy-start | bytes 98308
  6.5 84.6 %all-gather.12.cloned.1.call-start = ((), (), s32[]{:S(2)}) async-start(), calls=%async_computation.4 | async-start | bytes 1114112 | tf_op jit(solution)/shard_map/all_gather | solution.py:12
  7.3 210.4 %all-gather.8.cloned.1.call-start = ((), (), s32[]{:S(2)}) async-start(), calls=%async_computation.2 | async-start | bytes 2162688 | tf_op jit(solution)/shard_map/all_gather | solution.py:11
  8.0 290.5 %all-gather.6.cloned.1.call-start = ((), (), s32[]{:S(2)}) async-start(), calls=%async_computation.1 | async-start | bytes 4456448 | tf_op jit(solution)/shard_map/all_gather | solution.py:22
  94.5 123.2 %all-to-all-start = ((bf16[64,32,256]{2,0,1:T(8,128)(2,1)}), bf16[64,32,256]{2,0,1:T(8,128)(2,1)S(1)}, u32[]{:S(2)}, u32[]{:S(2)}) async-start(bf16[64,32,256]{2,0,1:T(8,128)(2,1)} %copy.7), calls=%async_computation | async-start | bytes 2097152 | tf_op jit(solution)/shard_map/all_to_all | solution.py:13
  118.9 325.7 %all-gather.10.cloned.1.call-start = ((), (), s32[]{:S(2)}) async-start(), calls=%async_computation.3 | async-start | bytes 8650752 | tf_op jit(solution)/shard_map/all_gather | solution.py:21
Sparse Core Ops, SparseCore 0:
  9.4 81.6 all-gather.11
  94.2 123.3 all-gather.7
  219.8 78.6 all-gather.5
  301.5 143.0 all-gather.9
where the time goes:
time: 459 us
  waiting for transfers between devices  404 us (88%)
  starting transfers between devices  24.5 us (5%)
  between operations  13.1 us (3%)
  matrix products  10.8 us (2%)
    all_gather x1, waiting for transfers between devices, local(): merged = lax.all_gather(shard_merged, 'client', axis=0, tiled=True)  143 us
    all_gather x1, waiting for transfers between devices, local(): up_stack = lax.all_gather(factor_b, 'client', axis=1, tiled=True)  98.7 us
    all_gather x1, waiting for transfers between devices, local(): client_rows = lax.all_gather(factor_a, 'tensor', axis=0, tiled=True)  82.4 us
    all_gather x1, waiting for transfers between devices, local(): whole = lax.all_gather(tokens, 'tensor', axis=1, tiled=True)  77.8 us
    all_to_all x1, starting transfers between devices, local(): lax.all_to_all(client_rows, 'client', split_axis=1, concat_axis=0, tiled=...  24.4 us
  transfers between devices with their start and end apart: 5, of which 4 were waited for; matrix products, arithmetic and copies ran while one was open for 2% of the time, Pallas kernels for 0%

commit v1 on v0

v1 whole, which is shorter than its diff:
```python
import jax
import jax.numpy as jnp
from jax import lax
from jax.sharding import Mesh, PartitionSpec as P

adapter_scale = 2.0
norm_epsilon = 1e-05
width = 8192

f32 = jnp.float32
bf16 = jnp.bfloat16


def spread(block, axes, count):
    copies = jnp.broadcast_to(block[None], (count,) + block.shape)
    return lax.all_to_all(copies, axes, split_axis=0, concat_axis=0)


def swap(block):
    return lax.ppermute(block, "core", [(0, 1), (1, 0)])


def turn(block, axis, step):
    return lax.ppermute(block, axis, [(i, (i + step) % 4) for i in range(4)])


def local(tokens, norm_gain, base_weight, factor_a, factor_b):
    core = lax.axis_index("core")
    z_hi = lax.axis_index("z_hi")
    client = (z_hi * 4 + lax.axis_index("x")) * 2 + core

    keep = lax.dynamic_slice_in_dim(tokens, core * 256, 256, axis=1)
    give = lax.dynamic_slice_in_dim(tokens, (1 - core) * 256, 256, axis=1)
    pair = jnp.concatenate([keep, swap(give)], axis=0)
    rows = lax.all_gather(pair, ("z_lo", "y"), axis=1, tiled=True)

    up = factor_b.T
    up = spread(up, "z_hi", 4)
    up = spread(up, "x", 4)
    down = factor_a.reshape(4, 16, 512).transpose(1, 0, 2)
    down = lax.all_to_all(down, ("z_hi", "x"), split_axis=0, concat_axis=0)
    down = spread(down, "z_lo", 4)
    down = spread(down, "y", 4)
    up = up.reshape(4, 4, 4, 4, 4, 512).transpose(3, 2, 1, 0, 4, 5).reshape(1024, 512)
    down = down.reshape(1024, 512)
    part = lax.dot_general(down, up, (((0,), (0,)), ((), ())), preferred_element_type=f32)
    mine = lax.dynamic_slice_in_dim(part, core * 256, 256, axis=0)
    other = lax.dynamic_slice_in_dim(part, (1 - core) * 256, 256, axis=0).astype(bf16)
    update = mine + swap(other).astype(f32)
    gain = lax.dynamic_slice_in_dim(norm_gain, client * 256, 256)[:, None]
    weight = (gain * (base_weight.astype(f32) + adapter_scale * update)).astype(bf16)

    blocks = [weight] + [turn(weight, "z_hi", step) for step in (1, 3, 2)]
    wide = [spread(block, "x", 4) for block in blocks]

    squares = rows.astype(f32)
    squares = jnp.sum(squares * squares, axis=1)
    total = squares[:256] + swap(squares[256:])
    scale = lax.rsqrt(total / width + norm_epsilon)

    acc = None
    for step, block in zip((0, 1, 3, 2), wide):
        source = lax.rem(z_hi + 4 - step, 4)
        left = lax.dynamic_slice_in_dim(rows, source * 1024, 1024, axis=1)
        term = jnp.dot(left, block.reshape(1024, 512), preferred_element_type=f32)
        acc = term if acc is None else acc + term
    query = acc[:256] + swap(acc[256:].astype(bf16)).astype(f32)
    return (query * scale[:, None]).astype(bf16)


def solution(mesh):
    fine = Mesh(mesh.devices.reshape(4, 4, 2, 4, 4), ("z_hi", "x", "core", "z_lo", "y"))
    client, tensor = ("z_hi", "x", "core"), ("z_lo", "y")
    return jax.shard_map(
        local,
        mesh=fine,
        in_specs=(
            P(client, tensor),
            P(),
            P(client, tensor),
            P(client + tensor, None),
            P(tensor, client),
        ),
        out_specs=P(client, tensor),
        check_vma=False,
    )
```

time: 459 us -> 269 us (0.59)
  the two profiles are of different devices: /device:TPU:1 before, /device:TPU:9 now
where the time goes in v1:
time: 269 us; the launch traced here: 268 us
  starting transfers between devices  90 us (33%)
  waiting for transfers between devices  73.7 us (27%)
  blocking collectives  65.2 us (24%)
  between operations  13.6 us (5%)
  local copies, waits for them, and re-layouts  12 us (4%)
  matrix products  10.2 us (4%)
  other arithmetic  3.58 us (1%)
    ppermute x3, waiting for transfers between devices, turn(): return lax.ppermute(block, axis, [(i, (i + step) % 4) for i in range(4)])  45.1 us
    all_to_all x6, starting transfers between devices, spread(): return lax.all_to_all(copies, axes, split_axis=0, concat_axis=0)  39.4 us
    ppermute x3, starting transfers between devices, turn(): return lax.ppermute(block, axis, [(i, (i + step) % 4) for i in range(4)])  36.1 us
    all_to_all x2, blocking collectives, spread(): return lax.all_to_all(copies, axes, split_axis=0, concat_axis=0)  34.1 us
    all_to_all x1, blocking collectives, local(): down = lax.all_to_all(down, ('z_hi', 'x'), split_axis=0, concat_axis=0)  31.1 us
    all_to_all x6, waiting for transfers between devices, spread(): return lax.all_to_all(copies, axes, split_axis=0, concat_axis=0)  26.1 us
    ppermute x4, starting transfers between devices, swap(): return lax.ppermute(block, 'core', [(0, 1), (1, 0)])  14.5 us
    dot_general x4, matrix products, local(): term = jnp.dot(left, block.reshape(1024, 512), preferred_element_type=f32)  9.5 us
  transfers between devices with their start and end apart: 14, of which 9 were waited for; matrix products, arithmetic and copies ran while one was open for 8% of the time, Pallas kernels for 0%

profile of v1, /device:TPU:9, one launch (start us, length us, event | category | flops | bytes accessed | tf_op | source)
XLA Modules:
  0.0 268.3 jit_solution(3958100973337401707)
XLA Ops:
  7.5 2.6 collective-permute-start
  11.8 31.1 %all_to_all.45 = bf16[16,4,512]{2,1,0:T(4,128)(2,1)S(1)} all-to-all(bf16[16,4,512]{2,1,0:T(4,128)(2,1)} %bitcast.23), channel_id=1, replica_groups=mesh['z_hi'=4,'x'=4,'core'=2,'z_lo'=4,'y'=4] {'z_hi','x'}, dimensions={0} | all-to-all | bytes 131072 | tf_op jit(solution)/shard_map/all_to_all | solution.py:41
  43.8 18.9 %all_to_all.46 = bf16[4,64,512]{2,1,0:T(8,128)(2,1)S(1)} all-to-all(bf16[4,64,512]{2,1,0:T(8,128)(2,1)S(1)} %broadcast_in_dim.18), channel_id=1, replica_groups=mesh['z_hi'=4,'x'=4,'core'=2,'z_lo'=4,'y'=4] {'z_hi'}, dimensions={0} | all-to-all | bytes 524288 | tf_op jit(solution)/shard_map/all_to_all | solution.py:16
  63.5 5.6 %all-to-all-start.1 = ((bf16[4,16,4,512]{3,2,1,0:T(4,128)(2,1)}), bf16[4,16,4,512]{3,2,1,0:T(4,128)(2,1)S(1)}, u32[]{:S(2)}, u32[]{:S(2)}) async-start(bf16[4,16,4,512]{3,2,1,0:T(4,128)(2,1)} %broadcast_in_dim.16), calls=%async_computation.1 | async-start | bytes 524288 | tf_op jit(solution)/shard_map/all_to_all | solution.py:16
  69.3 5.5 %all-to-all-done.1 = bf16[4,16,4,512]{3,2,1,0:T(4,128)(2,1)S(1)} async-done(((bf16[4,16,4,512]{3,2,1,0:T(4,128)(2,1)}), bf16[4,16,4,512]{3,2,1,0:T(4,128)(2,1)S(1)}, u32[]{:S(2)}, u32[]{:S(2)}) %all-to-all-start.1) | async-done | bytes 262176 | tf_op jit(solution)/shard_map/all_to_all | solution.py:16
  75.1 15.2 %all_to_all.47 = bf16[4,4,64,512]{3,1,2,0:T(4,128)(2,1)S(1)} all-to-all(bf16[4,4,64,512]{3,1,2,0:T(4,128)(2,1)S(1)} %broadcast_in_dim.19), channel_id=1, replica_groups=mesh['z_hi'=4,'x'=4,'core'=2,'z_lo'=4,'y'=4] {'x'}, dimensions={0} | all-to-all | bytes 2097152 | tf_op jit(solution)/shard_map/all_to_all | solution.py:16
  90.3 1.4 broadcast_in_dim.17
  91.7 17.6 %all-to-all-start.2 = ((bf16[4,4,16,4,512]{4,3,2,1,0:T(4,128)(2,1)}), bf16[4,4,16,4,512]{4,3,2,1,0:T(4,128)(2,1)S(1)}, u32[]{:S(2)}, u32[]{:S(2)}) async-start(bf16[4,4,16,4,512]{4,3,2,1,0:T(4,128)(2,1)} %broadcast_in_dim.17), calls=%async_computation.2 | async-start | bytes 2097152 | tf_op jit(solution)/shard_map/all_to_all | solution.py:16
  110.2 13.4 %all-to-all-done.2 = bf16[4,4,16,4,512]{4,3,2,1,0:T(4,128)(2,1)S(1)} async-done(((bf16[4,4,16,4,512]{4,3,2,1,0:T(4,128)(2,1)}), bf16[4,4,16,4,512]{4,3,2,1,0:T(4,128)(2,1)S(1)}, u32[]{:S(2)}, u32[]{:S(2)}) %all-to-all-start.2) | async-done | bytes 1048608 | tf_op jit(solution)/shard_map/all_to_all | solution.py:16
  124.6 6.4 %collective-permute-start.1 = (bf16[256,512]{1,0:T(8,128)(2,1)S(1)}, bf16[256,512]{1,0:T(8,128)(2,1)S(1)}, u32[]{:S(2)}, u32[]{:S(2)}) collective-permute-start(bf16[256,512]{1,0:T(8,128)(2,1)S(1)} %dynamic-slice_convert_fusion), channel_id=1, source_target_pairs={{0,16},{16,0},{1,17},{17,1},{2,18},{18,2},{3,19},{19,3},{4,20},{20... | collective-permute-start | bytes 786440 | tf_op jit(solution)/shard_map/ppermute | solution.py:20
  132.2 1.2 multiply_convert_fusion
  134.4 3.6 %all-to-all-start.5 = ((bf16[4,256,512]{2,1,0:T(8,128)(2,1)}), bf16[4,256,512]{2,1,0:T(8,128)(2,1)S(1)}, u32[]{:S(2)}, u32[]{:S(2)}) async-start(bf16[4,256,512]{2,1,0:T(8,128)(2,1)} %broadcast_in_dim.20), calls=%async_computation.5 | async-start | bytes 2097152 | tf_op jit(solution)/shard_map/all_to_all | solution.py:16
  138.1 3.9 %collective-permute-start.2 = (bf16[256,512]{1,0:T(8,128)(2,1)S(1)}, bf16[256,512]{1,0:T(8,128)(2,1)S(1)}, u32[]{:S(2)}, u32[]{:S(2)}) collective-permute-start(bf16[256,512]{1,0:T(8,128)(2,1)S(1)} %multiply_convert_fusion), channel_id=1, source_target_pairs={{0,128},{128,256},{256,384},{384,0},{1,129},{129,257},{257,385},{3... | collective-permute-start | bytes 786440 | tf_op jit(solution)/shard_map/ppermute | solution.py:24
  142.0 16.7 %collective-permute-done.2 = bf16[256,512]{1,0:T(8,128)(2,1)S(1)} collective-permute-done((bf16[256,512]{1,0:T(8,128)(2,1)S(1)}, bf16[256,512]{1,0:T(8,128)(2,1)S(1)}, u32[]{:S(2)}, u32[]{:S(2)}) %collective-permute-start.2) | collective-permute-done | bytes 262176 | tf_op jit(solution)/shard_map/ppermute | solution.py:24
  158.7 1.1 broadcast_in_dim.21
  159.8 3.8 %all-to-all-start.6 = ((bf16[4,256,512]{2,1,0:T(8,128)(2,1)}), bf16[4,256,512]{2,1,0:T(8,128)(2,1)S(1)}, u32[]{:S(2)}, u32[]{:S(2)}) async-start(bf16[4,256,512]{2,1,0:T(8,128)(2,1)} %broadcast_in_dim.21), calls=%async_computation.6 | async-start | bytes 2097152 | tf_op jit(solution)/shard_map/all_to_all | solution.py:16
  163.6 15.0 %collective-permute-start.4 = (bf16[256,512]{1,0:T(8,128)(2,1)S(1)}, bf16[256,512]{1,0:T(8,128)(2,1)S(1)}, u32[]{:S(2)}, u32[]{:S(2)}) collective-permute-start(bf16[256,512]{1,0:T(8,128)(2,1)S(1)} %multiply_convert_fusion), channel_id=1, source_target_pairs={{0,256},{128,384},{256,0},{384,128},{1,257},{129,385},{257,1},{385... | collective-permute-start | bytes 786440 | tf_op jit(solution)/shard_map/ppermute | solution.py:24
  178.6 12.8 %collective-permute-done.4 = bf16[256,512]{1,0:T(8,128)(2,1)S(1)} collective-permute-done((bf16[256,512]{1,0:T(8,128)(2,1)S(1)}, bf16[256,512]{1,0:T(8,128)(2,1)S(1)}, u32[]{:S(2)}, u32[]{:S(2)}) %collective-permute-start.4) | collective-permute-done | bytes 262176 | tf_op jit(solution)/shard_map/ppermute | solution.py:24
  191.4 1.1 broadcast_in_dim.23
  192.5 4.5 %all-to-all-start.8 = ((bf16[4,256,512]{2,1,0:T(8,128)(2,1)}), bf16[4,256,512]{2,1,0:T(8,128)(2,1)S(1)}, u32[]{:S(2)}, u32[]{:S(2)}) async-start(bf16[4,256,512]{2,1,0:T(8,128)(2,1)} %broadcast_in_dim.23), calls=%async_computation.8 | async-start | bytes 2097152 | tf_op jit(solution)/shard_map/all_to_all | solution.py:16
  197.0 17.2 %collective-permute-start.3 = (bf16[256,512]{1,0:T(8,128)(2,1)S(1)}, bf16[256,512]{1,0:T(8,128)(2,1)}, u32[]{:S(2)}, u32[]{:S(2)}) collective-permute-start(bf16[256,512]{1,0:T(8,128)(2,1)S(1)} %multiply_convert_fusion), channel_id=1, source_target_pairs={{0,384},{128,0},{256,128},{384,256},{1,385},{129,1},{257,129},{385... | collective-permute-start | bytes 786440 | tf_op jit(solution)/shard_map/ppermute | solution.py:24
  214.2 15.6 %collective-permute-done.3 = bf16[256,512]{1,0:T(8,128)(2,1)} collective-permute-done((bf16[256,512]{1,0:T(8,128)(2,1)S(1)}, bf16[256,512]{1,0:T(8,128)(2,1)}, u32[]{:S(2)}, u32[]{:S(2)}) %collective-permute-start.3) | collective-permute-done | bytes 262176 | tf_op jit(solution)/shard_map/ppermute | solution.py:24
  229.9 2.2 broadcast_in_dim.22
  232.0 4.2 %all-to-all-start.7 = ((bf16[4,256,512]{2,1,0:T(8,128)(2,1)}), bf16[4,256,512]{2,1,0:T(8,128)(2,1)S(1)}, u32[]{:S(2)}, u32[]{:S(2)}) async-start(bf16[4,256,512]{2,1,0:T(8,128)(2,1)} %broadcast_in_dim.22), calls=%async_computation.7 | async-start | bytes 2097152 | tf_op jit(solution)/shard_map/all_to_all | solution.py:16
  236.3 1.9 fusion.4
  238.2 3.2 %fusion.1 = f32[512,512]{1,0:T(8,128)} fusion(bf16[1024,512]{1,0:T(8,128)(2,1)} %bitcast.21, bf16[512,4096]{1,0:T(8,128)(2,1)} %all-gather.2.cloned.1.call-done, s32[]{:T(128)S(6)} %select_n.29), kind=kOutput, calls=%fused_computation.4 | convolution fusion | flops 536870912 | bytes 3145732 | tf_op jit(solution)/shard_map/dot_general | solution.py:65
  241.5 1.9 convolution_add_fusion.1
  243.4 7.3 %all-to-all-done.7 = bf16[4,256,512]{2,1,0:T(8,128)(2,1)S(1)} async-done(((bf16[4,256,512]{2,1,0:T(8,128)(2,1)}), bf16[4,256,512]{2,1,0:T(8,128)(2,1)S(1)}, u32[]{:S(2)}, u32[]{:S(2)}) %all-to-all-start.7) | async-done | bytes 1048608 | tf_op jit(solution)/shard_map/all_to_all | solution.py:16
  250.7 2.4 fusion
  253.1 3.6 %collective-permute-start.5 = (bf16[256,512]{1,0:T(8,128)(2,1)S(1)}, bf16[256,512]{1,0:T(8,128)(2,1)S(1)}, u32[]{:S(2)}, u32[]{:S(2)}) collective-permute-start(bf16[256,512]{1,0:T(8,128)(2,1)S(1)} %slice.26), channel_id=1, source_target_pairs={{0,16},{16,0},{1,17},{17,1},{2,18},{18,2},{3,19},{19,3},{4,20},{20... | collective-permute-start | bytes 786440 | tf_op jit(solution)/shard_map/ppermute | solution.py:20
  257.6 1.9 collective-permute-start.6
  259.5 1.1 collective-permute-done.6
  (35 shorter events, 10.7 us)
Async XLA Ops:
  6.5 229.7 %all-gather.2.cloned.1.call-start = ((), (), s32[]{:S(2)}) async-start(), calls=%async_computation.9 | async-start | bytes 4456448 | tf_op jit(solution)/shard_map/all_gather | solution.py:35
  7.5 3.6 %collective-permute-start = (bf16[256,256]{1,0:T(8,128)(2,1)S(1)}, bf16[256,256]{1,0:T(8,128)(2,1)S(1)}, u32[]{:S(2)}, u32[]{:S(2)}) collective-permute-start(bf16[256,256]{1,0:T(8,128)(2,1)S(1)} %get-tuple-element.6), channel_id=1, source_target_pairs={{0,16},{16,0},{1,17},{17,1},{2,18},{18,2},{3,19},{19,3},{4,20},{20... | collective-permute-start | bytes 393224 | tf_op jit(solution)/shard_map/ppermute | solution.py:20
  63.5 11.3 %all-to-all-start.1 = ((bf16[4,16,4,512]{3,2,1,0:T(4,128)(2,1)}), bf16[4,16,4,512]{3,2,1,0:T(4,128)(2,1)S(1)}, u32[]{:S(2)}, u32[]{:S(2)}) async-start(bf16[4,16,4,512]{3,2,1,0:T(4,128)(2,1)} %broadcast_in_dim.16), calls=%async_computation.1 | async-start | bytes 524288 | tf_op jit(solution)/shard_map/all_to_all | solution.py:16
  91.7 31.8 %all-to-all-start.2 = ((bf16[4,4,16,4,512]{4,3,2,1,0:T(4,128)(2,1)}), bf16[4,4,16,4,512]{4,3,2,1,0:T(4,128)(2,1)S(1)}, u32[]{:S(2)}, u32[]{:S(2)}) async-start(bf16[4,4,16,4,512]{4,3,2,1,0:T(4,128)(2,1)} %broadcast_in_dim.17), calls=%async_computation.2 | async-start | bytes 2097152 | tf_op jit(solution)/shard_map/all_to_all | solution.py:16
  110.2 22.0 %copy-start.3 = (bf16[256,512]{1,0:T(8,128)(2,1)S(1)}, bf16[256,512]{1,0:T(8,128)(2,1)}, u32[]{:S(2)}) copy-start(bf16[256,512]{1,0:T(8,128)(2,1)} %param.7) | copy-start | bytes 786436
  124.6 7.2 %copy-start.2 = (f32[512,512]{1,0:T(8,128)}, f32[512,512]{1,0:T(8,128)S(1)}, u32[]{:S(2)}) copy-start(f32[512,512]{1,0:T(8,128)S(1)} %fusion.13) | copy-start | bytes 3145732
  124.6 7.5 %collective-permute-start.1 = (bf16[256,512]{1,0:T(8,128)(2,1)S(1)}, bf16[256,512]{1,0:T(8,128)(2,1)S(1)}, u32[]{:S(2)}, u32[]{:S(2)}) collective-permute-start(bf16[256,512]{1,0:T(8,128)(2,1)S(1)} %dynamic-slice_convert_fusion), channel_id=1, source_target_pairs={{0,16},{16,0},{1,17},{17,1},{2,18},{18,2},{3,19},{19,3},{4,20},{20... | collective-permute-start | bytes 786440 | tf_op jit(solution)/shard_map/ppermute | solution.py:20
  134.4 24.3 %all-to-all-start.5 = ((bf16[4,256,512]{2,1,0:T(8,128)(2,1)}), bf16[4,256,512]{2,1,0:T(8,128)(2,1)S(1)}, u32[]{:S(2)}, u32[]{:S(2)}) async-start(bf16[4,256,512]{2,1,0:T(8,128)(2,1)} %broadcast_in_dim.20), calls=%async_computation.5 | async-start | bytes 2097152 | tf_op jit(solution)/shard_map/all_to_all | solution.py:16
  138.1 20.6 %collective-permute-start.2 = (bf16[256,512]{1,0:T(8,128)(2,1)S(1)}, bf16[256,512]{1,0:T(8,128)(2,1)S(1)}, u32[]{:S(2)}, u32[]{:S(2)}) collective-permute-start(bf16[256,512]{1,0:T(8,128)(2,1)S(1)} %multiply_convert_fusion), channel_id=1, source_target_pairs={{0,128},{128,256},{256,384},{384,0},{1,129},{129,257},{257,385},{3... | collective-permute-start | bytes 786440 | tf_op jit(solution)/shard_map/ppermute | solution.py:24
  159.8 31.7 %all-to-all-start.6 = ((bf16[4,256,512]{2,1,0:T(8,128)(2,1)}), bf16[4,256,512]{2,1,0:T(8,128)(2,1)S(1)}, u32[]{:S(2)}, u32[]{:S(2)}) async-start(bf16[4,256,512]{2,1,0:T(8,128)(2,1)} %broadcast_in_dim.21), calls=%async_computation.6 | async-start | bytes 2097152 | tf_op jit(solution)/shard_map/all_to_all | solution.py:16
  163.6 27.8 %collective-permute-start.4 = (bf16[256,512]{1,0:T(8,128)(2,1)S(1)}, bf16[256,512]{1,0:T(8,128)(2,1)S(1)}, u32[]{:S(2)}, u32[]{:S(2)}) collective-permute-start(bf16[256,512]{1,0:T(8,128)(2,1)S(1)} %multiply_convert_fusion), channel_id=1, source_target_pairs={{0,256},{128,384},{256,0},{384,128},{1,257},{129,385},{257,1},{385... | collective-permute-start | bytes 786440 | tf_op jit(solution)/shard_map/ppermute | solution.py:24
  192.5 37.3 %all-to-all-start.8 = ((bf16[4,256,512]{2,1,0:T(8,128)(2,1)}), bf16[4,256,512]{2,1,0:T(8,128)(2,1)S(1)}, u32[]{:S(2)}, u32[]{:S(2)}) async-start(bf16[4,256,512]{2,1,0:T(8,128)(2,1)} %broadcast_in_dim.23), calls=%async_computation.8 | async-start | bytes 2097152 | tf_op jit(solution)/shard_map/all_to_all | solution.py:16
  197.0 32.8 %collective-permute-start.3 = (bf16[256,512]{1,0:T(8,128)(2,1)S(1)}, bf16[256,512]{1,0:T(8,128)(2,1)}, u32[]{:S(2)}, u32[]{:S(2)}) collective-permute-start(bf16[256,512]{1,0:T(8,128)(2,1)S(1)} %multiply_convert_fusion), channel_id=1, source_target_pairs={{0,384},{128,0},{256,128},{384,256},{1,385},{129,1},{257,129},{385... | collective-permute-start | bytes 786440 | tf_op jit(solution)/shard_map/ppermute | solution.py:24
  229.9 2.2 copy-start.1
  232.0 18.6 %all-to-all-start.7 = ((bf16[4,256,512]{2,1,0:T(8,128)(2,1)}), bf16[4,256,512]{2,1,0:T(8,128)(2,1)S(1)}, u32[]{:S(2)}, u32[]{:S(2)}) async-start(bf16[4,256,512]{2,1,0:T(8,128)(2,1)} %broadcast_in_dim.22), calls=%async_computation.7 | async-start | bytes 2097152 | tf_op jit(solution)/shard_map/all_to_all | solution.py:16
  250.7 6.0 %copy-start = (bf16[512,4096]{1,0:T(8,128)(2,1)S(1)}, bf16[512,4096]{1,0:T(8,128)(2,1)}, u32[]{:S(2)}) copy-start(bf16[512,4096]{1,0:T(8,128)(2,1)} %all-gather.2.cloned.1.call-done) | copy-start | bytes 12582916
  253.1 7.5 %collective-permute-start.5 = (bf16[256,512]{1,0:T(8,128)(2,1)S(1)}, bf16[256,512]{1,0:T(8,128)(2,1)S(1)}, u32[]{:S(2)}, u32[]{:S(2)}) collective-permute-start(bf16[256,512]{1,0:T(8,128)(2,1)S(1)} %slice.26), channel_id=1, source_target_pairs={{0,16},{16,0},{1,17},{17,1},{2,18},{18,2},{3,19},{19,3},{4,20},{20... | collective-permute-start | bytes 786440 | tf_op jit(solution)/shard_map/ppermute | solution.py:20
  257.6 3.0 %collective-permute-start.6 = (f32[256]{0:T(256)S(1)}, f32[256]{0:T(256)S(1)}, u32[]{:S(2)}, u32[]{:S(2)}) collective-permute-start(f32[256]{0:T(256)S(1)} %slice.16), channel_id=1, source_target_pairs={{0,16},{16,0},{1,17},{17,1},{2,18},{18,2},{3,19},{19,3},{4,20},{20... | collective-permute-start | bytes 3080 | tf_op jit(solution)/shard_map/ppermute | solution.py:20
Sparse Core Ops, SparseCore 0:
  11.9 101.5 all-gather.1

commit v2 on v1

v2 whole, which is shorter than its diff:
```python
import jax
import jax.numpy as jnp
from jax import lax
from jax.experimental import pallas as pl
from jax.experimental.pallas import tpu as pltpu
from jax.sharding import Mesh, PartitionSpec as P

adapter_scale = 2.0
norm_epsilon = 1e-05
width = 8192

f32 = jnp.float32
bf16 = jnp.bfloat16


def exchange(blocks, axis):
    return lax.all_to_all(blocks, axis, split_axis=0, concat_axis=0)


def copies(block):
    return jnp.broadcast_to(block[None], (4,) + block.shape)


def ahead(block, axis, step):
    return lax.ppermute(block, axis, [(i, (i - step) % 4) for i in range(4)])


def ring(block, axis):
    blocks = [block] + [ahead(block, axis, r) for r in (1, 2, 3)]
    return lax.dynamic_slice_in_dim(
        jnp.stack(blocks + blocks), lax.rem(4 - lax.axis_index(axis), 4), 4, axis=0
    )


def swap(block):
    return lax.ppermute(block, "core", [(0, 1), (1, 0)])


def mirror(block, flip):
    pairs = [
        ((i * 2 + c) * 4 + j, (j * 2 + (c ^ flip)) * 4 + i)
        for i in range(4)
        for c in range(2)
        for j in range(4)
    ]
    return lax.ppermute(block, ("x", "core", "y"), pairs)


def thirds(value):
    parts = []
    for _ in range(3):
        part = lax.reduce_precision(value, 8, 7)
        parts.append(part.astype(bf16))
        value = value - part
    return jnp.stack(parts)


def product_kernel(place, rows, own, after, before, far_a, far_b, keep, give):
    far = jnp.concatenate([far_a[...], far_b[...]], axis=0)
    weights = [own[...], after[...], far, before[...]]

    def block(r, carry):
        y = lax.rem(place[1] + r, 4)
        for core, out in ((0, keep), (1, give)):
            total = None
            for step in range(4):
                z = lax.rem(place[0] + step, 4)
                left = rows[y, z, :256, core * 256 : core * 256 + 256]
                term = jnp.dot(left, weights[step], preferred_element_type=f32)
                total = term if total is None else total + term
            out[r] = total.astype(out.dtype)
        return carry

    lax.fori_loop(0, 4, block, 0)


def product(place, rows, own, after, before, far_a, far_b):
    vmem = pl.BlockSpec(memory_space=pltpu.VMEM)
    return pl.pallas_call(
        product_kernel,
        out_shape=(
            jax.ShapeDtypeStruct((4, 256, 512), f32),
            jax.ShapeDtypeStruct((4, 256, 512), bf16),
        ),
        in_specs=[pl.BlockSpec(memory_space=pltpu.SMEM)] + [vmem] * 6,
        out_specs=(vmem, vmem),
        compiler_params=pltpu.CompilerParams(vmem_limit_bytes=40 * 2**20),
        cost_estimate=pl.CostEstimate(
            flops=2 * 2048 * 1024 * 512, bytes_accessed=9 * 2**20, transcendentals=0
        ),
    )(place, rows, own, after, before, far_a, far_b)


def local(tokens, norm_gain, base_weight, factor_a, factor_b):
    core = lax.axis_index("core")
    z_hi, x = lax.axis_index("z_hi"), lax.axis_index("x")
    client = (z_hi * 4 + x) * 2 + core

    keep = lax.dynamic_slice_in_dim(tokens, core * 256, 256, axis=1)
    give = lax.dynamic_slice_in_dim(tokens, (1 - core) * 256, 256, axis=1)
    values = tokens.astype(f32)
    squares = thirds(jnp.sum(values * values, axis=1))
    squares = jnp.pad(squares, ((0, 13), (0, 256)))
    pair = jnp.concatenate([mirror(keep, 0), mirror(give, 1)], axis=1)

    down = factor_a.reshape(4, 4, 4, 512).transpose(1, 2, 0, 3).reshape(4, 16, 512)
    both = exchange(jnp.concatenate([copies(factor_b.T), down], axis=1), "z_hi")
    up = both[:, :64]
    down = both[:, 64:].reshape(4, 4, 4, 512).transpose(1, 0, 2, 3).reshape(64, 512)
    line = copies(jnp.concatenate([pair, squares, down], axis=0))
    line, up = lax.optimization_barrier((line, up))

    line = exchange(line, "z_lo")
    up = ring(up, "x")
    down = line[:, 272:].reshape(4, 4, 16, 512).transpose(1, 0, 2, 3)
    down = jnp.broadcast_to(down[:, None], (4, 4, 4, 16, 512)).reshape(16, 64, 512)
    line, up, down = lax.optimization_barrier((line, up, down))

    down = exchange(down, ("x", "y"))
    up = up.reshape(4, 4, 4, 4, 4, 512).transpose(0, 3, 2, 1, 4, 5).reshape(1024, 512)
    rows = copies(line[:, :272])
    rows, up, down = lax.optimization_barrier((rows, up, down))

    rows = exchange(rows, "y")
    part = lax.dot_general(
        down.reshape(1024, 512), up, (((0,), (0,)), ((), ())), preferred_element_type=f32
    )
    mine = lax.dynamic_slice_in_dim(part, core * 256, 256, axis=0)
    other = lax.dynamic_slice_in_dim(part, (1 - core) * 256, 256, axis=0).astype(bf16)
    update = mine + swap(other).astype(f32)
    gain = lax.dynamic_slice_in_dim(norm_gain, client * 256, 256)[:, None]
    weight = (gain * (base_weight.astype(f32) + adapter_scale * update)).astype(bf16)

    after, before = ahead(weight, "z_hi", 1), ahead(weight, "z_hi", 3)
    far_a, far_b = ahead(after[:128], "z_hi", 1), ahead(before[128:], "z_hi", 3)
    keep, give = product(jnp.stack([z_hi, x]), rows, weight, after, before, far_a, far_b)

    sums = keep + swap(give).astype(f32)
    query = sums[0]
    for r in (1, 2, 3):
        query = query + ahead(sums[r].astype(bf16), "x", 4 - r).astype(f32)
    squares = jnp.sum(rows[:, :, 256:259, :256].astype(f32), axis=(0, 1, 2))
    scale = lax.rsqrt(squares / width + norm_epsilon)
    return (query * scale[:, None]).astype(bf16)


def solution(mesh):
    fine = Mesh(mesh.devices.reshape(4, 4, 2, 4, 4), ("z_hi", "x", "core", "z_lo", "y"))
    client, tensor = ("z_hi", "x", "core"), ("z_lo", "y")
    return jax.shard_map(
        local,
        mesh=fine,
        in_specs=(
            P(client, tensor),
            P(),
            P(client, tensor),
            P(client + tensor, None),
            P(tensor, client),
        ),
        out_specs=P(client, tensor),
        check_vma=False,
    )
```

time: 269 us -> 193 us (0.72)
  the two profiles are of different devices: /device:TPU:9 before, /device:TPU:1 now
where the time goes in v2:
time: 193 us; the launch traced here: 190 us
  waiting for transfers between devices  86.6 us (45%)
  starting transfers between devices  83.4 us (43%)
  local copies, waits for them, and re-layouts  10.7 us (6%)
  Pallas kernels  5.22 us (3%)
  other arithmetic  3.24 us (2%)
    ppermute x10, waiting for transfers between devices, ahead(): return lax.ppermute(block, axis, [(i, (i - step) % 4) for i in range(4)])  44.3 us
    all_to_all x4, waiting for transfers between devices, exchange(): return lax.all_to_all(blocks, axis, split_axis=0, concat_axis=0)  39.6 us
    ppermute x10, starting transfers between devices, ahead(): return lax.ppermute(block, axis, [(i, (i - step) % 4) for i in range(4)])  36.7 us
    all_to_all x4, starting transfers between devices, exchange(): return lax.all_to_all(blocks, axis, split_axis=0, concat_axis=0)  35.7 us
    ppermute x2, starting transfers between devices, swap(): return lax.ppermute(block, 'core', [(0, 1), (1, 0)])  7.42 us
    pallas_call x1, Pallas kernels, product(): pl.pallas_call(product_kernel, out_shape=(jax.ShapeDtypeStruct((4, 256, 5...  5.22 us
    broadcast_in_dim x3, local copies, waits for them, and re-layouts, copies(): return jnp.broadcast_to(block[None], (4,) + block.shape)  4.58 us
  transfers between devices with their start and end apart: 18, of which 12 were waited for; matrix products, arithmetic and copies ran while one was open for 3% of the time, Pallas kernels for 0%

profile of v2, /device:TPU:1, one launch (start us, length us, event | category | flops | bytes accessed | tf_op | source)
XLA Modules:
  0.0 190.4 jit_solution(15783222129846609989)
XLA Ops:
  2.6 15.6 %all-to-all-start = ((bf16[4,80,512]{2,1,0:T(8,128)(2,1)}), bf16[4,80,512]{2,1,0:T(8,128)(2,1)S(1)}, u32[]{:S(2)}, u32[]{:S(2)}) async-start(bf16[4,80,512]{2,1,0:T(8,128)(2,1)} %pad_maximum_fusion.1), calls=%async_computation | async-start | bytes 655360 | tf_op jit(solution)/shard_map/all_to_all | solution.py:17
  19.0 2.9 %collective-permute-start.1 = (bf16[256,256]{1,0:T(8,128)(2,1)S(1)}, bf16[256,256]{1,0:T(8,128)(2,1)S(1)}, u32[]{:S(2)}, u32[]{:S(2)}) collective-permute-start(bf16[256,256]{1,0:T(8,128)(2,1)S(1)} %get-tuple-element.31), channel_id=1, source_target_pairs={{0,16},{1,48},{2,80},{3,112},{16,0},{17,32},{18,64},{19,96},{32,17... | collective-permute-start | bytes 393224 | tf_op jit(solution)/shard_map/ppermute | solution.py:46
  22.0 13.2 %all-to-all-done = bf16[4,80,512]{2,1,0:T(8,128)(2,1)S(1)} async-done(((bf16[4,80,512]{2,1,0:T(8,128)(2,1)}), bf16[4,80,512]{2,1,0:T(8,128)(2,1)S(1)}, u32[]{:S(2)}, u32[]{:S(2)}) %all-to-all-start) | async-done | bytes 327712 | tf_op jit(solution)/shard_map/all_to_all | solution.py:17
  35.3 1.2 broadcast_in_dim.9
  36.6 8.3 %all-to-all-start.1 = ((bf16[4,336,512]{2,1,0:T(8,128)(2,1)}), bf16[4,336,512]{2,1,0:T(8,128)(2,1)S(1)}, u32[]{:S(2)}, u32[]{:S(2)}) async-start(bf16[4,336,512]{2,1,0:T(8,128)(2,1)} %broadcast_in_dim.9), calls=%async_computation.1 | async-start | bytes 2752512 | tf_op jit(solution)/shard_map/all_to_all | solution.py:17
  44.9 4.4 %collective-permute-start.2 = (bf16[4,64,512]{2,1,0:T(8,128)(2,1)S(1)}, bf16[4,64,512]{2,1,0:T(8,128)(2,1)S(1)}, u32[]{:S(2)}, u32[]{:S(2)}) collective-permute-start(bf16[4,64,512]{2,1,0:T(8,128)(2,1)S(1)} %slice.48), channel_id=1, source_target_pairs={{0,96},{32,0},{64,32},{96,64},{1,97},{33,1},{65,33},{97,65},{2,98}... | collective-permute-start | bytes 786440 | tf_op jit(solution)/shard_map/ppermute | solution.py:25
  49.3 1.9 %collective-permute-start.4 = (bf16[4,64,512]{2,1,0:T(8,128)(2,1)S(1)}, bf16[4,64,512]{2,1,0:T(8,128)(2,1)S(1)}, u32[]{:S(2)}, u32[]{:S(2)}) collective-permute-start(bf16[4,64,512]{2,1,0:T(8,128)(2,1)S(1)} %slice.48), channel_id=1, source_target_pairs={{0,32},{32,64},{64,96},{96,0},{1,33},{33,65},{65,97},{97,1},{2,34}... | collective-permute-start | bytes 786440 | tf_op jit(solution)/shard_map/ppermute | solution.py:25
  51.2 3.6 %collective-permute-start.3 = (bf16[4,64,512]{2,1,0:T(8,128)(2,1)S(1)}, bf16[4,64,512]{2,1,0:T(8,128)(2,1)S(1)}, u32[]{:S(2)}, u32[]{:S(2)}) collective-permute-start(bf16[4,64,512]{2,1,0:T(8,128)(2,1)S(1)} %slice.48), channel_id=1, source_target_pairs={{0,64},{32,96},{64,0},{96,32},{1,65},{33,97},{65,1},{97,33},{2,66}... | collective-permute-start | bytes 786440 | tf_op jit(solution)/shard_map/ppermute | solution.py:25
  54.9 8.0 %collective-permute-done.3 = bf16[4,64,512]{2,1,0:T(8,128)(2,1)S(1)} collective-permute-done((bf16[4,64,512]{2,1,0:T(8,128)(2,1)S(1)}, bf16[4,64,512]{2,1,0:T(8,128)(2,1)S(1)}, u32[]{:S(2)}, u32[]{:S(2)}) %collective-permute-start.3) | collective-permute-done | bytes 262176 | tf_op jit(solution)/shard_map/ppermute | solution.py:25
  63.1 14.0 %all-to-all-done.1 = bf16[4,336,512]{2,1,0:T(8,128)(2,1)S(1)} async-done(((bf16[4,336,512]{2,1,0:T(8,128)(2,1)}), bf16[4,336,512]{2,1,0:T(8,128)(2,1)S(1)}, u32[]{:S(2)}, u32[]{:S(2)}) %all-to-all-start.1) | async-done | bytes 1376288 | tf_op jit(solution)/shard_map/all_to_all | solution.py:17
  77.2 1.3 broadcast_in_dim.10
  78.5 6.8 %all-to-all-start.2 = ((bf16[16,64,512]{2,1,0:T(8,128)(2,1)}), bf16[16,64,512]{2,1,0:T(8,128)(2,1)S(1)}, u32[]{:S(2)}, u32[]{:S(2)}) async-start(bf16[16,64,512]{2,1,0:T(8,128)(2,1)} %bitcast.14), calls=%async_computation.2 | async-start | bytes 2097152 | tf_op jit(solution)/shard_map/all_to_all | solution.py:17
  87.8 12.5 %all-to-all-done.2 = bf16[16,64,512]{2,1,0:T(8,128)(2,1)S(1)} async-done(((bf16[16,64,512]{2,1,0:T(8,128)(2,1)}), bf16[16,64,512]{2,1,0:T(8,128)(2,1)S(1)}, u32[]{:S(2)}, u32[]{:S(2)}) %all-to-all-start.2) | async-done | bytes 1048608 | tf_op jit(solution)/shard_map/all_to_all | solution.py:17
  100.3 2.5 %broadcast_in_dim.11 = bf16[4,4,272,512]{3,2,1,0:T(8,128)(2,1)} broadcast(bf16[4,272,512]{2,1,0:T(8,128)(2,1)S(1)} %slice-done), dimensions={1,2,3} | broadcast | bytes 5570560 | tf_op jit(solution)/shard_map/broadcast_in_dim | solution.py:21
  102.8 5.0 %all-to-all-start.3 = ((bf16[4,4,272,512]{3,2,1,0:T(8,128)(2,1)}), bf16[4,4,272,512]{3,2,1,0:T(8,128)(2,1)}, u32[]{:S(2)}, u32[]{:S(2)}) async-start(bf16[4,4,272,512]{3,2,1,0:T(8,128)(2,1)} %broadcast_in_dim.11), calls=%async_computation.3 | async-start | bytes 8912896 | tf_op jit(solution)/shard_map/all_to_all | solution.py:17
  108.7 5.0 %collective-permute-start.5 = (bf16[256,512]{1,0:T(8,128)(2,1)S(1)}, bf16[256,512]{1,0:T(8,128)(2,1)S(1)}, u32[]{:S(2)}, u32[]{:S(2)}) collective-permute-start(bf16[256,512]{1,0:T(8,128)(2,1)S(1)} %dynamic-slice_convert_fusion), channel_id=1, source_target_pairs={{0,16},{16,0},{1,17},{17,1},{2,18},{18,2},{3,19},{19,3},{4,20},{20... | collective-permute-start | bytes 786440 | tf_op jit(solution)/shard_map/ppermute | solution.py:36
  115.0 3.5 %collective-permute-start.7 = (bf16[256,512]{1,0:T(8,128)(2,1)S(1)}, bf16[256,512]{1,0:T(8,128)(2,1)S(1)}, u32[]{:S(2)}, u32[]{:S(2)}) collective-permute-start(bf16[256,512]{1,0:T(8,128)(2,1)S(1)} %multiply_convert_fusion.own), channel_id=1, source_target_pairs={{0,128},{128,256},{256,384},{384,0},{1,129},{129,257},{257,385},{3... | collective-permute-start | bytes 786440 | tf_op jit(solution)/shard_map/ppermute | solution.py:25
  118.5 5.6 %collective-permute-start.6 = (bf16[256,512]{1,0:T(8,128)(2,1)S(1)}, bf16[256,512]{1,0:T(8,128)(2,1)S(1)}, u32[]{:S(2)}, u32[]{:S(2)}) collective-permute-start(bf16[256,512]{1,0:T(8,128)(2,1)S(1)} %multiply_convert_fusion.own), channel_id=1, source_target_pairs={{0,384},{128,0},{256,128},{384,256},{1,385},{129,1},{257,129},{385... | collective-permute-start | bytes 786440 | tf_op jit(solution)/shard_map/ppermute | solution.py:25
  124.2 19.3 %collective-permute-done.7.before = bf16[256,512]{1,0:T(8,128)(2,1)S(1)} collective-permute-done((bf16[256,512]{1,0:T(8,128)(2,1)S(1)}, bf16[256,512]{1,0:T(8,128)(2,1)S(1)}, u32[]{:S(2)}, u32[]{:S(2)}) %collective-permute-start.7) | collective-permute-done | bytes 262176 | tf_op jit(solution)/shard_map/ppermute | solution.py:25
  143.4 6.0 %collective-permute-start.9 = (bf16[128,512]{1,0:T(8,128)(2,1)S(1)}, bf16[128,512]{1,0:T(8,128)(2,1)S(1)}, u32[]{:S(2)}, u32[]{:S(2)}) collective-permute-start(bf16[128,512]{1,0:T(8,128)(2,1)S(1)} %slice.51), channel_id=1, source_target_pairs={{0,128},{128,256},{256,384},{384,0},{1,129},{129,257},{257,385},{3... | collective-permute-start | bytes 393224 | tf_op jit(solution)/shard_map/ppermute | solution.py:25
  149.5 3.2 %collective-permute-start.8 = (bf16[128,512]{1,0:T(8,128)(2,1)S(1)}, bf16[128,512]{1,0:T(8,128)(2,1)S(1)}, u32[]{:S(2)}, u32[]{:S(2)}) collective-permute-start(bf16[128,512]{1,0:T(8,128)(2,1)S(1)} %slice.50), channel_id=1, source_target_pairs={{0,384},{128,0},{256,128},{384,256},{1,385},{129,1},{257,129},{385... | collective-permute-start | bytes 393224 | tf_op jit(solution)/shard_map/ppermute | solution.py:25
  152.8 6.1 %collective-permute-done.9.far_b = bf16[128,512]{1,0:T(8,128)(2,1)S(1)} collective-permute-done((bf16[128,512]{1,0:T(8,128)(2,1)S(1)}, bf16[128,512]{1,0:T(8,128)(2,1)S(1)}, u32[]{:S(2)}, u32[]{:S(2)}) %collective-permute-start.9) | collective-permute-done | bytes 131104 | tf_op jit(solution)/shard_map/ppermute | solution.py:25
  158.9 3.5 %collective-permute-done.8.far_a = bf16[128,512]{1,0:T(8,128)(2,1)S(1)} collective-permute-done((bf16[128,512]{1,0:T(8,128)(2,1)S(1)}, bf16[128,512]{1,0:T(8,128)(2,1)S(1)}, u32[]{:S(2)}, u32[]{:S(2)}) %collective-permute-start.8) | collective-permute-done | bytes 131104 | tf_op jit(solution)/shard_map/ppermute | solution.py:25
  162.4 5.2 %shard_map.55 = (f32[4,256,512]{2,1,0:T(8,128)S(1)}, bf16[4,256,512]{2,1,0:T(8,128)(2,1)S(1)}) custom-call(s32[2]{0:T(128)S(1)} %pad_add_fusion.place, bf16[4,4,272,512]{3,2,1,0:T(8,128)(2,1)} %all-to-all-done.3.rows, bf16[256,512]{1,0:T(8,128)(2,1)S(1)} %multiply_convert_fusion.own, bf16[256,512]{1,0:T(8,128)(2,1)S(1)} %collective-permute-done.6.after, ...), custom_call_target="tpu_custom_call" | custom-call | flops 2147483648 | bytes 9437184 | tf_op jit(solution)/shard_map/pallas_call | solution.py:79
  167.6 2.4 %collective-permute-start.10 = (bf16[4,256,512]{2,1,0:T(8,128)(2,1)S(1)}, bf16[4,256,512]{2,1,0:T(8,128)(2,1)S(1)}, u32[]{:S(2)}, u32[]{:S(2)}) collective-permute-start(bf16[4,256,512]{2,1,0:T(8,128)(2,1)S(1)} %get-tuple-element.24), channel_id=1, source_target_pairs={{0,16},{16,0},{1,17},{17,1},{2,18},{18,2},{3,19},{19,3},{4,20},{20... | collective-permute-start | bytes 3145736 | tf_op jit(solution)/shard_map/ppermute | solution.py:36
  170.0 2.3 %collective-permute-done.10 = bf16[4,256,512]{2,1,0:T(8,128)(2,1)S(1)} collective-permute-done((bf16[4,256,512]{2,1,0:T(8,128)(2,1)S(1)}, bf16[4,256,512]{2,1,0:T(8,128)(2,1)S(1)}, u32[]{:S(2)}, u32[]{:S(2)}) %collective-permute-start.10) | collective-permute-done | bytes 1048608 | tf_op jit(solution)/shard_map/ppermute | solution.py:36
  172.8 1.9 %collective-permute-start.11 = (bf16[256,512]{1,0:T(8,128)(2,1)S(1)}, bf16[256,512]{1,0:T(8,128)(2,1)S(1)}, u32[]{:S(2)}, u32[]{:S(2)}) collective-permute-start(bf16[256,512]{1,0:T(8,128)(2,1)S(1)} %get-tuple-element.27), channel_id=1, source_target_pairs={{0,32},{32,64},{64,96},{96,0},{1,33},{33,65},{65,97},{97,1},{2,34}... | collective-permute-start | bytes 786440 | tf_op jit(solution)/shard_map/ppermute | solution.py:25
  174.7 4.6 %collective-permute-start.13 = (bf16[256,512]{1,0:T(8,128)(2,1)S(1)}, bf16[256,512]{1,0:T(8,128)(2,1)S(1)}, u32[]{:S(2)}, u32[]{:S(2)}) collective-permute-start(bf16[256,512]{1,0:T(8,128)(2,1)S(1)} %get-tuple-element.28), channel_id=1, source_target_pairs={{0,96},{32,0},{64,32},{96,64},{1,97},{33,1},{65,33},{97,65},{2,98}... | collective-permute-start | bytes 786440 | tf_op jit(solution)/shard_map/ppermute | solution.py:25
  179.3 1.9 %collective-permute-start.12 = (bf16[256,512]{1,0:T(8,128)(2,1)S(1)}, bf16[256,512]{1,0:T(8,128)(2,1)S(1)}, u32[]{:S(2)}, u32[]{:S(2)}) collective-permute-start(bf16[256,512]{1,0:T(8,128)(2,1)S(1)} %get-tuple-element.29), channel_id=1, source_target_pairs={{0,64},{32,96},{64,0},{96,32},{1,65},{33,97},{65,1},{97,33},{2,66}... | collective-permute-start | bytes 786440 | tf_op jit(solution)/shard_map/ppermute | solution.py:25
  182.1 1.3 collective-permute-done.11
  183.4 1.5 collective-permute-done.13
  184.9 4.6 %collective-permute-done.12 = bf16[256,512]{1,0:T(8,128)(2,1)S(1)} collective-permute-done((bf16[256,512]{1,0:T(8,128)(2,1)S(1)}, bf16[256,512]{1,0:T(8,128)(2,1)S(1)}, u32[]{:S(2)}, u32[]{:S(2)}) %collective-permute-start.12) | collective-permute-done | bytes 262176 | tf_op jit(solution)/shard_map/ppermute | solution.py:25
  (59 shorter events, 10.7 us)
Async XLA Ops:
  0.0 18.3 %copy-start.2 = (bf16[256,512]{1,0:T(8,128)(2,1)S(1)}, bf16[256,512]{1,0:T(8,128)(2,1)}, u32[]{:S(2)}) copy-start(bf16[256,512]{1,0:T(8,128)(2,1)} %param.5) | copy-start | bytes 786436
  2.6 32.5 %all-to-all-start = ((bf16[4,80,512]{2,1,0:T(8,128)(2,1)}), bf16[4,80,512]{2,1,0:T(8,128)(2,1)S(1)}, u32[]{:S(2)}, u32[]{:S(2)}) async-start(bf16[4,80,512]{2,1,0:T(8,128)(2,1)} %pad_maximum_fusion.1), calls=%async_computation | async-start | bytes 655360 | tf_op jit(solution)/shard_map/all_to_all | solution.py:17
  18.3 17.0 %collective-permute-start = (bf16[256,256]{1,0:T(8,128)(2,1)S(1)}, bf16[256,256]{1,0:T(8,128)(2,1)S(1)}, u32[]{:S(2)}, u32[]{:S(2)}) collective-permute-start(bf16[256,256]{1,0:T(8,128)(2,1)S(1)} %get-tuple-element.30), channel_id=1, source_target_pairs={{0,0},{1,32},{2,64},{3,96},{16,16},{17,48},{18,80},{19,112},{32,1}... | collective-permute-start | bytes 393224 | tf_op jit(solution)/shard_map/ppermute | solution.py:46
  19.0 16.4 %collective-permute-start.1 = (bf16[256,256]{1,0:T(8,128)(2,1)S(1)}, bf16[256,256]{1,0:T(8,128)(2,1)S(1)}, u32[]{:S(2)}, u32[]{:S(2)}) collective-permute-start(bf16[256,256]{1,0:T(8,128)(2,1)S(1)} %get-tuple-element.31), channel_id=1, source_target_pairs={{0,16},{1,48},{2,80},{3,112},{16,0},{17,32},{18,64},{19,96},{32,17... | collective-permute-start | bytes 393224 | tf_op jit(solution)/shard_map/ppermute | solution.py:46
  36.6 40.6 %all-to-all-start.1 = ((bf16[4,336,512]{2,1,0:T(8,128)(2,1)}), bf16[4,336,512]{2,1,0:T(8,128)(2,1)S(1)}, u32[]{:S(2)}, u32[]{:S(2)}) async-start(bf16[4,336,512]{2,1,0:T(8,128)(2,1)} %broadcast_in_dim.9), calls=%async_computation.1 | async-start | bytes 2752512 | tf_op jit(solution)/shard_map/all_to_all | solution.py:17
  44.9 10.0 %collective-permute-start.2 = (bf16[4,64,512]{2,1,0:T(8,128)(2,1)S(1)}, bf16[4,64,512]{2,1,0:T(8,128)(2,1)S(1)}, u32[]{:S(2)}, u32[]{:S(2)}) collective-permute-start(bf16[4,64,512]{2,1,0:T(8,128)(2,1)S(1)} %slice.48), channel_id=1, source_target_pairs={{0,96},{32,0},{64,32},{96,64},{1,97},{33,1},{65,33},{97,65},{2,98}... | collective-permute-start | bytes 786440 | tf_op jit(solution)/shard_map/ppermute | solution.py:25
  49.3 13.6 %collective-permute-start.4 = (bf16[4,64,512]{2,1,0:T(8,128)(2,1)S(1)}, bf16[4,64,512]{2,1,0:T(8,128)(2,1)S(1)}, u32[]{:S(2)}, u32[]{:S(2)}) collective-permute-start(bf16[4,64,512]{2,1,0:T(8,128)(2,1)S(1)} %slice.48), channel_id=1, source_target_pairs={{0,32},{32,64},{64,96},{96,0},{1,33},{33,65},{65,97},{97,1},{2,34}... | collective-permute-start | bytes 786440 | tf_op jit(solution)/shard_map/ppermute | solution.py:25
  51.2 11.7 %collective-permute-start.3 = (bf16[4,64,512]{2,1,0:T(8,128)(2,1)S(1)}, bf16[4,64,512]{2,1,0:T(8,128)(2,1)S(1)}, u32[]{:S(2)}, u32[]{:S(2)}) collective-permute-start(bf16[4,64,512]{2,1,0:T(8,128)(2,1)S(1)} %slice.48), channel_id=1, source_target_pairs={{0,64},{32,96},{64,0},{96,32},{1,65},{33,97},{65,1},{97,33},{2,66}... | collective-permute-start | bytes 786440 | tf_op jit(solution)/shard_map/ppermute | solution.py:25
  77.1 8.1 %copy-start = (bf16[4,336,512]{2,1,0:T(8,128)(2,1)}, bf16[4,336,512]{2,1,0:T(8,128)(2,1)S(1)}, u32[]{:S(2)}) copy-start(bf16[4,336,512]{2,1,0:T(8,128)(2,1)S(1)} %all-to-all-done.1) | copy-start | bytes 4128772
  78.5 21.8 %all-to-all-start.2 = ((bf16[16,64,512]{2,1,0:T(8,128)(2,1)}), bf16[16,64,512]{2,1,0:T(8,128)(2,1)S(1)}, u32[]{:S(2)}, u32[]{:S(2)}) async-start(bf16[16,64,512]{2,1,0:T(8,128)(2,1)} %bitcast.14), calls=%async_computation.2 | async-start | bytes 2097152 | tf_op jit(solution)/shard_map/all_to_all | solution.py:17
  86.0 14.3 %slice-start = ((bf16[4,336,512]{2,1,0:T(8,128)(2,1)}), bf16[4,272,512]{2,1,0:T(8,128)(2,1)S(1)}, s32[]{:S(2)}) async-start(bf16[4,336,512]{2,1,0:T(8,128)(2,1)} %copy-done), calls=%async_computation.4 | async-start | bytes 2228224 | tf_op jit(solution)/shard_map/slice | solution.py:121
  102.8 5.0 %copy-start.1 = (bf16[1024,512]{1,0:T(8,128)(2,1)S(1)}, bf16[1024,512]{1,0:T(8,128)(2,1)}, u32[]{:S(2)}) copy-start(bf16[1024,512]{1,0:T(8,128)(2,1)} %reshape.83) | copy-start | bytes 3145732
  102.8 59.6 %all-to-all-start.3 = ((bf16[4,4,272,512]{3,2,1,0:T(8,128)(2,1)}), bf16[4,4,272,512]{3,2,1,0:T(8,128)(2,1)}, u32[]{:S(2)}, u32[]{:S(2)}) async-start(bf16[4,4,272,512]{3,2,1,0:T(8,128)(2,1)} %broadcast_in_dim.11), calls=%async_computation.3 | async-start | bytes 8912896 | tf_op jit(solution)/shard_map/all_to_all | solution.py:17
  107.9 7.0 %copy-start.3 = (bf16[256,512]{1,0:T(8,128)(2,1)S(1)}, bf16[256,512]{1,0:T(8,128)(2,1)}, u32[]{:S(2)}) copy-start(bf16[256,512]{1,0:T(8,128)(2,1)} %param.7) | copy-start | bytes 786436
  108.7 6.2 %collective-permute-start.5 = (bf16[256,512]{1,0:T(8,128)(2,1)S(1)}, bf16[256,512]{1,0:T(8,128)(2,1)S(1)}, u32[]{:S(2)}, u32[]{:S(2)}) collective-permute-start(bf16[256,512]{1,0:T(8,128)(2,1)S(1)} %dynamic-slice_convert_fusion), channel_id=1, source_target_pairs={{0,16},{16,0},{1,17},{17,1},{2,18},{18,2},{3,19},{19,3},{4,20},{20... | collective-permute-start | bytes 786440 | tf_op jit(solution)/shard_map/ppermute | solution.py:36
  115.0 28.5 %collective-permute-start.7 = (bf16[256,512]{1,0:T(8,128)(2,1)S(1)}, bf16[256,512]{1,0:T(8,128)(2,1)S(1)}, u32[]{:S(2)}, u32[]{:S(2)}) collective-permute-start(bf16[256,512]{1,0:T(8,128)(2,1)S(1)} %multiply_convert_fusion.own), channel_id=1, source_target_pairs={{0,128},{128,256},{256,384},{384,0},{1,129},{129,257},{257,385},{3... | collective-permute-start | bytes 786440 | tf_op jit(solution)/shard_map/ppermute | solution.py:25
  118.5 30.9 %collective-permute-start.6 = (bf16[256,512]{1,0:T(8,128)(2,1)S(1)}, bf16[256,512]{1,0:T(8,128)(2,1)S(1)}, u32[]{:S(2)}, u32[]{:S(2)}) collective-permute-start(bf16[256,512]{1,0:T(8,128)(2,1)S(1)} %multiply_convert_fusion.own), channel_id=1, source_target_pairs={{0,384},{128,0},{256,128},{384,256},{1,385},{129,1},{257,129},{385... | collective-permute-start | bytes 786440 | tf_op jit(solution)/shard_map/ppermute | solution.py:25
  143.4 15.5 %collective-permute-start.9 = (bf16[128,512]{1,0:T(8,128)(2,1)S(1)}, bf16[128,512]{1,0:T(8,128)(2,1)S(1)}, u32[]{:S(2)}, u32[]{:S(2)}) collective-permute-start(bf16[128,512]{1,0:T(8,128)(2,1)S(1)} %slice.51), channel_id=1, source_target_pairs={{0,128},{128,256},{256,384},{384,0},{1,129},{129,257},{257,385},{3... | collective-permute-start | bytes 393224 | tf_op jit(solution)/shard_map/ppermute | solution.py:25
  149.5 12.9 %collective-permute-start.8 = (bf16[128,512]{1,0:T(8,128)(2,1)S(1)}, bf16[128,512]{1,0:T(8,128)(2,1)S(1)}, u32[]{:S(2)}, u32[]{:S(2)}) collective-permute-start(bf16[128,512]{1,0:T(8,128)(2,1)S(1)} %slice.50), channel_id=1, source_target_pairs={{0,384},{128,0},{256,128},{384,256},{1,385},{129,1},{257,129},{385... | collective-permute-start | bytes 393224 | tf_op jit(solution)/shard_map/ppermute | solution.py:25
  167.6 4.7 %collective-permute-start.10 = (bf16[4,256,512]{2,1,0:T(8,128)(2,1)S(1)}, bf16[4,256,512]{2,1,0:T(8,128)(2,1)S(1)}, u32[]{:S(2)}, u32[]{:S(2)}) collective-permute-start(bf16[4,256,512]{2,1,0:T(8,128)(2,1)S(1)} %get-tuple-element.24), channel_id=1, source_target_pairs={{0,16},{16,0},{1,17},{17,1},{2,18},{18,2},{3,19},{19,3},{4,20},{20... | collective-permute-start | bytes 3145736 | tf_op jit(solution)/shard_map/ppermute | solution.py:36
  172.8 10.6 %collective-permute-start.11 = (bf16[256,512]{1,0:T(8,128)(2,1)S(1)}, bf16[256,512]{1,0:T(8,128)(2,1)S(1)}, u32[]{:S(2)}, u32[]{:S(2)}) collective-permute-start(bf16[256,512]{1,0:T(8,128)(2,1)S(1)} %get-tuple-element.27), channel_id=1, source_target_pairs={{0,32},{32,64},{64,96},{96,0},{1,33},{33,65},{65,97},{97,1},{2,34}... | collective-permute-start | bytes 786440 | tf_op jit(solution)/shard_map/ppermute | solution.py:25
  174.7 10.2 %collective-permute-start.13 = (bf16[256,512]{1,0:T(8,128)(2,1)S(1)}, bf16[256,512]{1,0:T(8,128)(2,1)S(1)}, u32[]{:S(2)}, u32[]{:S(2)}) collective-permute-start(bf16[256,512]{1,0:T(8,128)(2,1)S(1)} %get-tuple-element.28), channel_id=1, source_target_pairs={{0,96},{32,0},{64,32},{96,64},{1,97},{33,1},{65,33},{97,65},{2,98}... | collective-permute-start | bytes 786440 | tf_op jit(solution)/shard_map/ppermute | solution.py:25
  179.3 10.3 %collective-permute-start.12 = (bf16[256,512]{1,0:T(8,128)(2,1)S(1)}, bf16[256,512]{1,0:T(8,128)(2,1)S(1)}, u32[]{:S(2)}, u32[]{:S(2)}) collective-permute-start(bf16[256,512]{1,0:T(8,128)(2,1)S(1)} %get-tuple-element.29), channel_id=1, source_target_pairs={{0,64},{32,96},{64,0},{96,32},{1,65},{33,97},{65,1},{97,33},{2,66}... | collective-permute-start | bytes 786440 | tf_op jit(solution)/shard_map/ppermute | solution.py:25

commit v3 on v2

v3 whole, which is shorter than its diff:
```python
import jax
import jax.numpy as jnp
from jax import lax
from jax.experimental import pallas as pl
from jax.experimental.pallas import tpu as pltpu
from jax.sharding import Mesh, PartitionSpec as P

adapter_scale = 2.0
norm_epsilon = 1e-05
width = 8192

f32 = jnp.float32
bf16 = jnp.bfloat16


def exchange(blocks, axis):
    return lax.all_to_all(blocks, axis, split_axis=0, concat_axis=0)


def copies(block):
    return jnp.broadcast_to(block[None], (4,) + block.shape)


def ahead(block, axis, step):
    return lax.ppermute(block, axis, [(i, (i - step) % 4) for i in range(4)])


def turned(blocks, axis):
    return lax.dynamic_slice_in_dim(
        jnp.stack(blocks + blocks), lax.rem(4 - lax.axis_index(axis), 4), 4, axis=0
    )


def swap(block):
    return lax.ppermute(block, "core", [(0, 1), (1, 0)])


def mirror(block, flip):
    pairs = [
        ((i * 2 + c) * 4 + j, (j * 2 + (c ^ flip)) * 4 + i)
        for i in range(4)
        for c in range(2)
        for j in range(4)
    ]
    return lax.ppermute(block, ("x", "core", "y"), pairs)


def thirds(value):
    parts = []
    for _ in range(3):
        part = lax.reduce_precision(value, 8, 7)
        parts.append(part.astype(bf16))
        value = value - part
    return jnp.stack(parts)


def line_kernel(own, first, second, third, out):
    for z, block in enumerate((own, first, second, third)):
        value = block[...]
        for y in range(4):
            out[y, z] = value


def line_copies(*blocks):
    vmem = pl.BlockSpec(memory_space=pltpu.VMEM)
    return pl.pallas_call(
        line_kernel,
        out_shape=jax.ShapeDtypeStruct((4, 4) + blocks[0].shape, bf16),
        in_specs=[vmem] * 4,
        out_specs=vmem,
        compiler_params=pltpu.CompilerParams(vmem_limit_bytes=40 * 2**20),
        cost_estimate=pl.CostEstimate(flops=0, bytes_accessed=6 * 2**20, transcendentals=0),
    )(*blocks)


def product_kernel(place, rows, own, after_a, after_b, before_a, before_b, far_a, far_b, out, weights):
    weights[0] = own[...]
    for step, (upper, lower) in enumerate(
        ((after_a, after_b), (far_a, far_b), (before_a, before_b)), start=1
    ):
        weights[step, :128] = upper[...]
        weights[step, 128:] = lower[...]
    columns = 256 if out.dtype == bf16 else 0
    for y in range(4):
        total = None
        for z in range(4):
            left = rows[y, z, :256, columns : columns + 256]
            right = weights[lax.rem(place[0] + z, 4)]
            term = jnp.dot(left, right, preferred_element_type=f32)
            total = term if total is None else total + term
        out[lax.rem(place[1] + y, 4)] = total.astype(out.dtype)


def product(kind, place, rows, *weights):
    vmem = pl.BlockSpec(memory_space=pltpu.VMEM)
    return pl.pallas_call(
        product_kernel,
        out_shape=jax.ShapeDtypeStruct((4, 256, 512), kind),
        in_specs=[pl.BlockSpec(memory_space=pltpu.SMEM)] + [vmem] * 8,
        out_specs=vmem,
        scratch_shapes=[pltpu.VMEM((4, 256, 512), bf16)],
        compiler_params=pltpu.CompilerParams(vmem_limit_bytes=40 * 2**20),
        cost_estimate=pl.CostEstimate(
            flops=2048 * 1024 * 512, bytes_accessed=7 * 2**20, transcendentals=0
        ),
    )(place, rows, *weights)


def message_kernel(up, down, out):
    for z in range(4):
        out[z, :64] = up[...]
        out[z, 64:] = jnp.concatenate(
            [down[:, z * 2048 + x * 512 : z * 2048 + x * 512 + 512] for x in range(4)], axis=0
        )


def message(up, down):
    vmem = pl.BlockSpec(memory_space=pltpu.VMEM)
    return pl.pallas_call(
        message_kernel,
        out_shape=jax.ShapeDtypeStruct((4, 80, 512), bf16),
        in_specs=[vmem] * 2,
        out_specs=vmem,
        cost_estimate=pl.CostEstimate(flops=0, bytes_accessed=2**19, transcendentals=0),
    )(up, down)


def local(tokens, norm_gain, base_weight, factor_a, factor_b):
    core = lax.axis_index("core")
    z_hi, x = lax.axis_index("z_hi"), lax.axis_index("x")
    z_lo = lax.axis_index("z_lo")
    client = (z_hi * 4 + x) * 2 + core

    keep = lax.dynamic_slice_in_dim(tokens, core * 256, 256, axis=1)
    give = lax.dynamic_slice_in_dim(tokens, (1 - core) * 256, 256, axis=1)
    values = tokens.astype(f32)
    squares = thirds(jnp.sum(values * values, axis=1))
    squares = jnp.pad(squares, ((0, 13), (0, 256)))
    pair = jnp.concatenate([mirror(keep, 0), mirror(give, 1)], axis=1)

    both = exchange(message(factor_b.T, factor_a), "z_hi")
    up = both[:, :64]
    down = both[:, 64:].reshape(4, 4, 4, 512).transpose(1, 0, 2, 3).reshape(64, 512)
    pair = jnp.concatenate([pair, squares], axis=0)
    pair, up, down = lax.optimization_barrier((pair, up, copies(down)))

    rows = [ahead(pair, "z_lo", r) for r in (1, 3)]
    ups = [ahead(up, "x", r) for r in (1, 3)]
    down = exchange(down, "z_lo").reshape(4, 4, 16, 512).transpose(1, 0, 2, 3)
    down = jnp.broadcast_to(down[:, None], (4, 4, 4, 16, 512)).reshape(16, 64, 512)
    rows, ups, down = lax.optimization_barrier((rows, ups, down))

    rows = line_copies(pair, rows[0], ahead(pair, "z_lo", 2), rows[1])
    down = exchange(down, ("x", "y"))
    up = turned([up, ups[0], ahead(up, "x", 2), ups[1]], "x").reshape(4, 4, 4, 4, 4, 512).transpose(0, 3, 2, 1, 4, 5).reshape(1024, 512)
    rows, up, down = lax.optimization_barrier((rows, up, down))

    rows = exchange(rows, "y")
    part = lax.dot_general(
        down.reshape(1024, 512), up, (((0,), (0,)), ((), ())), preferred_element_type=f32
    )
    mine = lax.dynamic_slice_in_dim(part, core * 256, 256, axis=0)
    other = lax.dynamic_slice_in_dim(part, (1 - core) * 256, 256, axis=0).astype(bf16)
    update = mine + swap(other).astype(f32)
    gain = lax.dynamic_slice_in_dim(norm_gain, client * 256, 256)[:, None]
    weight = (gain * (base_weight.astype(f32) + adapter_scale * update)).astype(bf16)

    upper, lower = weight[:128], weight[128:]
    after_a, before_b = ahead(upper, "z_hi", 1), ahead(lower, "z_hi", 3)
    after_b, before_a = ahead(lower, "z_hi", 1), ahead(upper, "z_hi", 3)
    far_a, far_b = ahead(after_a, "z_hi", 1), ahead(before_b, "z_hi", 3)
    place = jnp.stack([lax.rem(z_lo + 4 - z_hi, 4), 4 - x])
    weights = (weight, after_a, after_b, before_a, before_b, far_a, far_b)
    give = product(bf16, place, rows, *weights)
    keep = product(f32, place, rows, *weights)

    sums = keep + swap(give).astype(f32)
    query = sums[0]
    for r in (1, 2, 3):
        query = query + ahead(sums[r].astype(bf16), "x", 4 - r).astype(f32)
    squares = jnp.sum(rows[:, :, 256:259, :256].astype(f32), axis=(0, 1, 2))
    scale = lax.rsqrt(squares / width + norm_epsilon)
    return (query * scale[:, None]).astype(bf16)


def solution(mesh):
    fine = Mesh(mesh.devices.reshape(4, 4, 2, 4, 4), ("z_hi", "x", "core", "z_lo", "y"))
    client, tensor = ("z_hi", "x", "core"), ("z_lo", "y")
    return jax.shard_map(
        local,
        mesh=fine,
        in_specs=(
            P(client, tensor),
            P(),
            P(client, tensor),
            P(client + tensor, None),
            P(tensor, client),
        ),
        out_specs=P(client, tensor),
        check_vma=False,
    )
```

time: 193 us -> 176 us (0.912)
  the two profiles are of different devices: /device:TPU:1 before, /device:TPU:107 now
where the time goes in v3:
time: 176 us; the launch traced here: 175 us
  starting transfers between devices  108 us (61%)
  waiting for transfers between devices  37.9 us (22%)
  local copies, waits for them, and re-layouts  15.5 us (9%)
  Pallas kernels  9.12 us (5%)
  other arithmetic  3.43 us (2%)
    ppermute x15, starting transfers between devices, ahead(): return lax.ppermute(block, axis, [(i, (i - step) % 4) for i in range(4)])  58.4 us
    all_to_all x4, starting transfers between devices, exchange(): return lax.all_to_all(blocks, axis, split_axis=0, concat_axis=0)  33.1 us
    ppermute x15, waiting for transfers between devices, ahead(): return lax.ppermute(block, axis, [(i, (i - step) % 4) for i in range(4)])  26.4 us
    ppermute x2, starting transfers between devices, swap(): return lax.ppermute(block, 'core', [(0, 1), (1, 0)])  12.5 us
    all_to_all x4, waiting for transfers between devices, exchange(): return lax.all_to_all(blocks, axis, split_axis=0, concat_axis=0)  11.2 us
    pallas_call x2, Pallas kernels, product(): pl.pallas_call(product_kernel, out_shape=jax.ShapeDtypeStruct((4, 256, 51...  7.21 us
    unnamed x13, local copies, waits for them, and re-layouts  7.14 us
    ppermute x2, starting transfers between devices, mirror(): return lax.ppermute(block, ('x', 'core', 'y'), pairs)  3.53 us
  transfers between devices with their start and end apart: 23, of which 8 were waited for; matrix products, arithmetic and copies ran while one was open for 9% of the time, Pallas kernels for 2%

profile of v3, /device:TPU:107, one launch (start us, length us, event | category | flops | bytes accessed | tf_op | source)
XLA Modules:
  0.0 174.8 jit_solution(14723855605889879527)
XLA Ops:
  1.6 12.1 %all-to-all-start = ((bf16[4,80,512]{2,1,0:T(8,128)(2,1)}), bf16[4,80,512]{2,1,0:T(8,128)(2,1)S(1)}, u32[]{:S(2)}, u32[]{:S(2)}) async-start(bf16[4,80,512]{2,1,0:T(8,128)(2,1)} %shard_map.55), calls=%async_computation | async-start | bytes 655360 | tf_op jit(solution)/shard_map/all_to_all | solution.py:17
  15.4 2.9 %collective-permute-start.1 = (bf16[256,256]{1,0:T(8,128)(2,1)S(1)}, bf16[256,256]{1,0:T(8,128)(2,1)S(1)}, u32[]{:S(2)}, u32[]{:S(2)}) collective-permute-start(bf16[256,256]{1,0:T(8,128)(2,1)S(1)} %get-tuple-element.35), channel_id=1, source_target_pairs={{0,16},{1,48},{2,80},{3,112},{16,0},{17,32},{18,64},{19,96},{32,17... | collective-permute-start | bytes 393224 | tf_op jit(solution)/shard_map/ppermute | solution.py:45
  19.4 11.2 %all-to-all-done = bf16[4,80,512]{2,1,0:T(8,128)(2,1)S(1)} async-done(((bf16[4,80,512]{2,1,0:T(8,128)(2,1)}), bf16[4,80,512]{2,1,0:T(8,128)(2,1)S(1)}, u32[]{:S(2)}, u32[]{:S(2)}) %all-to-all-start) | async-done | bytes 327712 | tf_op jit(solution)/shard_map/all_to_all | solution.py:17
  31.5 9.9 %all-to-all-start.1 = ((bf16[4,64,512]{2,1,0:T(8,128)(2,1)}), bf16[4,64,512]{2,1,0:T(8,128)(2,1)S(1)}, u32[]{:S(2)}, u32[]{:S(2)}) async-start(bf16[4,64,512]{2,1,0:T(8,128)(2,1)} %broadcast_in_dim.7), calls=%async_computation.1 | async-start | bytes 524288 | tf_op jit(solution)/shard_map/all_to_all | solution.py:17
  41.4 2.2 %collective-permute-start.2 = (bf16[272,512]{1,0:T(8,128)(2,1)S(1)}, bf16[272,512]{1,0:T(8,128)(2,1)S(1)}, u32[]{:S(2)}, u32[]{:S(2)}) collective-permute-start(bf16[272,512]{1,0:T(8,128)(2,1)S(1)} %pad_maximum_fusion.own), channel_id=1, source_target_pairs={{0,12},{4,0},{8,4},{12,8},{1,13},{5,1},{9,5},{13,9},{2,14},{6,2},{... | collective-permute-start | bytes 835592 | tf_op jit(solution)/shard_map/ppermute | solution.py:25
  43.6 4.9 %collective-permute-start.3 = (bf16[272,512]{1,0:T(8,128)(2,1)S(1)}, bf16[272,512]{1,0:T(8,128)(2,1)S(1)}, u32[]{:S(2)}, u32[]{:S(2)}) collective-permute-start(bf16[272,512]{1,0:T(8,128)(2,1)S(1)} %pad_maximum_fusion.own), channel_id=1, source_target_pairs={{0,4},{4,8},{8,12},{12,0},{1,5},{5,9},{9,13},{13,1},{2,6},{6,10},{... | collective-permute-start | bytes 835592 | tf_op jit(solution)/shard_map/ppermute | solution.py:25
  48.5 2.2 %collective-permute-start.4 = (bf16[4,64,512]{2,1,0:T(8,128)(2,1)S(1)}, bf16[4,64,512]{2,1,0:T(8,128)(2,1)S(1)}, u32[]{:S(2)}, u32[]{:S(2)}) collective-permute-start(bf16[4,64,512]{2,1,0:T(8,128)(2,1)S(1)} %slice.39), channel_id=1, source_target_pairs={{0,96},{32,0},{64,32},{96,64},{1,97},{33,1},{65,33},{97,65},{2,98}... | collective-permute-start | bytes 786440 | tf_op jit(solution)/shard_map/ppermute | solution.py:25
  50.6 3.1 %collective-permute-start.5 = (bf16[4,64,512]{2,1,0:T(8,128)(2,1)S(1)}, bf16[4,64,512]{2,1,0:T(8,128)(2,1)S(1)}, u32[]{:S(2)}, u32[]{:S(2)}) collective-permute-start(bf16[4,64,512]{2,1,0:T(8,128)(2,1)S(1)} %slice.39), channel_id=1, source_target_pairs={{0,32},{32,64},{64,96},{96,0},{1,33},{33,65},{65,97},{97,1},{2,34}... | collective-permute-start | bytes 786440 | tf_op jit(solution)/shard_map/ppermute | solution.py:25
  53.8 5.0 %collective-permute-start.7 = (bf16[4,64,512]{2,1,0:T(8,128)(2,1)S(1)}, bf16[4,64,512]{2,1,0:T(8,128)(2,1)S(1)}, u32[]{:S(2)}, u32[]{:S(2)}) collective-permute-start(bf16[4,64,512]{2,1,0:T(8,128)(2,1)S(1)} %slice.39), channel_id=1, source_target_pairs={{0,64},{32,96},{64,0},{96,32},{1,65},{33,97},{65,1},{97,33},{2,66}... | collective-permute-start | bytes 786440 | tf_op jit(solution)/shard_map/ppermute | solution.py:25
  59.5 1.9 %collective-permute-start.6 = (bf16[272,512]{1,0:T(8,128)(2,1)S(1)}, bf16[272,512]{1,0:T(8,128)(2,1)S(1)}, u32[]{:S(2)}, u32[]{:S(2)}) collective-permute-start(bf16[272,512]{1,0:T(8,128)(2,1)S(1)} %pad_maximum_fusion.own), channel_id=1, source_target_pairs={{0,8},{4,12},{8,0},{12,4},{1,9},{5,13},{9,1},{13,5},{2,10},{6,14},... | collective-permute-start | bytes 835592 | tf_op jit(solution)/shard_map/ppermute | solution.py:25
  62.6 5.8 %all-to-all-start.2 = ((bf16[16,64,512]{2,1,0:T(8,128)(2,1)}), bf16[16,64,512]{2,1,0:T(8,128)(2,1)S(1)}, u32[]{:S(2)}, u32[]{:S(2)}) async-start(bf16[16,64,512]{2,1,0:T(8,128)(2,1)} %bitcast.7), calls=%async_computation.2 | async-start | bytes 2097152 | tf_op jit(solution)/shard_map/all_to_all | solution.py:17
  77.7 2.0 %copy-done = bf16[4,4,272,512]{3,2,1,0:T(8,128)(2,1)} copy-done((bf16[4,4,272,512]{3,2,1,0:T(8,128)(2,1)}, bf16[4,4,272,512]{3,2,1,0:T(8,128)(2,1)S(1)}, u32[]{:S(2)}) %copy-start) | copy-done | bytes 4456472
  79.7 5.3 %all-to-all-start.3 = ((bf16[4,4,272,512]{3,2,1,0:T(8,128)(2,1)}), bf16[4,4,272,512]{3,2,1,0:T(8,128)(2,1)}, u32[]{:S(2)}, u32[]{:S(2)}) async-start(bf16[4,4,272,512]{3,2,1,0:T(8,128)(2,1)} %copy-done), calls=%async_computation.3 | async-start | bytes 8912896 | tf_op jit(solution)/shard_map/all_to_all | solution.py:17
  85.8 10.1 %collective-permute-start.8 = (bf16[256,512]{1,0:T(8,128)(2,1)S(1)}, bf16[256,512]{1,0:T(8,128)(2,1)S(1)}, u32[]{:S(2)}, u32[]{:S(2)}) collective-permute-start(bf16[256,512]{1,0:T(8,128)(2,1)S(1)} %dynamic-slice_convert_fusion), channel_id=1, source_target_pairs={{0,16},{16,0},{1,17},{17,1},{2,18},{18,2},{3,19},{19,3},{4,20},{20... | collective-permute-start | bytes 786440 | tf_op jit(solution)/shard_map/ppermute | solution.py:35
  97.2 4.2 %collective-permute-start.9 = (bf16[128,512]{1,0:T(8,128)(2,1)S(1)}, bf16[128,512]{1,0:T(8,128)(2,1)S(1)}, u32[]{:S(2)}, u32[]{:S(2)}) collective-permute-start(bf16[128,512]{1,0:T(8,128)(2,1)S(1)} %get-tuple-element.33), channel_id=1, source_target_pairs={{0,384},{128,0},{256,128},{384,256},{1,385},{129,1},{257,129},{385... | collective-permute-start | bytes 393224 | tf_op jit(solution)/shard_map/ppermute | solution.py:25
  101.5 5.0 %collective-permute-start.12 = (bf16[128,512]{1,0:T(8,128)(2,1)S(1)}, bf16[128,512]{1,0:T(8,128)(2,1)S(1)}, u32[]{:S(2)}, u32[]{:S(2)}) collective-permute-start(bf16[128,512]{1,0:T(8,128)(2,1)S(1)} %get-tuple-element.32), channel_id=1, source_target_pairs={{0,128},{128,256},{256,384},{384,0},{1,129},{129,257},{257,385},{3... | collective-permute-start | bytes 393224 | tf_op jit(solution)/shard_map/ppermute | solution.py:25
  106.4 4.2 %collective-permute-start.10 = (bf16[128,512]{1,0:T(8,128)(2,1)S(1)}, bf16[128,512]{1,0:T(8,128)(2,1)S(1)}, u32[]{:S(2)}, u32[]{:S(2)}) collective-permute-start(bf16[128,512]{1,0:T(8,128)(2,1)S(1)} %get-tuple-element.32), channel_id=1, source_target_pairs={{0,384},{128,0},{256,128},{384,256},{1,385},{129,1},{257,129},{385... | collective-permute-start | bytes 393224 | tf_op jit(solution)/shard_map/ppermute | solution.py:25
  110.7 5.0 %collective-permute-start.11 = (bf16[128,512]{1,0:T(8,128)(2,1)S(1)}, bf16[128,512]{1,0:T(8,128)(2,1)S(1)}, u32[]{:S(2)}, u32[]{:S(2)}) collective-permute-start(bf16[128,512]{1,0:T(8,128)(2,1)S(1)} %get-tuple-element.33), channel_id=1, source_target_pairs={{0,128},{128,256},{256,384},{384,0},{1,129},{129,257},{257,385},{3... | collective-permute-start | bytes 393224 | tf_op jit(solution)/shard_map/ppermute | solution.py:25
  115.6 3.8 %collective-permute-done.9.after_a = bf16[128,512]{1,0:T(8,128)(2,1)S(1)} collective-permute-done((bf16[128,512]{1,0:T(8,128)(2,1)S(1)}, bf16[128,512]{1,0:T(8,128)(2,1)S(1)}, u32[]{:S(2)}, u32[]{:S(2)}) %collective-permute-start.9) | collective-permute-done | bytes 131104 | tf_op jit(solution)/shard_map/ppermute | solution.py:25
  119.5 5.2 %collective-permute-start.13 = (bf16[128,512]{1,0:T(8,128)(2,1)S(1)}, bf16[128,512]{1,0:T(8,128)(2,1)S(1)}, u32[]{:S(2)}, u32[]{:S(2)}) collective-permute-start(bf16[128,512]{1,0:T(8,128)(2,1)S(1)} %collective-permute-done.9.after_a), channel_id=1, source_target_pairs={{0,384},{128,0},{256,128},{384,256},{1,385},{129,1},{257,129},{385... | collective-permute-start | bytes 393224 | tf_op jit(solution)/shard_map/ppermute | solution.py:25
  124.7 2.2 %collective-permute-done.12.before_b = bf16[128,512]{1,0:T(8,128)(2,1)S(1)} collective-permute-done((bf16[128,512]{1,0:T(8,128)(2,1)S(1)}, bf16[128,512]{1,0:T(8,128)(2,1)S(1)}, u32[]{:S(2)}, u32[]{:S(2)}) %collective-permute-start.12) | collective-permute-done | bytes 131104 | tf_op jit(solution)/shard_map/ppermute | solution.py:25
  126.8 4.7 %collective-permute-start.14 = (bf16[128,512]{1,0:T(8,128)(2,1)S(1)}, bf16[128,512]{1,0:T(8,128)(2,1)S(1)}, u32[]{:S(2)}, u32[]{:S(2)}) collective-permute-start(bf16[128,512]{1,0:T(8,128)(2,1)S(1)} %collective-permute-done.12.before_b), channel_id=1, source_target_pairs={{0,128},{128,256},{256,384},{384,0},{1,129},{129,257},{257,385},{3... | collective-permute-start | bytes 393224 | tf_op jit(solution)/shard_map/ppermute | solution.py:25
  131.6 3.3 %collective-permute-done.11.before_a = bf16[128,512]{1,0:T(8,128)(2,1)S(1)} collective-permute-done((bf16[128,512]{1,0:T(8,128)(2,1)S(1)}, bf16[128,512]{1,0:T(8,128)(2,1)S(1)}, u32[]{:S(2)}, u32[]{:S(2)}) %collective-permute-start.11) | collective-permute-done | bytes 131104 | tf_op jit(solution)/shard_map/ppermute | solution.py:25
  134.9 6.4 %collective-permute-done.13.far_a = bf16[128,512]{1,0:T(8,128)(2,1)S(1)} collective-permute-done((bf16[128,512]{1,0:T(8,128)(2,1)S(1)}, bf16[128,512]{1,0:T(8,128)(2,1)S(1)}, u32[]{:S(2)}, u32[]{:S(2)}) %collective-permute-start.13) | collective-permute-done | bytes 131104 | tf_op jit(solution)/shard_map/ppermute | solution.py:25
  141.2 3.6 %shard_map.58 = bf16[4,256,512]{2,1,0:T(8,128)(2,1)S(1)} custom-call(s32[2]{0:T(128)S(1)} %pad_add_fusion.place, bf16[4,4,272,512]{3,2,1,0:T(8,128)(2,1)} %all-to-all-done.3.rows, bf16[256,512]{1,0:T(8,128)(2,1)S(1)} %multiply_convert_fusion.own, bf16[128,512]{1,0:T(8,128)(2,1)S(1)} %collective-permute-done.9.after_a, ...), custom_call_target="tpu_custom_call" | custom-call | flops 1073741824 | bytes 7340032 | tf_op jit(solution)/shard_map/pallas_call | solution.py:96
  144.9 2.4 %collective-permute-start.15 = (bf16[4,256,512]{2,1,0:T(8,128)(2,1)S(1)}, bf16[4,256,512]{2,1,0:T(8,128)(2,1)S(1)}, u32[]{:S(2)}, u32[]{:S(2)}) collective-permute-start(bf16[4,256,512]{2,1,0:T(8,128)(2,1)S(1)} %shard_map.58), channel_id=1, source_target_pairs={{0,16},{16,0},{1,17},{17,1},{2,18},{18,2},{3,19},{19,3},{4,20},{20... | collective-permute-start | bytes 3145736 | tf_op jit(solution)/shard_map/ppermute | solution.py:35
  147.3 3.6 %shard_map.57 = f32[4,256,512]{2,1,0:T(8,128)S(1)} custom-call(s32[2]{0:T(128)S(1)} %pad_add_fusion.place, bf16[4,4,272,512]{3,2,1,0:T(8,128)(2,1)} %all-to-all-done.3.rows, bf16[256,512]{1,0:T(8,128)(2,1)S(1)} %multiply_convert_fusion.own, bf16[128,512]{1,0:T(8,128)(2,1)S(1)} %collective-permute-done.9.after_a, ...), custom_call_target="tpu_custom_call" | custom-call | flops 1073741824 | bytes 7340032 | tf_op jit(solution)/shard_map/pallas_call | solution.py:96
  151.3 5.3 %collective-permute-start.16 = (bf16[256,512]{1,0:T(8,128)(2,1)S(1)}, bf16[256,512]{1,0:T(8,128)(2,1)S(1)}, u32[]{:S(2)}, u32[]{:S(2)}) collective-permute-start(bf16[256,512]{1,0:T(8,128)(2,1)S(1)} %get-tuple-element.29), channel_id=1, source_target_pairs={{0,32},{32,64},{64,96},{96,0},{1,33},{33,65},{65,97},{97,1},{2,34}... | collective-permute-start | bytes 786440 | tf_op jit(solution)/shard_map/ppermute | solution.py:25
  156.7 3.7 %collective-permute-start.17 = (bf16[256,512]{1,0:T(8,128)(2,1)S(1)}, bf16[256,512]{1,0:T(8,128)(2,1)S(1)}, u32[]{:S(2)}, u32[]{:S(2)}) collective-permute-start(bf16[256,512]{1,0:T(8,128)(2,1)S(1)} %get-tuple-element.31), channel_id=1, source_target_pairs={{0,64},{32,96},{64,0},{96,32},{1,65},{33,97},{65,1},{97,33},{2,66}... | collective-permute-start | bytes 786440 | tf_op jit(solution)/shard_map/ppermute | solution.py:25
  160.4 1.9 %collective-permute-start.18 = (bf16[256,512]{1,0:T(8,128)(2,1)S(1)}, bf16[256,512]{1,0:T(8,128)(2,1)S(1)}, u32[]{:S(2)}, u32[]{:S(2)}) collective-permute-start(bf16[256,512]{1,0:T(8,128)(2,1)S(1)} %get-tuple-element.30), channel_id=1, source_target_pairs={{0,96},{32,0},{64,32},{96,64},{1,97},{33,1},{65,33},{97,65},{2,98}... | collective-permute-start | bytes 786440 | tf_op jit(solution)/shard_map/ppermute | solution.py:25
  163.2 4.5 %collective-permute-done.17 = bf16[256,512]{1,0:T(8,128)(2,1)S(1)} collective-permute-done((bf16[256,512]{1,0:T(8,128)(2,1)S(1)}, bf16[256,512]{1,0:T(8,128)(2,1)S(1)}, u32[]{:S(2)}, u32[]{:S(2)}) %collective-permute-start.17) | collective-permute-done | bytes 262176 | tf_op jit(solution)/shard_map/ppermute | solution.py:25
  167.7 6.2 %collective-permute-done.18 = bf16[256,512]{1,0:T(8,128)(2,1)S(1)} collective-permute-done((bf16[256,512]{1,0:T(8,128)(2,1)S(1)}, bf16[256,512]{1,0:T(8,128)(2,1)S(1)}, u32[]{:S(2)}, u32[]{:S(2)}) %collective-permute-start.18) | collective-permute-done | bytes 262176 | tf_op jit(solution)/shard_map/ppermute | solution.py:25
  (60 shorter events, 20.6 us)
Async XLA Ops:
  1.6 29.0 %all-to-all-start = ((bf16[4,80,512]{2,1,0:T(8,128)(2,1)}), bf16[4,80,512]{2,1,0:T(8,128)(2,1)S(1)}, u32[]{:S(2)}, u32[]{:S(2)}) async-start(bf16[4,80,512]{2,1,0:T(8,128)(2,1)} %shard_map.55), calls=%async_computation | async-start | bytes 655360 | tf_op jit(solution)/shard_map/all_to_all | solution.py:17
  14.7 4.7 %collective-permute-start = (bf16[256,256]{1,0:T(8,128)(2,1)S(1)}, bf16[256,256]{1,0:T(8,128)(2,1)S(1)}, u32[]{:S(2)}, u32[]{:S(2)}) collective-permute-start(bf16[256,256]{1,0:T(8,128)(2,1)S(1)} %get-tuple-element.34), channel_id=1, source_target_pairs={{0,0},{1,32},{2,64},{3,96},{16,16},{17,48},{18,80},{19,112},{32,1}... | collective-permute-start | bytes 393224 | tf_op jit(solution)/shard_map/ppermute | solution.py:45
  15.4 4.0 %collective-permute-start.1 = (bf16[256,256]{1,0:T(8,128)(2,1)S(1)}, bf16[256,256]{1,0:T(8,128)(2,1)S(1)}, u32[]{:S(2)}, u32[]{:S(2)}) collective-permute-start(bf16[256,256]{1,0:T(8,128)(2,1)S(1)} %get-tuple-element.35), channel_id=1, source_target_pairs={{0,16},{1,48},{2,80},{3,112},{16,0},{17,32},{18,64},{19,96},{32,17... | collective-permute-start | bytes 393224 | tf_op jit(solution)/shard_map/ppermute | solution.py:45
  31.5 28.0 %all-to-all-start.1 = ((bf16[4,64,512]{2,1,0:T(8,128)(2,1)}), bf16[4,64,512]{2,1,0:T(8,128)(2,1)S(1)}, u32[]{:S(2)}, u32[]{:S(2)}) async-start(bf16[4,64,512]{2,1,0:T(8,128)(2,1)} %broadcast_in_dim.7), calls=%async_computation.1 | async-start | bytes 524288 | tf_op jit(solution)/shard_map/all_to_all | solution.py:17
  41.4 20.1 %collective-permute-start.2 = (bf16[272,512]{1,0:T(8,128)(2,1)S(1)}, bf16[272,512]{1,0:T(8,128)(2,1)S(1)}, u32[]{:S(2)}, u32[]{:S(2)}) collective-permute-start(bf16[272,512]{1,0:T(8,128)(2,1)S(1)} %pad_maximum_fusion.own), channel_id=1, source_target_pairs={{0,12},{4,0},{8,4},{12,8},{1,13},{5,1},{9,5},{13,9},{2,14},{6,2},{... | collective-permute-start | bytes 835592 | tf_op jit(solution)/shard_map/ppermute | solution.py:25
  43.6 17.9 %collective-permute-start.3 = (bf16[272,512]{1,0:T(8,128)(2,1)S(1)}, bf16[272,512]{1,0:T(8,128)(2,1)S(1)}, u32[]{:S(2)}, u32[]{:S(2)}) collective-permute-start(bf16[272,512]{1,0:T(8,128)(2,1)S(1)} %pad_maximum_fusion.own), channel_id=1, source_target_pairs={{0,4},{4,8},{8,12},{12,0},{1,5},{5,9},{9,13},{13,1},{2,6},{6,10},{... | collective-permute-start | bytes 835592 | tf_op jit(solution)/shard_map/ppermute | solution.py:25
  48.5 11.0 %collective-permute-start.4 = (bf16[4,64,512]{2,1,0:T(8,128)(2,1)S(1)}, bf16[4,64,512]{2,1,0:T(8,128)(2,1)S(1)}, u32[]{:S(2)}, u32[]{:S(2)}) collective-permute-start(bf16[4,64,512]{2,1,0:T(8,128)(2,1)S(1)} %slice.39), channel_id=1, source_target_pairs={{0,96},{32,0},{64,32},{96,64},{1,97},{33,1},{65,33},{97,65},{2,98}... | collective-permute-start | bytes 786440 | tf_op jit(solution)/shard_map/ppermute | solution.py:25
  50.6 10.8 %collective-permute-start.5 = (bf16[4,64,512]{2,1,0:T(8,128)(2,1)S(1)}, bf16[4,64,512]{2,1,0:T(8,128)(2,1)S(1)}, u32[]{:S(2)}, u32[]{:S(2)}) collective-permute-start(bf16[4,64,512]{2,1,0:T(8,128)(2,1)S(1)} %slice.39), channel_id=1, source_target_pairs={{0,32},{32,64},{64,96},{96,0},{1,33},{33,65},{65,97},{97,1},{2,34}... | collective-permute-start | bytes 786440 | tf_op jit(solution)/shard_map/ppermute | solution.py:25
  53.8 15.3 %collective-permute-start.7 = (bf16[4,64,512]{2,1,0:T(8,128)(2,1)S(1)}, bf16[4,64,512]{2,1,0:T(8,128)(2,1)S(1)}, u32[]{:S(2)}, u32[]{:S(2)}) collective-permute-start(bf16[4,64,512]{2,1,0:T(8,128)(2,1)S(1)} %slice.39), channel_id=1, source_target_pairs={{0,64},{32,96},{64,0},{96,32},{1,65},{33,97},{65,1},{97,33},{2,66}... | collective-permute-start | bytes 786440 | tf_op jit(solution)/shard_map/ppermute | solution.py:25
  59.5 17.8 %collective-permute-start.6 = (bf16[272,512]{1,0:T(8,128)(2,1)S(1)}, bf16[272,512]{1,0:T(8,128)(2,1)S(1)}, u32[]{:S(2)}, u32[]{:S(2)}) collective-permute-start(bf16[272,512]{1,0:T(8,128)(2,1)S(1)} %pad_maximum_fusion.own), channel_id=1, source_target_pairs={{0,8},{4,12},{8,0},{12,4},{1,9},{5,13},{9,1},{13,5},{2,10},{6,14},... | collective-permute-start | bytes 835592 | tf_op jit(solution)/shard_map/ppermute | solution.py:25
  62.6 17.1 %all-to-all-start.2 = ((bf16[16,64,512]{2,1,0:T(8,128)(2,1)}), bf16[16,64,512]{2,1,0:T(8,128)(2,1)S(1)}, u32[]{:S(2)}, u32[]{:S(2)}) async-start(bf16[16,64,512]{2,1,0:T(8,128)(2,1)} %bitcast.7), calls=%async_computation.2 | async-start | bytes 2097152 | tf_op jit(solution)/shard_map/all_to_all | solution.py:17
  77.6 2.1 %copy-start = (bf16[4,4,272,512]{3,2,1,0:T(8,128)(2,1)}, bf16[4,4,272,512]{3,2,1,0:T(8,128)(2,1)S(1)}, u32[]{:S(2)}) copy-start(bf16[4,4,272,512]{3,2,1,0:T(8,128)(2,1)S(1)} %shard_map.56) | copy-start | bytes 13369348
  79.7 5.3 %copy-start.1 = (bf16[1024,512]{1,0:T(8,128)(2,1)S(1)}, bf16[1024,512]{1,0:T(8,128)(2,1)}, u32[]{:S(2)}) copy-start(bf16[1024,512]{1,0:T(8,128)(2,1)} %reshape.69) | copy-start | bytes 3145732
  79.7 61.5 %all-to-all-start.3 = ((bf16[4,4,272,512]{3,2,1,0:T(8,128)(2,1)}), bf16[4,4,272,512]{3,2,1,0:T(8,128)(2,1)}, u32[]{:S(2)}, u32[]{:S(2)}) async-start(bf16[4,4,272,512]{3,2,1,0:T(8,128)(2,1)} %copy-done), calls=%async_computation.3 | async-start | bytes 8912896 | tf_op jit(solution)/shard_map/all_to_all | solution.py:17
  85.0 12.1 %copy-start.2 = (bf16[256,512]{1,0:T(8,128)(2,1)S(1)}, bf16[256,512]{1,0:T(8,128)(2,1)}, u32[]{:S(2)}) copy-start(bf16[256,512]{1,0:T(8,128)(2,1)} %param.7) | copy-start | bytes 786436
  85.8 11.3 %collective-permute-start.8 = (bf16[256,512]{1,0:T(8,128)(2,1)S(1)}, bf16[256,512]{1,0:T(8,128)(2,1)S(1)}, u32[]{:S(2)}, u32[]{:S(2)}) collective-permute-start(bf16[256,512]{1,0:T(8,128)(2,1)S(1)} %dynamic-slice_convert_fusion), channel_id=1, source_target_pairs={{0,16},{16,0},{1,17},{17,1},{2,18},{18,2},{3,19},{19,3},{4,20},{20... | collective-permute-start | bytes 786440 | tf_op jit(solution)/shard_map/ppermute | solution.py:35
  97.2 22.2 %collective-permute-start.9 = (bf16[128,512]{1,0:T(8,128)(2,1)S(1)}, bf16[128,512]{1,0:T(8,128)(2,1)S(1)}, u32[]{:S(2)}, u32[]{:S(2)}) collective-permute-start(bf16[128,512]{1,0:T(8,128)(2,1)S(1)} %get-tuple-element.33), channel_id=1, source_target_pairs={{0,384},{128,0},{256,128},{384,256},{1,385},{129,1},{257,129},{385... | collective-permute-start | bytes 393224 | tf_op jit(solution)/shard_map/ppermute | solution.py:25
  101.5 25.4 %collective-permute-start.12 = (bf16[128,512]{1,0:T(8,128)(2,1)S(1)}, bf16[128,512]{1,0:T(8,128)(2,1)S(1)}, u32[]{:S(2)}, u32[]{:S(2)}) collective-permute-start(bf16[128,512]{1,0:T(8,128)(2,1)S(1)} %get-tuple-element.32), channel_id=1, source_target_pairs={{0,128},{128,256},{256,384},{384,0},{1,129},{129,257},{257,385},{3... | collective-permute-start | bytes 393224 | tf_op jit(solution)/shard_map/ppermute | solution.py:25
  106.4 25.2 %collective-permute-start.10 = (bf16[128,512]{1,0:T(8,128)(2,1)S(1)}, bf16[128,512]{1,0:T(8,128)(2,1)S(1)}, u32[]{:S(2)}, u32[]{:S(2)}) collective-permute-start(bf16[128,512]{1,0:T(8,128)(2,1)S(1)} %get-tuple-element.32), channel_id=1, source_target_pairs={{0,384},{128,0},{256,128},{384,256},{1,385},{129,1},{257,129},{385... | collective-permute-start | bytes 393224 | tf_op jit(solution)/shard_map/ppermute | solution.py:25
  110.7 24.2 %collective-permute-start.11 = (bf16[128,512]{1,0:T(8,128)(2,1)S(1)}, bf16[128,512]{1,0:T(8,128)(2,1)S(1)}, u32[]{:S(2)}, u32[]{:S(2)}) collective-permute-start(bf16[128,512]{1,0:T(8,128)(2,1)S(1)} %get-tuple-element.33), channel_id=1, source_target_pairs={{0,128},{128,256},{256,384},{384,0},{1,129},{129,257},{257,385},{3... | collective-permute-start | bytes 393224 | tf_op jit(solution)/shard_map/ppermute | solution.py:25
  119.5 21.8 %collective-permute-start.13 = (bf16[128,512]{1,0:T(8,128)(2,1)S(1)}, bf16[128,512]{1,0:T(8,128)(2,1)S(1)}, u32[]{:S(2)}, u32[]{:S(2)}) collective-permute-start(bf16[128,512]{1,0:T(8,128)(2,1)S(1)} %collective-permute-done.9.after_a), channel_id=1, source_target_pairs={{0,384},{128,0},{256,128},{384,256},{1,385},{129,1},{257,129},{385... | collective-permute-start | bytes 393224 | tf_op jit(solution)/shard_map/ppermute | solution.py:25
  126.8 14.4 %collective-permute-start.14 = (bf16[128,512]{1,0:T(8,128)(2,1)S(1)}, bf16[128,512]{1,0:T(8,128)(2,1)S(1)}, u32[]{:S(2)}, u32[]{:S(2)}) collective-permute-start(bf16[128,512]{1,0:T(8,128)(2,1)S(1)} %collective-permute-done.12.before_b), channel_id=1, source_target_pairs={{0,128},{128,256},{256,384},{384,0},{1,129},{129,257},{257,385},{3... | collective-permute-start | bytes 393224 | tf_op jit(solution)/shard_map/ppermute | solution.py:25
  144.9 6.0 %collective-permute-start.15 = (bf16[4,256,512]{2,1,0:T(8,128)(2,1)S(1)}, bf16[4,256,512]{2,1,0:T(8,128)(2,1)S(1)}, u32[]{:S(2)}, u32[]{:S(2)}) collective-permute-start(bf16[4,256,512]{2,1,0:T(8,128)(2,1)S(1)} %shard_map.58), channel_id=1, source_target_pairs={{0,16},{16,0},{1,17},{17,1},{2,18},{18,2},{3,19},{19,3},{4,20},{20... | collective-permute-start | bytes 3145736 | tf_op jit(solution)/shard_map/ppermute | solution.py:35
  151.3 11.9 %collective-permute-start.16 = (bf16[256,512]{1,0:T(8,128)(2,1)S(1)}, bf16[256,512]{1,0:T(8,128)(2,1)S(1)}, u32[]{:S(2)}, u32[]{:S(2)}) collective-permute-start(bf16[256,512]{1,0:T(8,128)(2,1)S(1)} %get-tuple-element.29), channel_id=1, source_target_pairs={{0,32},{32,64},{64,96},{96,0},{1,33},{33,65},{65,97},{97,1},{2,34}... | collective-permute-start | bytes 786440 | tf_op jit(solution)/shard_map/ppermute | solution.py:25
  156.7 11.1 %collective-permute-start.17 = (bf16[256,512]{1,0:T(8,128)(2,1)S(1)}, bf16[256,512]{1,0:T(8,128)(2,1)S(1)}, u32[]{:S(2)}, u32[]{:S(2)}) collective-permute-start(bf16[256,512]{1,0:T(8,128)(2,1)S(1)} %get-tuple-element.31), channel_id=1, source_target_pairs={{0,64},{32,96},{64,0},{96,32},{1,65},{33,97},{65,1},{97,33},{2,66}... | collective-permute-start | bytes 786440 | tf_op jit(solution)/shard_map/ppermute | solution.py:25
  160.4 13.5 %collective-permute-start.18 = (bf16[256,512]{1,0:T(8,128)(2,1)S(1)}, bf16[256,512]{1,0:T(8,128)(2,1)S(1)}, u32[]{:S(2)}, u32[]{:S(2)}) collective-permute-start(bf16[256,512]{1,0:T(8,128)(2,1)S(1)} %get-tuple-element.30), channel_id=1, source_target_pairs={{0,96},{32,0},{64,32},{96,64},{1,97},{33,1},{65,33},{97,65},{2,98}... | collective-permute-start | bytes 786440 | tf_op jit(solution)/shard_map/ppermute | solution.py:25

commit v4 on v3

--- a/solution.py
+++ b/solution.py
@@ -68,42 +68,59 @@
         out_shape=jax.ShapeDtypeStruct((4, 4) + blocks[0].shape, bf16),
         in_specs=[vmem] * 4,
         out_specs=vmem,
-        compiler_params=pltpu.CompilerParams(vmem_limit_bytes=40 * 2**20),
+        compiler_params=pltpu.CompilerParams(vmem_limit_bytes=14 * 2**20),
         cost_estimate=pl.CostEstimate(flops=0, bytes_accessed=6 * 2**20, transcendentals=0),
     )(*blocks)
 
 
-def product_kernel(place, rows, own, after_a, after_b, before_a, before_b, far_a, far_b, out, weights):
-    weights[0] = own[...]
-    for step, (upper, lower) in enumerate(
-        ((after_a, after_b), (far_a, far_b), (before_a, before_b)), start=1
-    ):
-        weights[step, :128] = upper[...]
-        weights[step, 128:] = lower[...]
-    columns = 256 if out.dtype == bf16 else 0
+def first_kernel(place, rows, own, after_a, after_b, keep, give, keep_rows, give_rows):
+    right = jnp.concatenate([own[...], after_a[...], after_b[...]], axis=0)
+    where = [lax.rem(place[0] + step, 4) for step in (0, 1, 3, 2)]
     for y in range(4):
-        total = None
-        for z in range(4):
-            left = rows[y, z, :256, columns : columns + 256]
-            right = weights[lax.rem(place[0] + z, 4)]
-            term = jnp.dot(left, right, preferred_element_type=f32)
-            total = term if total is None else total + term
-        out[lax.rem(place[1] + y, 4)] = total.astype(out.dtype)
-
-
-def product(kind, place, rows, *weights):
-    vmem = pl.BlockSpec(memory_space=pltpu.VMEM)
-    return pl.pallas_call(
-        product_kernel,
-        out_shape=jax.ShapeDtypeStruct((4, 256, 512), kind),
-        in_specs=[pl.BlockSpec(memory_space=pltpu.SMEM)] + [vmem] * 8,
-        out_specs=vmem,
-        scratch_shapes=[pltpu.VMEM((4, 256, 512), bf16)],
-        compiler_params=pltpu.CompilerParams(vmem_limit_bytes=40 * 2**20),
+        for core, (out, rest) in enumerate(((keep, keep_rows), (give, give_rows))):
+            blocks = [rows[y, z, :256, core * 256 : core * 256 + 256] for z in where]
+            left = jnp.concatenate(blocks[:2], axis=1)
+            out[y] = jnp.dot(left, right, preferred_element_type=f32)
+            rest[y, :, :256] = blocks[2]
+            rest[y, :, 256:] = blocks[3]
+
+
+def first_product(place, rows, *weights):
+    vmem = pl.BlockSpec(memory_space=pltpu.VMEM)
+    part = jax.ShapeDtypeStruct((4, 256, 512), f32)
+    left = jax.ShapeDtypeStruct((4, 256, 512), bf16)
+    return pl.pallas_call(
+        first_kernel,
+        out_shape=(part, part, left, left),
+        in_specs=[pl.BlockSpec(memory_space=pltpu.SMEM)] + [vmem] * 4,
+        out_specs=(vmem,) * 4,
+        compiler_params=pltpu.CompilerParams(vmem_limit_bytes=20 * 2**20),
         cost_estimate=pl.CostEstimate(
-            flops=2048 * 1024 * 512, bytes_accessed=7 * 2**20, transcendentals=0
+            flops=2 * 2048 * 512 * 512, bytes_accessed=11 * 2**20, transcendentals=0
         ),
     )(place, rows, *weights)
+
+
+def last_kernel(part, left, before_a, before_b, far_a, far_b, out):
+    pieces = (before_a, before_b, far_a, far_b)
+    right = jnp.concatenate([piece[...] for piece in pieces], axis=0)
+    for y in range(4):
+        total = part[y] + jnp.dot(left[y], right, preferred_element_type=f32)
+        out[y] = total.astype(out.dtype)
+
+
+def last_product(kind, *operands):
+    vmem = pl.BlockSpec(memory_space=pltpu.VMEM)
+    return pl.pallas_call(
+        last_kernel,
+        out_shape=jax.ShapeDtypeStruct((4, 256, 512), kind),
+        in_specs=[vmem] * 6,
+        out_specs=vmem,
+        compiler_params=pltpu.CompilerParams(vmem_limit_bytes=14 * 2**20),
+        cost_estimate=pl.CostEstimate(
+            flops=2048 * 512 * 512, bytes_accessed=5 * 2**20, transcendentals=0
+        ),
+    )(*operands)
 
 
 def message_kernel(up, down, out):
@@ -139,45 +156,46 @@
     pair = jnp.concatenate([mirror(keep, 0), mirror(give, 1)], axis=1)
 
     both = exchange(message(factor_b.T, factor_a), "z_hi")
-    up = both[:, :64]
-    down = both[:, 64:].reshape(4, 4, 4, 512).transpose(1, 0, 2, 3).reshape(64, 512)
+    up = both[:, :64].reshape(4, 4, 4, 4, 512).transpose(2, 1, 0, 3, 4).reshape(256, 512)
+    down = both[:, 64:].reshape(4, 4, 4, 512).transpose(1, 0, 2, 3).reshape(4, 16, 512)
+    down = jnp.broadcast_to(down[:, None], (4, 4, 16, 512)).reshape(16, 16, 512)
     pair = jnp.concatenate([pair, squares], axis=0)
-    pair, up, down = lax.optimization_barrier((pair, up, copies(down)))
+    pair, up, down = lax.optimization_barrier((pair, up, down))
 
     rows = [ahead(pair, "z_lo", r) for r in (1, 3)]
     ups = [ahead(up, "x", r) for r in (1, 3)]
-    down = exchange(down, "z_lo").reshape(4, 4, 16, 512).transpose(1, 0, 2, 3)
-    down = jnp.broadcast_to(down[:, None], (4, 4, 4, 16, 512)).reshape(16, 64, 512)
+    down = copies(exchange(down, ("x", "z_lo")).reshape(256, 512))
     rows, ups, down = lax.optimization_barrier((rows, ups, down))
 
     rows = line_copies(pair, rows[0], ahead(pair, "z_lo", 2), rows[1])
-    down = exchange(down, ("x", "y"))
-    up = turned([up, ups[0], ahead(up, "x", 2), ups[1]], "x").reshape(4, 4, 4, 4, 4, 512).transpose(0, 3, 2, 1, 4, 5).reshape(1024, 512)
-    rows, up, down = lax.optimization_barrier((rows, up, down))
-
-    rows = exchange(rows, "y")
+    down = exchange(down, "y")
+    up = turned([up, ups[0], ahead(up, "x", 2), ups[1]], "x")
+    up = up.reshape(4, 4, 64, 512).transpose(1, 0, 2, 3).reshape(1024, 512)
+    up, down = lax.optimization_barrier((up, down))
+
     part = lax.dot_general(
         down.reshape(1024, 512), up, (((0,), (0,)), ((), ())), preferred_element_type=f32
     )
     mine = lax.dynamic_slice_in_dim(part, core * 256, 256, axis=0)
     other = lax.dynamic_slice_in_dim(part, (1 - core) * 256, 256, axis=0).astype(bf16)
+    rows, other = lax.optimization_barrier((rows, other))
+    rows = exchange(rows, "y")
     update = mine + swap(other).astype(f32)
     gain = lax.dynamic_slice_in_dim(norm_gain, client * 256, 256)[:, None]
     weight = (gain * (base_weight.astype(f32) + adapter_scale * update)).astype(bf16)
 
     upper, lower = weight[:128], weight[128:]
-    after_a, before_b = ahead(upper, "z_hi", 1), ahead(lower, "z_hi", 3)
-    after_b, before_a = ahead(lower, "z_hi", 1), ahead(upper, "z_hi", 3)
-    far_a, far_b = ahead(after_a, "z_hi", 1), ahead(before_b, "z_hi", 3)
-    place = jnp.stack([lax.rem(z_lo + 4 - z_hi, 4), 4 - x])
-    weights = (weight, after_a, after_b, before_a, before_b, far_a, far_b)
-    give = product(bf16, place, rows, *weights)
-    keep = product(f32, place, rows, *weights)
+    before_a, after_b = ahead(upper, "z_hi", 3), ahead(lower, "z_hi", 1)
+    before_b, after_a = ahead(lower, "z_hi", 3), ahead(upper, "z_hi", 1)
+    far_a, far_b = ahead(before_a, "z_hi", 3), ahead(after_b, "z_hi", 1)
+    place = lax.rem(z_hi + 4 - z_lo, 4)[None]
+    keep, give, keep_rows, give_rows = first_product(place, rows, weight, after_a, after_b)
+    rest = (before_a, before_b, far_a, far_b)
+    give = last_product(bf16, give, give_rows, *rest)
+    keep = last_product(f32, keep, keep_rows, *rest)
 
     sums = keep + swap(give).astype(f32)
-    query = sums[0]
-    for r in (1, 2, 3):
-        query = query + ahead(sums[r].astype(bf16), "x", 4 - r).astype(f32)
+    query = jnp.sum(exchange(sums.astype(bf16), "x").astype(f32), axis=0)
     squares = jnp.sum(rows[:, :, 256:259, :256].astype(f32), axis=(0, 1, 2))
     scale = lax.rsqrt(squares / width + norm_epsilon)
     return (query * scale[:, None]).astype(bf16)

time: 176 us -> 176 us (level)
  the two profiles are of different devices: /device:TPU:107 before, /device:TPU:1 now
where the time goes in v4:
time: 176 us; the launch traced here: 174 us
  starting transfers between devices  106 us (60%)
  waiting for transfers between devices  42.1 us (24%)
  local copies, waits for them, and re-layouts  14.1 us (8%)
  Pallas kernels  6.97 us (4%)
  other arithmetic  4.42 us (3%)
    ppermute x12, starting transfers between devices, ahead(): return lax.ppermute(block, axis, [(i, (i - step) % 4) for i in range(4)])  46.9 us
    all_to_all x5, starting transfers between devices, exchange(): return lax.all_to_all(blocks, axis, split_axis=0, concat_axis=0)  43.3 us
    all_to_all x5, waiting for transfers between devices, exchange(): return lax.all_to_all(blocks, axis, split_axis=0, concat_axis=0)  32.9 us
    ppermute x2, starting transfers between devices, swap(): return lax.ppermute(block, 'core', [(0, 1), (1, 0)])  11.9 us
    unnamed x15, local copies, waits for them, and re-layouts  8.03 us
    ppermute x12, waiting for transfers between devices, ahead(): return lax.ppermute(block, axis, [(i, (i - step) % 4) for i in range(4)])  7.28 us
    pallas_call x1, Pallas kernels, first_product(): pl.pallas_call(first_kernel, out_shape=(part, part, left, left), in_specs...  3.64 us
    ppermute x2, starting transfers between devices, mirror(): return lax.ppermute(block, ('x', 'core', 'y'), pairs)  3.53 us
  transfers between devices with their start and end apart: 21, of which 9 were waited for; matrix products, arithmetic and copies ran while one was open for 7% of the time, Pallas kernels for 3%

profile of v4, /device:TPU:1, one launch (start us, length us, event | category | flops | bytes accessed | tf_op | source)
XLA Modules:
  0.0 174.3 jit_solution(15417982603913269490)
XLA Ops:
  0.0 1.6 shard_map.55
  1.6 15.6 %all-to-all-start = ((bf16[4,80,512]{2,1,0:T(8,128)(2,1)}), bf16[4,80,512]{2,1,0:T(8,128)(2,1)S(1)}, u32[]{:S(2)}, u32[]{:S(2)}) async-start(bf16[4,80,512]{2,1,0:T(8,128)(2,1)} %shard_map.55), calls=%async_computation | async-start | bytes 655360 | tf_op jit(solution)/shard_map/all_to_all | solution.py:17
  18.9 2.9 %collective-permute-start.1 = (bf16[256,256]{1,0:T(8,128)(2,1)S(1)}, bf16[256,256]{1,0:T(8,128)(2,1)S(1)}, u32[]{:S(2)}, u32[]{:S(2)}) collective-permute-start(bf16[256,256]{1,0:T(8,128)(2,1)S(1)} %get-tuple-element.40), channel_id=1, source_target_pairs={{0,16},{1,48},{2,80},{3,112},{16,0},{17,32},{18,64},{19,96},{32,17... | collective-permute-start | bytes 393224 | tf_op jit(solution)/shard_map/ppermute | solution.py:45
  23.0 11.2 %all-to-all-done = bf16[4,80,512]{2,1,0:T(8,128)(2,1)S(1)} async-done(((bf16[4,80,512]{2,1,0:T(8,128)(2,1)}), bf16[4,80,512]{2,1,0:T(8,128)(2,1)S(1)}, u32[]{:S(2)}, u32[]{:S(2)}) %all-to-all-start) | async-done | bytes 327712 | tf_op jit(solution)/shard_map/all_to_all | solution.py:17
  35.3 10.9 %all-to-all-start.1 = ((bf16[16,16,512]{2,1,0:T(8,128)(2,1)}), bf16[16,16,512]{2,1,0:T(8,128)(2,1)S(1)}, u32[]{:S(2)}, u32[]{:S(2)}) async-start(bf16[16,16,512]{2,1,0:T(8,128)(2,1)} %bitcast.6), calls=%async_computation.1 | async-start | bytes 524288 | tf_op jit(solution)/shard_map/all_to_all | solution.py:17
  46.2 3.3 %collective-permute-start.3 = (bf16[272,512]{1,0:T(8,128)(2,1)S(1)}, bf16[272,512]{1,0:T(8,128)(2,1)S(1)}, u32[]{:S(2)}, u32[]{:S(2)}) collective-permute-start(bf16[272,512]{1,0:T(8,128)(2,1)S(1)} %pad_maximum_fusion.own), channel_id=1, source_target_pairs={{0,4},{4,8},{8,12},{12,0},{1,5},{5,9},{9,13},{13,1},{2,6},{6,10},{... | collective-permute-start | bytes 835592 | tf_op jit(solution)/shard_map/ppermute | solution.py:25
  49.4 3.8 %collective-permute-start.2 = (bf16[272,512]{1,0:T(8,128)(2,1)S(1)}, bf16[272,512]{1,0:T(8,128)(2,1)S(1)}, u32[]{:S(2)}, u32[]{:S(2)}) collective-permute-start(bf16[272,512]{1,0:T(8,128)(2,1)S(1)} %pad_maximum_fusion.own), channel_id=1, source_target_pairs={{0,12},{4,0},{8,4},{12,8},{1,13},{5,1},{9,5},{13,9},{2,14},{6,2},{... | collective-permute-start | bytes 835592 | tf_op jit(solution)/shard_map/ppermute | solution.py:25
  53.3 3.3 %collective-permute-start.5 = (bf16[256,512]{1,0:T(8,128)(2,1)S(1)}, bf16[256,512]{1,0:T(8,128)(2,1)S(1)}, u32[]{:S(2)}, u32[]{:S(2)}) collective-permute-start(bf16[256,512]{1,0:T(8,128)(2,1)S(1)} %reshape.66), channel_id=1, source_target_pairs={{0,32},{32,64},{64,96},{96,0},{1,33},{33,65},{65,97},{97,1},{2,34}... | collective-permute-start | bytes 786440 | tf_op jit(solution)/shard_map/ppermute | solution.py:25
  56.5 3.2 %collective-permute-start.4 = (bf16[256,512]{1,0:T(8,128)(2,1)S(1)}, bf16[256,512]{1,0:T(8,128)(2,1)S(1)}, u32[]{:S(2)}, u32[]{:S(2)}) collective-permute-start(bf16[256,512]{1,0:T(8,128)(2,1)S(1)} %reshape.66), channel_id=1, source_target_pairs={{0,96},{32,0},{64,32},{96,64},{1,97},{33,1},{65,33},{97,65},{2,98}... | collective-permute-start | bytes 786440 | tf_op jit(solution)/shard_map/ppermute | solution.py:25
  59.8 3.6 %collective-permute-start.7 = (bf16[256,512]{1,0:T(8,128)(2,1)S(1)}, bf16[256,512]{1,0:T(8,128)(2,1)S(1)}, u32[]{:S(2)}, u32[]{:S(2)}) collective-permute-start(bf16[256,512]{1,0:T(8,128)(2,1)S(1)} %reshape.66), channel_id=1, source_target_pairs={{0,64},{32,96},{64,0},{96,32},{1,65},{33,97},{65,1},{97,33},{2,66}... | collective-permute-start | bytes 786440 | tf_op jit(solution)/shard_map/ppermute | solution.py:25
  64.1 2.2 %collective-permute-start.6 = (bf16[272,512]{1,0:T(8,128)(2,1)S(1)}, bf16[272,512]{1,0:T(8,128)(2,1)S(1)}, u32[]{:S(2)}, u32[]{:S(2)}) collective-permute-start(bf16[272,512]{1,0:T(8,128)(2,1)S(1)} %pad_maximum_fusion.own), channel_id=1, source_target_pairs={{0,8},{4,12},{8,0},{12,4},{1,9},{5,13},{9,1},{13,5},{2,10},{6,14},... | collective-permute-start | bytes 835592 | tf_op jit(solution)/shard_map/ppermute | solution.py:25
  67.4 4.2 %all-to-all-start.2 = ((bf16[4,256,512]{2,1,0:T(8,128)(2,1)}), bf16[4,256,512]{2,1,0:T(8,128)(2,1)S(1)}, u32[]{:S(2)}, u32[]{:S(2)}) async-start(bf16[4,256,512]{2,1,0:T(8,128)(2,1)} %broadcast_in_dim.23), calls=%async_computation.2 | async-start | bytes 2097152 | tf_op jit(solution)/shard_map/all_to_all | solution.py:17
  76.6 1.3 constant_dynamic-slice_fusion
  78.0 1.3 collective-permute-done.6.second
  79.6 2.0 %copy-done = bf16[4,4,272,512]{3,2,1,0:T(8,128)(2,1)} copy-done((bf16[4,4,272,512]{3,2,1,0:T(8,128)(2,1)}, bf16[4,4,272,512]{3,2,1,0:T(8,128)(2,1)S(1)}, u32[]{:S(2)}) %copy-start) | copy-done | bytes 4456472
  83.7 5.1 %all-to-all-start.3 = ((bf16[4,4,272,512]{3,2,1,0:T(8,128)(2,1)}), bf16[4,4,272,512]{3,2,1,0:T(8,128)(2,1)}, u32[]{:S(2)}, u32[]{:S(2)}) async-start(bf16[4,4,272,512]{3,2,1,0:T(8,128)(2,1)} %copy-done), calls=%async_computation.3 | async-start | bytes 8912896 | tf_op jit(solution)/shard_map/all_to_all | solution.py:17
  88.8 7.6 %collective-permute-start.8 = (bf16[256,512]{1,0:T(8,128)(2,1)S(1)}, bf16[256,512]{1,0:T(8,128)(2,1)S(1)}, u32[]{:S(2)}, u32[]{:S(2)}) collective-permute-start(bf16[256,512]{1,0:T(8,128)(2,1)S(1)} %dynamic-slice_convert_fusion), channel_id=1, source_target_pairs={{0,16},{16,0},{1,17},{17,1},{2,18},{18,2},{3,19},{19,3},{4,20},{20... | collective-permute-start | bytes 786440 | tf_op jit(solution)/shard_map/ppermute | solution.py:35
  97.7 4.0 %collective-permute-start.10 = (bf16[128,512]{1,0:T(8,128)(2,1)S(1)}, bf16[128,512]{1,0:T(8,128)(2,1)S(1)}, u32[]{:S(2)}, u32[]{:S(2)}) collective-permute-start(bf16[128,512]{1,0:T(8,128)(2,1)S(1)} %get-tuple-element.37), channel_id=1, source_target_pairs={{0,384},{128,0},{256,128},{384,256},{1,385},{129,1},{257,129},{385... | collective-permute-start | bytes 393224 | tf_op jit(solution)/shard_map/ppermute | solution.py:25
  101.7 5.2 %collective-permute-start.11 = (bf16[128,512]{1,0:T(8,128)(2,1)S(1)}, bf16[128,512]{1,0:T(8,128)(2,1)S(1)}, u32[]{:S(2)}, u32[]{:S(2)}) collective-permute-start(bf16[128,512]{1,0:T(8,128)(2,1)S(1)} %get-tuple-element.38), channel_id=1, source_target_pairs={{0,128},{128,256},{256,384},{384,0},{1,129},{129,257},{257,385},{3... | collective-permute-start | bytes 393224 | tf_op jit(solution)/shard_map/ppermute | solution.py:25
  106.9 4.0 %collective-permute-start.9 = (bf16[128,512]{1,0:T(8,128)(2,1)S(1)}, bf16[128,512]{1,0:T(8,128)(2,1)S(1)}, u32[]{:S(2)}, u32[]{:S(2)}) collective-permute-start(bf16[128,512]{1,0:T(8,128)(2,1)S(1)} %get-tuple-element.38), channel_id=1, source_target_pairs={{0,384},{128,0},{256,128},{384,256},{1,385},{129,1},{257,129},{385... | collective-permute-start | bytes 393224 | tf_op jit(solution)/shard_map/ppermute | solution.py:25
  110.9 5.2 %collective-permute-start.12 = (bf16[128,512]{1,0:T(8,128)(2,1)S(1)}, bf16[128,512]{1,0:T(8,128)(2,1)S(1)}, u32[]{:S(2)}, u32[]{:S(2)}) collective-permute-start(bf16[128,512]{1,0:T(8,128)(2,1)S(1)} %get-tuple-element.37), channel_id=1, source_target_pairs={{0,128},{128,256},{256,384},{384,0},{1,129},{129,257},{257,385},{3... | collective-permute-start | bytes 393224 | tf_op jit(solution)/shard_map/ppermute | solution.py:25
  116.1 4.0 %collective-permute-start.14 = (bf16[128,512]{1,0:T(8,128)(2,1)S(1)}, bf16[128,512]{1,0:T(8,128)(2,1)S(1)}, u32[]{:S(2)}, u32[]{:S(2)}) collective-permute-start(bf16[128,512]{1,0:T(8,128)(2,1)S(1)} %collective-permute-done.10.after_b), channel_id=1, source_target_pairs={{0,384},{128,0},{256,128},{384,256},{1,385},{129,1},{257,129},{385... | collective-permute-start | bytes 393224 | tf_op jit(solution)/shard_map/ppermute | solution.py:25
  120.1 5.2 %collective-permute-start.13 = (bf16[128,512]{1,0:T(8,128)(2,1)S(1)}, bf16[128,512]{1,0:T(8,128)(2,1)S(1)}, u32[]{:S(2)}, u32[]{:S(2)}) collective-permute-start(bf16[128,512]{1,0:T(8,128)(2,1)S(1)} %collective-permute-done.11.before_a), channel_id=1, source_target_pairs={{0,128},{128,256},{256,384},{384,0},{1,129},{129,257},{257,385},{3... | collective-permute-start | bytes 393224 | tf_op jit(solution)/shard_map/ppermute | solution.py:25
  125.3 1.7 collective-permute-done.9.after_a
  127.0 7.8 %all-to-all-done.3.rows = bf16[4,4,272,512]{3,2,1,0:T(8,128)(2,1)} async-done(((bf16[4,4,272,512]{3,2,1,0:T(8,128)(2,1)}), bf16[4,4,272,512]{3,2,1,0:T(8,128)(2,1)}, u32[]{:S(2)}, u32[]{:S(2)}) %all-to-all-start.3) | async-done | bytes 4456480 | tf_op jit(solution)/shard_map/all_to_all | solution.py:17
  134.8 3.6 %shard_map.57 = (f32[4,256,512]{2,1,0:T(8,128)S(1)}, f32[4,256,512]{2,1,0:T(8,128)S(1)}, bf16[4,256,512]{2,1,0:T(8,128)(2,1)S(1)}, bf16[4,256,512]{2,1,0:T(8,128)(2,1)S(1)}) custom-call(s32[1]{0:T(128)} %bitcast.place, bf16[4,4,272,512]{3,2,1,0:T(8,128)(2,1)} %all-to-all-done.3.rows, bf16[256,512]{1,0:T(8,128)(2,1)S(1)} %multiply_convert_fusion.1.own, ...), custom_call_target="tpu_custom_call" | custom-call | flops 1073741824 | bytes 11534336 | tf_op jit(solution)/shard_map/pallas_call | solution.py:92
  138.5 4.2 %collective-permute-done.13.far_a = bf16[128,512]{1,0:T(8,128)(2,1)S(1)} collective-permute-done((bf16[128,512]{1,0:T(8,128)(2,1)S(1)}, bf16[128,512]{1,0:T(8,128)(2,1)S(1)}, u32[]{:S(2)}, u32[]{:S(2)}) %collective-permute-start.13) | collective-permute-done | bytes 131104 | tf_op jit(solution)/shard_map/ppermute | solution.py:25
  143.5 4.3 %collective-permute-start.15 = (bf16[4,256,512]{2,1,0:T(8,128)(2,1)S(1)}, bf16[4,256,512]{2,1,0:T(8,128)(2,1)S(1)}, u32[]{:S(2)}, u32[]{:S(2)}) collective-permute-start(bf16[4,256,512]{2,1,0:T(8,128)(2,1)S(1)} %shard_map.59), channel_id=1, source_target_pairs={{0,16},{16,0},{1,17},{17,1},{2,18},{18,2},{3,19},{19,3},{4,20},{20... | collective-permute-start | bytes 3145736 | tf_op jit(solution)/shard_map/ppermute | solution.py:35
  148.5 1.5 collective-permute-done.15
  150.0 1.3 add_convert_fusion
  151.3 7.5 %all-to-all-start.4 = ((bf16[4,256,512]{2,1,0:T(8,128)(2,1)}), bf16[4,256,512]{2,1,0:T(8,128)(2,1)S(1)}, u32[]{:S(2)}, u32[]{:S(2)}) async-start(bf16[4,256,512]{2,1,0:T(8,128)(2,1)} %add_convert_fusion), calls=%async_computation.4 | async-start | bytes 2097152 | tf_op jit(solution)/shard_map/all_to_all | solution.py:17
  159.7 13.6 %all-to-all-done.4 = bf16[4,256,512]{2,1,0:T(8,128)(2,1)S(1)} async-done(((bf16[4,256,512]{2,1,0:T(8,128)(2,1)}), bf16[4,256,512]{2,1,0:T(8,128)(2,1)S(1)}, u32[]{:S(2)}, u32[]{:S(2)}) %all-to-all-start.4) | async-done | bytes 1048608 | tf_op jit(solution)/shard_map/all_to_all | solution.py:17
  (58 shorter events, 17.6 us)
Async XLA Ops:
  1.6 32.5 %all-to-all-start = ((bf16[4,80,512]{2,1,0:T(8,128)(2,1)}), bf16[4,80,512]{2,1,0:T(8,128)(2,1)S(1)}, u32[]{:S(2)}, u32[]{:S(2)}) async-start(bf16[4,80,512]{2,1,0:T(8,128)(2,1)} %shard_map.55), calls=%async_computation | async-start | bytes 655360 | tf_op jit(solution)/shard_map/all_to_all | solution.py:17
  18.2 4.7 %collective-permute-start = (bf16[256,256]{1,0:T(8,128)(2,1)S(1)}, bf16[256,256]{1,0:T(8,128)(2,1)S(1)}, u32[]{:S(2)}, u32[]{:S(2)}) collective-permute-start(bf16[256,256]{1,0:T(8,128)(2,1)S(1)} %get-tuple-element.39), channel_id=1, source_target_pairs={{0,0},{1,32},{2,64},{3,96},{16,16},{17,48},{18,80},{19,112},{32,1}... | collective-permute-start | bytes 393224 | tf_op jit(solution)/shard_map/ppermute | solution.py:45
  18.9 4.0 %collective-permute-start.1 = (bf16[256,256]{1,0:T(8,128)(2,1)S(1)}, bf16[256,256]{1,0:T(8,128)(2,1)S(1)}, u32[]{:S(2)}, u32[]{:S(2)}) collective-permute-start(bf16[256,256]{1,0:T(8,128)(2,1)S(1)} %get-tuple-element.40), channel_id=1, source_target_pairs={{0,16},{1,48},{2,80},{3,112},{16,0},{17,32},{18,64},{19,96},{32,17... | collective-permute-start | bytes 393224 | tf_op jit(solution)/shard_map/ppermute | solution.py:45
  35.3 31.0 %all-to-all-start.1 = ((bf16[16,16,512]{2,1,0:T(8,128)(2,1)}), bf16[16,16,512]{2,1,0:T(8,128)(2,1)S(1)}, u32[]{:S(2)}, u32[]{:S(2)}) async-start(bf16[16,16,512]{2,1,0:T(8,128)(2,1)} %bitcast.6), calls=%async_computation.1 | async-start | bytes 524288 | tf_op jit(solution)/shard_map/all_to_all | solution.py:17
  46.2 20.1 %collective-permute-start.3 = (bf16[272,512]{1,0:T(8,128)(2,1)S(1)}, bf16[272,512]{1,0:T(8,128)(2,1)S(1)}, u32[]{:S(2)}, u32[]{:S(2)}) collective-permute-start(bf16[272,512]{1,0:T(8,128)(2,1)S(1)} %pad_maximum_fusion.own), channel_id=1, source_target_pairs={{0,4},{4,8},{8,12},{12,0},{1,5},{5,9},{9,13},{13,1},{2,6},{6,10},{... | collective-permute-start | bytes 835592 | tf_op jit(solution)/shard_map/ppermute | solution.py:25
  49.4 16.9 %collective-permute-start.2 = (bf16[272,512]{1,0:T(8,128)(2,1)S(1)}, bf16[272,512]{1,0:T(8,128)(2,1)S(1)}, u32[]{:S(2)}, u32[]{:S(2)}) collective-permute-start(bf16[272,512]{1,0:T(8,128)(2,1)S(1)} %pad_maximum_fusion.own), channel_id=1, source_target_pairs={{0,12},{4,0},{8,4},{12,8},{1,13},{5,1},{9,5},{13,9},{2,14},{6,2},{... | collective-permute-start | bytes 835592 | tf_op jit(solution)/shard_map/ppermute | solution.py:25
  53.3 10.8 %collective-permute-start.5 = (bf16[256,512]{1,0:T(8,128)(2,1)S(1)}, bf16[256,512]{1,0:T(8,128)(2,1)S(1)}, u32[]{:S(2)}, u32[]{:S(2)}) collective-permute-start(bf16[256,512]{1,0:T(8,128)(2,1)S(1)} %reshape.66), channel_id=1, source_target_pairs={{0,32},{32,64},{64,96},{96,0},{1,33},{33,65},{65,97},{97,1},{2,34}... | collective-permute-start | bytes 786440 | tf_op jit(solution)/shard_map/ppermute | solution.py:25
  56.5 9.7 %collective-permute-start.4 = (bf16[256,512]{1,0:T(8,128)(2,1)S(1)}, bf16[256,512]{1,0:T(8,128)(2,1)S(1)}, u32[]{:S(2)}, u32[]{:S(2)}) collective-permute-start(bf16[256,512]{1,0:T(8,128)(2,1)S(1)} %reshape.66), channel_id=1, source_target_pairs={{0,96},{32,0},{64,32},{96,64},{1,97},{33,1},{65,33},{97,65},{2,98}... | collective-permute-start | bytes 786440 | tf_op jit(solution)/shard_map/ppermute | solution.py:25
  59.8 12.5 %collective-permute-start.7 = (bf16[256,512]{1,0:T(8,128)(2,1)S(1)}, bf16[256,512]{1,0:T(8,128)(2,1)S(1)}, u32[]{:S(2)}, u32[]{:S(2)}) collective-permute-start(bf16[256,512]{1,0:T(8,128)(2,1)S(1)} %reshape.66), channel_id=1, source_target_pairs={{0,64},{32,96},{64,0},{96,32},{1,65},{33,97},{65,1},{97,33},{2,66}... | collective-permute-start | bytes 786440 | tf_op jit(solution)/shard_map/ppermute | solution.py:25
  64.1 15.3 %collective-permute-start.6 = (bf16[272,512]{1,0:T(8,128)(2,1)S(1)}, bf16[272,512]{1,0:T(8,128)(2,1)S(1)}, u32[]{:S(2)}, u32[]{:S(2)}) collective-permute-start(bf16[272,512]{1,0:T(8,128)(2,1)S(1)} %pad_maximum_fusion.own), channel_id=1, source_target_pairs={{0,8},{4,12},{8,0},{12,4},{1,9},{5,13},{9,1},{13,5},{2,10},{6,14},... | collective-permute-start | bytes 835592 | tf_op jit(solution)/shard_map/ppermute | solution.py:25
  67.4 14.6 %all-to-all-start.2 = ((bf16[4,256,512]{2,1,0:T(8,128)(2,1)}), bf16[4,256,512]{2,1,0:T(8,128)(2,1)S(1)}, u32[]{:S(2)}, u32[]{:S(2)}) async-start(bf16[4,256,512]{2,1,0:T(8,128)(2,1)} %broadcast_in_dim.23), calls=%async_computation.2 | async-start | bytes 2097152 | tf_op jit(solution)/shard_map/all_to_all | solution.py:17
  79.6 2.1 %copy-start = (bf16[4,4,272,512]{3,2,1,0:T(8,128)(2,1)}, bf16[4,4,272,512]{3,2,1,0:T(8,128)(2,1)S(1)}, u32[]{:S(2)}) copy-start(bf16[4,4,272,512]{3,2,1,0:T(8,128)(2,1)S(1)} %shard_map.56) | copy-start | bytes 13369348
  82.7 1.0 copy-start.1
  83.7 13.8 %copy-start.2 = (f32[512,512]{1,0:T(8,128)S(1)}, f32[512,512]{1,0:T(8,128)}, u32[]{:S(2)}) copy-start(f32[512,512]{1,0:T(8,128)} %copy-done.1) | copy-start | bytes 3145732
  83.7 13.8 %copy-start.3 = (bf16[256,512]{1,0:T(8,128)(2,1)S(1)}, bf16[256,512]{1,0:T(8,128)(2,1)}, u32[]{:S(2)}) copy-start(bf16[256,512]{1,0:T(8,128)(2,1)} %param.7) | copy-start | bytes 786436
  83.7 51.1 %all-to-all-start.3 = ((bf16[4,4,272,512]{3,2,1,0:T(8,128)(2,1)}), bf16[4,4,272,512]{3,2,1,0:T(8,128)(2,1)}, u32[]{:S(2)}, u32[]{:S(2)}) async-start(bf16[4,4,272,512]{3,2,1,0:T(8,128)(2,1)} %copy-done), calls=%async_computation.3 | async-start | bytes 8912896 | tf_op jit(solution)/shard_map/all_to_all | solution.py:17
  88.8 8.7 %collective-permute-start.8 = (bf16[256,512]{1,0:T(8,128)(2,1)S(1)}, bf16[256,512]{1,0:T(8,128)(2,1)S(1)}, u32[]{:S(2)}, u32[]{:S(2)}) collective-permute-start(bf16[256,512]{1,0:T(8,128)(2,1)S(1)} %dynamic-slice_convert_fusion), channel_id=1, source_target_pairs={{0,16},{16,0},{1,17},{17,1},{2,18},{18,2},{3,19},{19,3},{4,20},{20... | collective-permute-start | bytes 786440 | tf_op jit(solution)/shard_map/ppermute | solution.py:35
  97.7 18.4 %collective-permute-start.10 = (bf16[128,512]{1,0:T(8,128)(2,1)S(1)}, bf16[128,512]{1,0:T(8,128)(2,1)S(1)}, u32[]{:S(2)}, u32[]{:S(2)}) collective-permute-start(bf16[128,512]{1,0:T(8,128)(2,1)S(1)} %get-tuple-element.37), channel_id=1, source_target_pairs={{0,384},{128,0},{256,128},{384,256},{1,385},{129,1},{257,129},{385... | collective-permute-start | bytes 393224 | tf_op jit(solution)/shard_map/ppermute | solution.py:25
  101.7 18.4 %collective-permute-start.11 = (bf16[128,512]{1,0:T(8,128)(2,1)S(1)}, bf16[128,512]{1,0:T(8,128)(2,1)S(1)}, u32[]{:S(2)}, u32[]{:S(2)}) collective-permute-start(bf16[128,512]{1,0:T(8,128)(2,1)S(1)} %get-tuple-element.38), channel_id=1, source_target_pairs={{0,128},{128,256},{256,384},{384,0},{1,129},{129,257},{257,385},{3... | collective-permute-start | bytes 393224 | tf_op jit(solution)/shard_map/ppermute | solution.py:25
  106.9 20.1 %collective-permute-start.9 = (bf16[128,512]{1,0:T(8,128)(2,1)S(1)}, bf16[128,512]{1,0:T(8,128)(2,1)S(1)}, u32[]{:S(2)}, u32[]{:S(2)}) collective-permute-start(bf16[128,512]{1,0:T(8,128)(2,1)S(1)} %get-tuple-element.38), channel_id=1, source_target_pairs={{0,384},{128,0},{256,128},{384,256},{1,385},{129,1},{257,129},{385... | collective-permute-start | bytes 393224 | tf_op jit(solution)/shard_map/ppermute | solution.py:25
  110.9 27.6 %collective-permute-start.12 = (bf16[128,512]{1,0:T(8,128)(2,1)S(1)}, bf16[128,512]{1,0:T(8,128)(2,1)S(1)}, u32[]{:S(2)}, u32[]{:S(2)}) collective-permute-start(bf16[128,512]{1,0:T(8,128)(2,1)S(1)} %get-tuple-element.37), channel_id=1, source_target_pairs={{0,128},{128,256},{256,384},{384,0},{1,129},{129,257},{257,385},{3... | collective-permute-start | bytes 393224 | tf_op jit(solution)/shard_map/ppermute | solution.py:25
  116.1 22.4 %collective-permute-start.14 = (bf16[128,512]{1,0:T(8,128)(2,1)S(1)}, bf16[128,512]{1,0:T(8,128)(2,1)S(1)}, u32[]{:S(2)}, u32[]{:S(2)}) collective-permute-start(bf16[128,512]{1,0:T(8,128)(2,1)S(1)} %collective-permute-done.10.after_b), channel_id=1, source_target_pairs={{0,384},{128,0},{256,128},{384,256},{1,385},{129,1},{257,129},{385... | collective-permute-start | bytes 393224 | tf_op jit(solution)/shard_map/ppermute | solution.py:25
  120.1 22.6 %collective-permute-start.13 = (bf16[128,512]{1,0:T(8,128)(2,1)S(1)}, bf16[128,512]{1,0:T(8,128)(2,1)S(1)}, u32[]{:S(2)}, u32[]{:S(2)}) collective-permute-start(bf16[128,512]{1,0:T(8,128)(2,1)S(1)} %collective-permute-done.11.before_a), channel_id=1, source_target_pairs={{0,128},{128,256},{256,384},{384,0},{1,129},{129,257},{257,385},{3... | collective-permute-start | bytes 393224 | tf_op jit(solution)/shard_map/ppermute | solution.py:25
  143.5 6.5 %collective-permute-start.15 = (bf16[4,256,512]{2,1,0:T(8,128)(2,1)S(1)}, bf16[4,256,512]{2,1,0:T(8,128)(2,1)S(1)}, u32[]{:S(2)}, u32[]{:S(2)}) collective-permute-start(bf16[4,256,512]{2,1,0:T(8,128)(2,1)S(1)} %shard_map.59), channel_id=1, source_target_pairs={{0,16},{16,0},{1,17},{17,1},{2,18},{18,2},{3,19},{19,3},{4,20},{20... | collective-permute-start | bytes 3145736 | tf_op jit(solution)/shard_map/ppermute | solution.py:35
  151.3 22.0 %all-to-all-start.4 = ((bf16[4,256,512]{2,1,0:T(8,128)(2,1)}), bf16[4,256,512]{2,1,0:T(8,128)(2,1)S(1)}, u32[]{:S(2)}, u32[]{:S(2)}) async-start(bf16[4,256,512]{2,1,0:T(8,128)(2,1)} %add_convert_fusion), calls=%async_computation.4 | async-start | bytes 2097152 | tf_op jit(solution)/shard_map/all_to_all | solution.py:17

commit v5 on v4

--- a/solution.py
+++ b/solution.py
@@ -173,11 +173,17 @@
     up = up.reshape(4, 4, 64, 512).transpose(1, 0, 2, 3).reshape(1024, 512)
     up, down = lax.optimization_barrier((up, down))
 
-    part = lax.dot_general(
-        down.reshape(1024, 512), up, (((0,), (0,)), ((), ())), preferred_element_type=f32
-    )
-    mine = lax.dynamic_slice_in_dim(part, core * 256, 256, axis=0)
-    other = lax.dynamic_slice_in_dim(part, (1 - core) * 256, 256, axis=0).astype(bf16)
+    down = down.reshape(1024, 512)
+    other, mine = [
+        lax.dot_general(
+            lax.dynamic_slice_in_dim(down, place * 256, 256, axis=1),
+            up,
+            (((0,), (0,)), ((), ())),
+            preferred_element_type=f32,
+        )
+        for place in (1 - core, core)
+    ]
+    other = other.astype(bf16)
     rows, other = lax.optimization_barrier((rows, other))
     rows = exchange(rows, "y")
     update = mine + swap(other).astype(f32)

time: 176 us -> 175 us (level)
    unnamed x15 -> x11, local copies, waits for them, and re-layouts: 8.03 us -> 7.07 us
where the time goes in v5:
time: 175 us; the launch traced here: 174 us
  starting transfers between devices  106 us (61%)
  waiting for transfers between devices  42.3 us (24%)
  local copies, waits for them, and re-layouts  13.1 us (7%)
  Pallas kernels  6.96 us (4%)
  other arithmetic  4.44 us (3%)
    ppermute x12, starting transfers between devices, ahead(): return lax.ppermute(block, axis, [(i, (i - step) % 4) for i in range(4)])  46.9 us
    all_to_all x5, starting transfers between devices, exchange(): return lax.all_to_all(blocks, axis, split_axis=0, concat_axis=0)  44 us
    all_to_all x5, waiting for transfers between devices, exchange(): return lax.all_to_all(blocks, axis, split_axis=0, concat_axis=0)  32.1 us
    ppermute x2, starting transfers between devices, swap(): return lax.ppermute(block, 'core', [(0, 1), (1, 0)])  11.1 us
    ppermute x12, waiting for transfers between devices, ahead(): return lax.ppermute(block, axis, [(i, (i - step) % 4) for i in range(4)])  8.06 us
    unnamed x11, local copies, waits for them, and re-layouts  7.07 us
    pallas_call x1, Pallas kernels, first_product(): pl.pallas_call(first_kernel, out_shape=(part, part, left, left), in_specs...  3.64 us
    ppermute x2, starting transfers between devices, mirror(): return lax.ppermute(block, ('x', 'core', 'y'), pairs)  3.53 us
  transfers between devices with their start and end apart: 21, of which 9 were waited for; matrix products, arithmetic and copies ran while one was open for 7% of the time, Pallas kernels for 3%

profile of v5, /device:TPU:1, one launch (start us, length us, event | category | flops | bytes accessed | tf_op | source)
XLA Modules:
  0.0 173.8 jit_solution(11128514118423427922)
XLA Ops:
  0.0 1.6 shard_map.55
  1.6 15.6 %all-to-all-start = ((bf16[4,80,512]{2,1,0:T(8,128)(2,1)}), bf16[4,80,512]{2,1,0:T(8,128)(2,1)S(1)}, u32[]{:S(2)}, u32[]{:S(2)}) async-start(bf16[4,80,512]{2,1,0:T(8,128)(2,1)} %shard_map.55), calls=%async_computation | async-start | bytes 655360 | tf_op jit(solution)/shard_map/all_to_all | solution.py:17
  18.9 2.9 %collective-permute-start.1 = (bf16[256,256]{1,0:T(8,128)(2,1)S(1)}, bf16[256,256]{1,0:T(8,128)(2,1)S(1)}, u32[]{:S(2)}, u32[]{:S(2)}) collective-permute-start(bf16[256,256]{1,0:T(8,128)(2,1)S(1)} %get-tuple-element.40), channel_id=1, source_target_pairs={{0,16},{1,48},{2,80},{3,112},{16,0},{17,32},{18,64},{19,96},{32,17... | collective-permute-start | bytes 393224 | tf_op jit(solution)/shard_map/ppermute | solution.py:45
  23.0 11.2 %all-to-all-done = bf16[4,80,512]{2,1,0:T(8,128)(2,1)S(1)} async-done(((bf16[4,80,512]{2,1,0:T(8,128)(2,1)}), bf16[4,80,512]{2,1,0:T(8,128)(2,1)S(1)}, u32[]{:S(2)}, u32[]{:S(2)}) %all-to-all-start) | async-done | bytes 327712 | tf_op jit(solution)/shard_map/all_to_all | solution.py:17
  35.3 10.9 %all-to-all-start.1 = ((bf16[16,16,512]{2,1,0:T(8,128)(2,1)}), bf16[16,16,512]{2,1,0:T(8,128)(2,1)S(1)}, u32[]{:S(2)}, u32[]{:S(2)}) async-start(bf16[16,16,512]{2,1,0:T(8,128)(2,1)} %bitcast.6), calls=%async_computation.1 | async-start | bytes 524288 | tf_op jit(solution)/shard_map/all_to_all | solution.py:17
  46.2 3.3 %collective-permute-start.3 = (bf16[272,512]{1,0:T(8,128)(2,1)S(1)}, bf16[272,512]{1,0:T(8,128)(2,1)S(1)}, u32[]{:S(2)}, u32[]{:S(2)}) collective-permute-start(bf16[272,512]{1,0:T(8,128)(2,1)S(1)} %pad_maximum_fusion.own), channel_id=1, source_target_pairs={{0,4},{4,8},{8,12},{12,0},{1,5},{5,9},{9,13},{13,1},{2,6},{6,10},{... | collective-permute-start | bytes 835592 | tf_op jit(solution)/shard_map/ppermute | solution.py:25
  49.4 3.8 %collective-permute-start.2 = (bf16[272,512]{1,0:T(8,128)(2,1)S(1)}, bf16[272,512]{1,0:T(8,128)(2,1)S(1)}, u32[]{:S(2)}, u32[]{:S(2)}) collective-permute-start(bf16[272,512]{1,0:T(8,128)(2,1)S(1)} %pad_maximum_fusion.own), channel_id=1, source_target_pairs={{0,12},{4,0},{8,4},{12,8},{1,13},{5,1},{9,5},{13,9},{2,14},{6,2},{... | collective-permute-start | bytes 835592 | tf_op jit(solution)/shard_map/ppermute | solution.py:25
  53.3 3.3 %collective-permute-start.5 = (bf16[256,512]{1,0:T(8,128)(2,1)S(1)}, bf16[256,512]{1,0:T(8,128)(2,1)S(1)}, u32[]{:S(2)}, u32[]{:S(2)}) collective-permute-start(bf16[256,512]{1,0:T(8,128)(2,1)S(1)} %reshape.66), channel_id=1, source_target_pairs={{0,32},{32,64},{64,96},{96,0},{1,33},{33,65},{65,97},{97,1},{2,34}... | collective-permute-start | bytes 786440 | tf_op jit(solution)/shard_map/ppermute | solution.py:25
  56.5 3.2 %collective-permute-start.4 = (bf16[256,512]{1,0:T(8,128)(2,1)S(1)}, bf16[256,512]{1,0:T(8,128)(2,1)S(1)}, u32[]{:S(2)}, u32[]{:S(2)}) collective-permute-start(bf16[256,512]{1,0:T(8,128)(2,1)S(1)} %reshape.66), channel_id=1, source_target_pairs={{0,96},{32,0},{64,32},{96,64},{1,97},{33,1},{65,33},{97,65},{2,98}... | collective-permute-start | bytes 786440 | tf_op jit(solution)/shard_map/ppermute | solution.py:25
  59.8 3.6 %collective-permute-start.7 = (bf16[256,512]{1,0:T(8,128)(2,1)S(1)}, bf16[256,512]{1,0:T(8,128)(2,1)S(1)}, u32[]{:S(2)}, u32[]{:S(2)}) collective-permute-start(bf16[256,512]{1,0:T(8,128)(2,1)S(1)} %reshape.66), channel_id=1, source_target_pairs={{0,64},{32,96},{64,0},{96,32},{1,65},{33,97},{65,1},{97,33},{2,66}... | collective-permute-start | bytes 786440 | tf_op jit(solution)/shard_map/ppermute | solution.py:25
  64.1 2.2 %collective-permute-start.6 = (bf16[272,512]{1,0:T(8,128)(2,1)S(1)}, bf16[272,512]{1,0:T(8,128)(2,1)S(1)}, u32[]{:S(2)}, u32[]{:S(2)}) collective-permute-start(bf16[272,512]{1,0:T(8,128)(2,1)S(1)} %pad_maximum_fusion.own), channel_id=1, source_target_pairs={{0,8},{4,12},{8,0},{12,4},{1,9},{5,13},{9,1},{13,5},{2,10},{6,14},... | collective-permute-start | bytes 835592 | tf_op jit(solution)/shard_map/ppermute | solution.py:25
  67.4 4.2 %all-to-all-start.2 = ((bf16[4,256,512]{2,1,0:T(8,128)(2,1)}), bf16[4,256,512]{2,1,0:T(8,128)(2,1)S(1)}, u32[]{:S(2)}, u32[]{:S(2)}) async-start(bf16[4,256,512]{2,1,0:T(8,128)(2,1)} %broadcast_in_dim.23), calls=%async_computation.2 | async-start | bytes 2097152 | tf_op jit(solution)/shard_map/all_to_all | solution.py:17
  76.5 1.3 constant_dynamic-slice_fusion
  77.9 1.4 collective-permute-done.6.second
  79.6 2.1 %copy-done = bf16[4,4,272,512]{3,2,1,0:T(8,128)(2,1)} copy-done((bf16[4,4,272,512]{3,2,1,0:T(8,128)(2,1)}, bf16[4,4,272,512]{3,2,1,0:T(8,128)(2,1)S(1)}, u32[]{:S(2)}) %copy-start) | copy-done | bytes 4456472
  82.4 4.9 %all-to-all-start.3 = ((bf16[4,4,272,512]{3,2,1,0:T(8,128)(2,1)}), bf16[4,4,272,512]{3,2,1,0:T(8,128)(2,1)}, u32[]{:S(2)}, u32[]{:S(2)}) async-start(bf16[4,4,272,512]{3,2,1,0:T(8,128)(2,1)} %copy-done), calls=%async_computation.3 | async-start | bytes 8912896 | tf_op jit(solution)/shard_map/all_to_all | solution.py:17
  88.2 7.6 %collective-permute-start.8 = (bf16[256,512]{1,0:T(8,128)(2,1)S(1)}, bf16[256,512]{1,0:T(8,128)(2,1)S(1)}, u32[]{:S(2)}, u32[]{:S(2)}) collective-permute-start(bf16[256,512]{1,0:T(8,128)(2,1)S(1)} %convolution_convert_fusion), channel_id=1, source_target_pairs={{0,16},{16,0},{1,17},{17,1},{2,18},{18,2},{3,19},{19,3},{4,20},{20... | collective-permute-start | bytes 786440 | tf_op jit(solution)/shard_map/ppermute | solution.py:35
  97.1 4.0 %collective-permute-start.10 = (bf16[128,512]{1,0:T(8,128)(2,1)S(1)}, bf16[128,512]{1,0:T(8,128)(2,1)S(1)}, u32[]{:S(2)}, u32[]{:S(2)}) collective-permute-start(bf16[128,512]{1,0:T(8,128)(2,1)S(1)} %get-tuple-element.37), channel_id=1, source_target_pairs={{0,384},{128,0},{256,128},{384,256},{1,385},{129,1},{257,129},{385... | collective-permute-start | bytes 393224 | tf_op jit(solution)/shard_map/ppermute | solution.py:25
  101.1 5.2 %collective-permute-start.11 = (bf16[128,512]{1,0:T(8,128)(2,1)S(1)}, bf16[128,512]{1,0:T(8,128)(2,1)S(1)}, u32[]{:S(2)}, u32[]{:S(2)}) collective-permute-start(bf16[128,512]{1,0:T(8,128)(2,1)S(1)} %get-tuple-element.38), channel_id=1, source_target_pairs={{0,128},{128,256},{256,384},{384,0},{1,129},{129,257},{257,385},{3... | collective-permute-start | bytes 393224 | tf_op jit(solution)/shard_map/ppermute | solution.py:25
  106.3 4.0 %collective-permute-start.9 = (bf16[128,512]{1,0:T(8,128)(2,1)S(1)}, bf16[128,512]{1,0:T(8,128)(2,1)S(1)}, u32[]{:S(2)}, u32[]{:S(2)}) collective-permute-start(bf16[128,512]{1,0:T(8,128)(2,1)S(1)} %get-tuple-element.38), channel_id=1, source_target_pairs={{0,384},{128,0},{256,128},{384,256},{1,385},{129,1},{257,129},{385... | collective-permute-start | bytes 393224 | tf_op jit(solution)/shard_map/ppermute | solution.py:25
  110.3 5.2 %collective-permute-start.12 = (bf16[128,512]{1,0:T(8,128)(2,1)S(1)}, bf16[128,512]{1,0:T(8,128)(2,1)S(1)}, u32[]{:S(2)}, u32[]{:S(2)}) collective-permute-start(bf16[128,512]{1,0:T(8,128)(2,1)S(1)} %get-tuple-element.37), channel_id=1, source_target_pairs={{0,128},{128,256},{256,384},{384,0},{1,129},{129,257},{257,385},{3... | collective-permute-start | bytes 393224 | tf_op jit(solution)/shard_map/ppermute | solution.py:25
  115.5 4.0 %collective-permute-start.14 = (bf16[128,512]{1,0:T(8,128)(2,1)S(1)}, bf16[128,512]{1,0:T(8,128)(2,1)S(1)}, u32[]{:S(2)}, u32[]{:S(2)}) collective-permute-start(bf16[128,512]{1,0:T(8,128)(2,1)S(1)} %collective-permute-done.10.after_b), channel_id=1, source_target_pairs={{0,384},{128,0},{256,128},{384,256},{1,385},{129,1},{257,129},{385... | collective-permute-start | bytes 393224 | tf_op jit(solution)/shard_map/ppermute | solution.py:25
  119.5 5.2 %collective-permute-start.13 = (bf16[128,512]{1,0:T(8,128)(2,1)S(1)}, bf16[128,512]{1,0:T(8,128)(2,1)S(1)}, u32[]{:S(2)}, u32[]{:S(2)}) collective-permute-start(bf16[128,512]{1,0:T(8,128)(2,1)S(1)} %collective-permute-done.11.before_a), channel_id=1, source_target_pairs={{0,128},{128,256},{256,384},{384,0},{1,129},{129,257},{257,385},{3... | collective-permute-start | bytes 393224 | tf_op jit(solution)/shard_map/ppermute | solution.py:25
  124.7 1.6 collective-permute-done.9.after_a
  126.3 7.0 %all-to-all-done.3.rows = bf16[4,4,272,512]{3,2,1,0:T(8,128)(2,1)} async-done(((bf16[4,4,272,512]{3,2,1,0:T(8,128)(2,1)}), bf16[4,4,272,512]{3,2,1,0:T(8,128)(2,1)}, u32[]{:S(2)}, u32[]{:S(2)}) %all-to-all-start.3) | async-done | bytes 4456480 | tf_op jit(solution)/shard_map/all_to_all | solution.py:17
  133.4 3.6 %shard_map.57 = (f32[4,256,512]{2,1,0:T(8,128)S(1)}, f32[4,256,512]{2,1,0:T(8,128)S(1)}, bf16[4,256,512]{2,1,0:T(8,128)(2,1)S(1)}, bf16[4,256,512]{2,1,0:T(8,128)(2,1)S(1)}) custom-call(s32[1]{0:T(128)} %bitcast.place, bf16[4,4,272,512]{3,2,1,0:T(8,128)(2,1)} %all-to-all-done.3.rows, bf16[256,512]{1,0:T(8,128)(2,1)S(1)} %multiply_convert_fusion.1.own, ...), custom_call_target="tpu_custom_call" | custom-call | flops 1073741824 | bytes 11534336 | tf_op jit(solution)/shard_map/pallas_call | solution.py:92
  137.0 5.0 %collective-permute-done.13.far_a = bf16[128,512]{1,0:T(8,128)(2,1)S(1)} collective-permute-done((bf16[128,512]{1,0:T(8,128)(2,1)S(1)}, bf16[128,512]{1,0:T(8,128)(2,1)S(1)}, u32[]{:S(2)}, u32[]{:S(2)}) %collective-permute-start.13) | collective-permute-done | bytes 131104 | tf_op jit(solution)/shard_map/ppermute | solution.py:25
  142.7 3.5 %collective-permute-start.15 = (bf16[4,256,512]{2,1,0:T(8,128)(2,1)S(1)}, bf16[4,256,512]{2,1,0:T(8,128)(2,1)S(1)}, u32[]{:S(2)}, u32[]{:S(2)}) collective-permute-start(bf16[4,256,512]{2,1,0:T(8,128)(2,1)S(1)} %shard_map.59), channel_id=1, source_target_pairs={{0,16},{16,0},{1,17},{17,1},{2,18},{18,2},{3,19},{19,3},{4,20},{20... | collective-permute-start | bytes 3145736 | tf_op jit(solution)/shard_map/ppermute | solution.py:35
  147.0 1.5 collective-permute-done.15
  148.6 1.4 add_convert_fusion
  149.9 8.4 %all-to-all-start.4 = ((bf16[4,256,512]{2,1,0:T(8,128)(2,1)}), bf16[4,256,512]{2,1,0:T(8,128)(2,1)S(1)}, u32[]{:S(2)}, u32[]{:S(2)}) async-start(bf16[4,256,512]{2,1,0:T(8,128)(2,1)} %add_convert_fusion), calls=%async_computation.4 | async-start | bytes 2097152 | tf_op jit(solution)/shard_map/all_to_all | solution.py:17
  159.2 13.6 %all-to-all-done.4 = bf16[4,256,512]{2,1,0:T(8,128)(2,1)S(1)} async-done(((bf16[4,256,512]{2,1,0:T(8,128)(2,1)}), bf16[4,256,512]{2,1,0:T(8,128)(2,1)S(1)}, u32[]{:S(2)}, u32[]{:S(2)}) %all-to-all-start.4) | async-done | bytes 1048608 | tf_op jit(solution)/shard_map/all_to_all | solution.py:17
  (54 shorter events, 17.0 us)
Async XLA Ops:
  1.6 32.5 %all-to-all-start = ((bf16[4,80,512]{2,1,0:T(8,128)(2,1)}), bf16[4,80,512]{2,1,0:T(8,128)(2,1)S(1)}, u32[]{:S(2)}, u32[]{:S(2)}) async-start(bf16[4,80,512]{2,1,0:T(8,128)(2,1)} %shard_map.55), calls=%async_computation | async-start | bytes 655360 | tf_op jit(solution)/shard_map/all_to_all | solution.py:17
  18.2 4.7 %collective-permute-start = (bf16[256,256]{1,0:T(8,128)(2,1)S(1)}, bf16[256,256]{1,0:T(8,128)(2,1)S(1)}, u32[]{:S(2)}, u32[]{:S(2)}) collective-permute-start(bf16[256,256]{1,0:T(8,128)(2,1)S(1)} %get-tuple-element.39), channel_id=1, source_target_pairs={{0,0},{1,32},{2,64},{3,96},{16,16},{17,48},{18,80},{19,112},{32,1}... | collective-permute-start | bytes 393224 | tf_op jit(solution)/shard_map/ppermute | solution.py:45
  18.9 4.0 %collective-permute-start.1 = (bf16[256,256]{1,0:T(8,128)(2,1)S(1)}, bf16[256,256]{1,0:T(8,128)(2,1)S(1)}, u32[]{:S(2)}, u32[]{:S(2)}) collective-permute-start(bf16[256,256]{1,0:T(8,128)(2,1)S(1)} %get-tuple-element.40), channel_id=1, source_target_pairs={{0,16},{1,48},{2,80},{3,112},{16,0},{17,32},{18,64},{19,96},{32,17... | collective-permute-start | bytes 393224 | tf_op jit(solution)/shard_map/ppermute | solution.py:45
  35.3 31.0 %all-to-all-start.1 = ((bf16[16,16,512]{2,1,0:T(8,128)(2,1)}), bf16[16,16,512]{2,1,0:T(8,128)(2,1)S(1)}, u32[]{:S(2)}, u32[]{:S(2)}) async-start(bf16[16,16,512]{2,1,0:T(8,128)(2,1)} %bitcast.6), calls=%async_computation.1 | async-start | bytes 524288 | tf_op jit(solution)/shard_map/all_to_all | solution.py:17
  46.2 20.1 %collective-permute-start.3 = (bf16[272,512]{1,0:T(8,128)(2,1)S(1)}, bf16[272,512]{1,0:T(8,128)(2,1)S(1)}, u32[]{:S(2)}, u32[]{:S(2)}) collective-permute-start(bf16[272,512]{1,0:T(8,128)(2,1)S(1)} %pad_maximum_fusion.own), channel_id=1, source_target_pairs={{0,4},{4,8},{8,12},{12,0},{1,5},{5,9},{9,13},{13,1},{2,6},{6,10},{... | collective-permute-start | bytes 835592 | tf_op jit(solution)/shard_map/ppermute | solution.py:25
  49.4 16.8 %collective-permute-start.2 = (bf16[272,512]{1,0:T(8,128)(2,1)S(1)}, bf16[272,512]{1,0:T(8,128)(2,1)S(1)}, u32[]{:S(2)}, u32[]{:S(2)}) collective-permute-start(bf16[272,512]{1,0:T(8,128)(2,1)S(1)} %pad_maximum_fusion.own), channel_id=1, source_target_pairs={{0,12},{4,0},{8,4},{12,8},{1,13},{5,1},{9,5},{13,9},{2,14},{6,2},{... | collective-permute-start | bytes 835592 | tf_op jit(solution)/shard_map/ppermute | solution.py:25
  53.3 10.8 %collective-permute-start.5 = (bf16[256,512]{1,0:T(8,128)(2,1)S(1)}, bf16[256,512]{1,0:T(8,128)(2,1)S(1)}, u32[]{:S(2)}, u32[]{:S(2)}) collective-permute-start(bf16[256,512]{1,0:T(8,128)(2,1)S(1)} %reshape.66), channel_id=1, source_target_pairs={{0,32},{32,64},{64,96},{96,0},{1,33},{33,65},{65,97},{97,1},{2,34}... | collective-permute-start | bytes 786440 | tf_op jit(solution)/shard_map/ppermute | solution.py:25
  56.5 9.7 %collective-permute-start.4 = (bf16[256,512]{1,0:T(8,128)(2,1)S(1)}, bf16[256,512]{1,0:T(8,128)(2,1)S(1)}, u32[]{:S(2)}, u32[]{:S(2)}) collective-permute-start(bf16[256,512]{1,0:T(8,128)(2,1)S(1)} %reshape.66), channel_id=1, source_target_pairs={{0,96},{32,0},{64,32},{96,64},{1,97},{33,1},{65,33},{97,65},{2,98}... | collective-permute-start | bytes 786440 | tf_op jit(solution)/shard_map/ppermute | solution.py:25
  59.8 12.5 %collective-permute-start.7 = (bf16[256,512]{1,0:T(8,128)(2,1)S(1)}, bf16[256,512]{1,0:T(8,128)(2,1)S(1)}, u32[]{:S(2)}, u32[]{:S(2)}) collective-permute-start(bf16[256,512]{1,0:T(8,128)(2,1)S(1)} %reshape.66), channel_id=1, source_target_pairs={{0,64},{32,96},{64,0},{96,32},{1,65},{33,97},{65,1},{97,33},{2,66}... | collective-permute-start | bytes 786440 | tf_op jit(solution)/shard_map/ppermute | solution.py:25
  64.1 15.3 %collective-permute-start.6 = (bf16[272,512]{1,0:T(8,128)(2,1)S(1)}, bf16[272,512]{1,0:T(8,128)(2,1)S(1)}, u32[]{:S(2)}, u32[]{:S(2)}) collective-permute-start(bf16[272,512]{1,0:T(8,128)(2,1)S(1)} %pad_maximum_fusion.own), channel_id=1, source_target_pairs={{0,8},{4,12},{8,0},{12,4},{1,9},{5,13},{9,1},{13,5},{2,10},{6,14},... | collective-permute-start | bytes 835592 | tf_op jit(solution)/shard_map/ppermute | solution.py:25
  67.4 14.6 %all-to-all-start.2 = ((bf16[4,256,512]{2,1,0:T(8,128)(2,1)}), bf16[4,256,512]{2,1,0:T(8,128)(2,1)S(1)}, u32[]{:S(2)}, u32[]{:S(2)}) async-start(bf16[4,256,512]{2,1,0:T(8,128)(2,1)} %broadcast_in_dim.23), calls=%async_computation.2 | async-start | bytes 2097152 | tf_op jit(solution)/shard_map/all_to_all | solution.py:17
  79.6 2.1 %copy-start = (bf16[4,4,272,512]{3,2,1,0:T(8,128)(2,1)}, bf16[4,4,272,512]{3,2,1,0:T(8,128)(2,1)S(1)}, u32[]{:S(2)}) copy-start(bf16[4,4,272,512]{3,2,1,0:T(8,128)(2,1)S(1)} %shard_map.56) | copy-start | bytes 13369348
  82.4 51.0 %all-to-all-start.3 = ((bf16[4,4,272,512]{3,2,1,0:T(8,128)(2,1)}), bf16[4,4,272,512]{3,2,1,0:T(8,128)(2,1)}, u32[]{:S(2)}, u32[]{:S(2)}) async-start(bf16[4,4,272,512]{3,2,1,0:T(8,128)(2,1)} %copy-done), calls=%async_computation.3 | async-start | bytes 8912896 | tf_op jit(solution)/shard_map/all_to_all | solution.py:17
  87.3 9.6 %copy-start.1 = (bf16[256,512]{1,0:T(8,128)(2,1)S(1)}, bf16[256,512]{1,0:T(8,128)(2,1)}, u32[]{:S(2)}) copy-start(bf16[256,512]{1,0:T(8,128)(2,1)} %param.7) | copy-start | bytes 786436
  88.2 8.7 %collective-permute-start.8 = (bf16[256,512]{1,0:T(8,128)(2,1)S(1)}, bf16[256,512]{1,0:T(8,128)(2,1)S(1)}, u32[]{:S(2)}, u32[]{:S(2)}) collective-permute-start(bf16[256,512]{1,0:T(8,128)(2,1)S(1)} %convolution_convert_fusion), channel_id=1, source_target_pairs={{0,16},{16,0},{1,17},{17,1},{2,18},{18,2},{3,19},{19,3},{4,20},{20... | collective-permute-start | bytes 786440 | tf_op jit(solution)/shard_map/ppermute | solution.py:35
  97.1 18.4 %collective-permute-start.10 = (bf16[128,512]{1,0:T(8,128)(2,1)S(1)}, bf16[128,512]{1,0:T(8,128)(2,1)S(1)}, u32[]{:S(2)}, u32[]{:S(2)}) collective-permute-start(bf16[128,512]{1,0:T(8,128)(2,1)S(1)} %get-tuple-element.37), channel_id=1, source_target_pairs={{0,384},{128,0},{256,128},{384,256},{1,385},{129,1},{257,129},{385... | collective-permute-start | bytes 393224 | tf_op jit(solution)/shard_map/ppermute | solution.py:25
  101.1 18.4 %collective-permute-start.11 = (bf16[128,512]{1,0:T(8,128)(2,1)S(1)}, bf16[128,512]{1,0:T(8,128)(2,1)S(1)}, u32[]{:S(2)}, u32[]{:S(2)}) collective-permute-start(bf16[128,512]{1,0:T(8,128)(2,1)S(1)} %get-tuple-element.38), channel_id=1, source_target_pairs={{0,128},{128,256},{256,384},{384,0},{1,129},{129,257},{257,385},{3... | collective-permute-start | bytes 393224 | tf_op jit(solution)/shard_map/ppermute | solution.py:25
  106.3 20.1 %collective-permute-start.9 = (bf16[128,512]{1,0:T(8,128)(2,1)S(1)}, bf16[128,512]{1,0:T(8,128)(2,1)S(1)}, u32[]{:S(2)}, u32[]{:S(2)}) collective-permute-start(bf16[128,512]{1,0:T(8,128)(2,1)S(1)} %get-tuple-element.38), channel_id=1, source_target_pairs={{0,384},{128,0},{256,128},{384,256},{1,385},{129,1},{257,129},{385... | collective-permute-start | bytes 393224 | tf_op jit(solution)/shard_map/ppermute | solution.py:25
  110.3 26.7 %collective-permute-start.12 = (bf16[128,512]{1,0:T(8,128)(2,1)S(1)}, bf16[128,512]{1,0:T(8,128)(2,1)S(1)}, u32[]{:S(2)}, u32[]{:S(2)}) collective-permute-start(bf16[128,512]{1,0:T(8,128)(2,1)S(1)} %get-tuple-element.37), channel_id=1, source_target_pairs={{0,128},{128,256},{256,384},{384,0},{1,129},{129,257},{257,385},{3... | collective-permute-start | bytes 393224 | tf_op jit(solution)/shard_map/ppermute | solution.py:25
  115.5 21.6 %collective-permute-start.14 = (bf16[128,512]{1,0:T(8,128)(2,1)S(1)}, bf16[128,512]{1,0:T(8,128)(2,1)S(1)}, u32[]{:S(2)}, u32[]{:S(2)}) collective-permute-start(bf16[128,512]{1,0:T(8,128)(2,1)S(1)} %collective-permute-done.10.after_b), channel_id=1, source_target_pairs={{0,384},{128,0},{256,128},{384,256},{1,385},{129,1},{257,129},{385... | collective-permute-start | bytes 393224 | tf_op jit(solution)/shard_map/ppermute | solution.py:25
  119.5 22.5 %collective-permute-start.13 = (bf16[128,512]{1,0:T(8,128)(2,1)S(1)}, bf16[128,512]{1,0:T(8,128)(2,1)S(1)}, u32[]{:S(2)}, u32[]{:S(2)}) collective-permute-start(bf16[128,512]{1,0:T(8,128)(2,1)S(1)} %collective-permute-done.11.before_a), channel_id=1, source_target_pairs={{0,128},{128,256},{256,384},{384,0},{1,129},{129,257},{257,385},{3... | collective-permute-start | bytes 393224 | tf_op jit(solution)/shard_map/ppermute | solution.py:25
  142.7 5.8 %collective-permute-start.15 = (bf16[4,256,512]{2,1,0:T(8,128)(2,1)S(1)}, bf16[4,256,512]{2,1,0:T(8,128)(2,1)S(1)}, u32[]{:S(2)}, u32[]{:S(2)}) collective-permute-start(bf16[4,256,512]{2,1,0:T(8,128)(2,1)S(1)} %shard_map.59), channel_id=1, source_target_pairs={{0,16},{16,0},{1,17},{17,1},{2,18},{18,2},{3,19},{19,3},{4,20},{20... | collective-permute-start | bytes 3145736 | tf_op jit(solution)/shard_map/ppermute | solution.py:35
  149.9 22.9 %all-to-all-start.4 = ((bf16[4,256,512]{2,1,0:T(8,128)(2,1)}), bf16[4,256,512]{2,1,0:T(8,128)(2,1)S(1)}, u32[]{:S(2)}, u32[]{:S(2)}) async-start(bf16[4,256,512]{2,1,0:T(8,128)(2,1)} %add_convert_fusion), calls=%async_computation.4 | async-start | bytes 2097152 | tf_op jit(solution)/shard_map/all_to_all | solution.py:17

commit v6 on v5

--- a/solution.py
+++ b/solution.py
@@ -26,9 +26,11 @@
 
 
 def turned(blocks, axis):
-    return lax.dynamic_slice_in_dim(
-        jnp.stack(blocks + blocks), lax.rem(4 - lax.axis_index(axis), 4), 4, axis=0
-    )
+    out = jnp.zeros((4,) + blocks[0].shape, blocks[0].dtype)
+    for r, block in enumerate(blocks):
+        place = lax.rem(lax.axis_index(axis) + r, 4)
+        out = lax.dynamic_update_index_in_dim(out, block, place, 0)
+    return out
 
 
 def swap(block):

time: 175 us -> 175 us (level)
  waiting for transfers between devices: 42.3 us -> 49.5 us
  local copies, waits for them, and re-layouts: 13.1 us -> 6.3 us
    ppermute x12, waiting for transfers between devices: 8.06 us -> 16.8 us  [ahead(): return lax.ppermute(block, axis, [(i, (i - step) % 4) for i in range(4)])]
    unnamed x11 -> x4, local copies, waits for them, and re-layouts: 7.07 us -> 2.09 us
    all_to_all x5, starting transfers between devices: 44 us -> 42.1 us  [exchange(): return lax.all_to_all(blocks, axis, split_axis=0, concat_axis=0)]
  transfers between devices with their start and end apart: 21 -> 21, of which waited for: 9 -> 11; matrix products, arithmetic and copies ran while one was open for 7% -> 3% of each run, Pallas kernels for 3% -> 3%
where the time goes in v6:
time: 175 us; the launch traced here: 174 us
  starting transfers between devices  105 us (60%)
  waiting for transfers between devices  49.5 us (28%)
  Pallas kernels  6.96 us (4%)
  local copies, waits for them, and re-layouts  6.3 us (4%)
  other arithmetic  4.44 us (3%)
    ppermute x12, starting transfers between devices, ahead(): return lax.ppermute(block, axis, [(i, (i - step) % 4) for i in range(4)])  48.2 us
    all_to_all x5, starting transfers between devices, exchange(): return lax.all_to_all(blocks, axis, split_axis=0, concat_axis=0)  42.1 us
    all_to_all x5, waiting for transfers between devices, exchange(): return lax.all_to_all(blocks, axis, split_axis=0, concat_axis=0)  30.4 us
    ppermute x12, waiting for transfers between devices, ahead(): return lax.ppermute(block, axis, [(i, (i - step) % 4) for i in range(4)])  16.8 us
    ppermute x2, starting transfers between devices, swap(): return lax.ppermute(block, 'core', [(0, 1), (1, 0)])  11.4 us
    pallas_call x1, Pallas kernels, first_product(): pl.pallas_call(first_kernel, out_shape=(part, part, left, left), in_specs...  3.64 us
    ppermute x2, starting transfers between devices, mirror(): return lax.ppermute(block, ('x', 'core', 'y'), pairs)  3.53 us
  transfers between devices with their start and end apart: 21, of which 11 were waited for; matrix products, arithmetic and copies ran while one was open for 3% of the time, Pallas kernels for 3%

profile of v6, /device:TPU:1, one launch (start us, length us, event | category | flops | bytes accessed | tf_op | source)
XLA Modules:
  0.0 173.8 jit_solution(8452667160068901239)
XLA Ops:
  0.0 1.6 shard_map.55
  1.6 15.6 %all-to-all-start = ((bf16[4,80,512]{2,1,0:T(8,128)(2,1)}), bf16[4,80,512]{2,1,0:T(8,128)(2,1)S(1)}, u32[]{:S(2)}, u32[]{:S(2)}) async-start(bf16[4,80,512]{2,1,0:T(8,128)(2,1)} %shard_map.55), calls=%async_computation | async-start | bytes 655360 | tf_op jit(solution)/shard_map/all_to_all | solution.py:17
  18.9 2.9 %collective-permute-start.1 = (bf16[256,256]{1,0:T(8,128)(2,1)S(1)}, bf16[256,256]{1,0:T(8,128)(2,1)S(1)}, u32[]{:S(2)}, u32[]{:S(2)}) collective-permute-start(bf16[256,256]{1,0:T(8,128)(2,1)S(1)} %get-tuple-element.40), channel_id=1, source_target_pairs={{0,16},{1,48},{2,80},{3,112},{16,0},{17,32},{18,64},{19,96},{32,17... | collective-permute-start | bytes 393224 | tf_op jit(solution)/shard_map/ppermute | solution.py:47
  23.0 11.2 %all-to-all-done = bf16[4,80,512]{2,1,0:T(8,128)(2,1)S(1)} async-done(((bf16[4,80,512]{2,1,0:T(8,128)(2,1)}), bf16[4,80,512]{2,1,0:T(8,128)(2,1)S(1)}, u32[]{:S(2)}, u32[]{:S(2)}) %all-to-all-start) | async-done | bytes 327712 | tf_op jit(solution)/shard_map/all_to_all | solution.py:17
  35.3 10.9 %all-to-all-start.1 = ((bf16[16,16,512]{2,1,0:T(8,128)(2,1)}), bf16[16,16,512]{2,1,0:T(8,128)(2,1)S(1)}, u32[]{:S(2)}, u32[]{:S(2)}) async-start(bf16[16,16,512]{2,1,0:T(8,128)(2,1)} %bitcast.6), calls=%async_computation.1 | async-start | bytes 524288 | tf_op jit(solution)/shard_map/all_to_all | solution.py:17
  46.2 3.3 %collective-permute-start.3 = (bf16[272,512]{1,0:T(8,128)(2,1)S(1)}, bf16[272,512]{1,0:T(8,128)(2,1)S(1)}, u32[]{:S(2)}, u32[]{:S(2)}) collective-permute-start(bf16[272,512]{1,0:T(8,128)(2,1)S(1)} %pad_maximum_fusion.own), channel_id=1, source_target_pairs={{0,4},{4,8},{8,12},{12,0},{1,5},{5,9},{9,13},{13,1},{2,6},{6,10},{... | collective-permute-start | bytes 835592 | tf_op jit(solution)/shard_map/ppermute | solution.py:25
  49.4 3.8 %collective-permute-start.2 = (bf16[272,512]{1,0:T(8,128)(2,1)S(1)}, bf16[272,512]{1,0:T(8,128)(2,1)S(1)}, u32[]{:S(2)}, u32[]{:S(2)}) collective-permute-start(bf16[272,512]{1,0:T(8,128)(2,1)S(1)} %pad_maximum_fusion.own), channel_id=1, source_target_pairs={{0,12},{4,0},{8,4},{12,8},{1,13},{5,1},{9,5},{13,9},{2,14},{6,2},{... | collective-permute-start | bytes 835592 | tf_op jit(solution)/shard_map/ppermute | solution.py:25
  53.3 3.3 %collective-permute-start.5 = (bf16[256,512]{1,0:T(8,128)(2,1)S(1)}, bf16[256,512]{1,0:T(8,128)(2,1)S(1)}, u32[]{:S(2)}, u32[]{:S(2)}) collective-permute-start(bf16[256,512]{1,0:T(8,128)(2,1)S(1)} %reshape.66), channel_id=1, source_target_pairs={{0,32},{32,64},{64,96},{96,0},{1,33},{33,65},{65,97},{97,1},{2,34}... | collective-permute-start | bytes 786440 | tf_op jit(solution)/shard_map/ppermute | solution.py:25
  56.5 3.2 %collective-permute-start.4 = (bf16[256,512]{1,0:T(8,128)(2,1)S(1)}, bf16[256,512]{1,0:T(8,128)(2,1)S(1)}, u32[]{:S(2)}, u32[]{:S(2)}) collective-permute-start(bf16[256,512]{1,0:T(8,128)(2,1)S(1)} %reshape.66), channel_id=1, source_target_pairs={{0,96},{32,0},{64,32},{96,64},{1,97},{33,1},{65,33},{97,65},{2,98}... | collective-permute-start | bytes 786440 | tf_op jit(solution)/shard_map/ppermute | solution.py:25
  59.8 3.6 %collective-permute-start.7 = (bf16[256,512]{1,0:T(8,128)(2,1)S(1)}, bf16[256,512]{1,0:T(8,128)(2,1)S(1)}, u32[]{:S(2)}, u32[]{:S(2)}) collective-permute-start(bf16[256,512]{1,0:T(8,128)(2,1)S(1)} %reshape.66), channel_id=1, source_target_pairs={{0,64},{32,96},{64,0},{96,32},{1,65},{33,97},{65,1},{97,33},{2,66}... | collective-permute-start | bytes 786440 | tf_op jit(solution)/shard_map/ppermute | solution.py:25
  63.4 2.2 %collective-permute-start.6 = (bf16[272,512]{1,0:T(8,128)(2,1)S(1)}, bf16[272,512]{1,0:T(8,128)(2,1)S(1)}, u32[]{:S(2)}, u32[]{:S(2)}) collective-permute-start(bf16[272,512]{1,0:T(8,128)(2,1)S(1)} %pad_maximum_fusion.own), channel_id=1, source_target_pairs={{0,8},{4,12},{8,0},{12,4},{1,9},{5,13},{9,1},{13,5},{2,10},{6,14},... | collective-permute-start | bytes 835592 | tf_op jit(solution)/shard_map/ppermute | solution.py:25
  67.0 4.2 %all-to-all-start.2 = ((bf16[4,256,512]{2,1,0:T(8,128)(2,1)}), bf16[4,256,512]{2,1,0:T(8,128)(2,1)S(1)}, u32[]{:S(2)}, u32[]{:S(2)}) async-start(bf16[4,256,512]{2,1,0:T(8,128)(2,1)} %broadcast_in_dim.39), calls=%async_computation.2 | async-start | bytes 2097152 | tf_op jit(solution)/shard_map/all_to_all | solution.py:17
  71.5 7.2 %collective-permute-done.6.second = bf16[272,512]{1,0:T(8,128)(2,1)S(1)} collective-permute-done((bf16[272,512]{1,0:T(8,128)(2,1)S(1)}, bf16[272,512]{1,0:T(8,128)(2,1)S(1)}, u32[]{:S(2)}, u32[]{:S(2)}) %collective-permute-start.6) | collective-permute-done | bytes 278560 | tf_op jit(solution)/shard_map/ppermute | solution.py:25
  79.0 2.1 %copy-done = bf16[4,4,272,512]{3,2,1,0:T(8,128)(2,1)} copy-done((bf16[4,4,272,512]{3,2,1,0:T(8,128)(2,1)}, bf16[4,4,272,512]{3,2,1,0:T(8,128)(2,1)S(1)}, u32[]{:S(2)}) %copy-start) | copy-done | bytes 4456472
  81.7 4.9 %all-to-all-start.3 = ((bf16[4,4,272,512]{3,2,1,0:T(8,128)(2,1)}), bf16[4,4,272,512]{3,2,1,0:T(8,128)(2,1)}, u32[]{:S(2)}, u32[]{:S(2)}) async-start(bf16[4,4,272,512]{3,2,1,0:T(8,128)(2,1)} %copy-done), calls=%async_computation.3 | async-start | bytes 8912896 | tf_op jit(solution)/shard_map/all_to_all | solution.py:17
  87.4 7.9 %collective-permute-start.8 = (bf16[256,512]{1,0:T(8,128)(2,1)S(1)}, bf16[256,512]{1,0:T(8,128)(2,1)S(1)}, u32[]{:S(2)}, u32[]{:S(2)}) collective-permute-start(bf16[256,512]{1,0:T(8,128)(2,1)S(1)} %convolution_convert_fusion), channel_id=1, source_target_pairs={{0,16},{16,0},{1,17},{17,1},{2,18},{18,2},{3,19},{19,3},{4,20},{20... | collective-permute-start | bytes 786440 | tf_op jit(solution)/shard_map/ppermute | solution.py:37
  96.7 4.1 %collective-permute-start.10 = (bf16[128,512]{1,0:T(8,128)(2,1)S(1)}, bf16[128,512]{1,0:T(8,128)(2,1)S(1)}, u32[]{:S(2)}, u32[]{:S(2)}) collective-permute-start(bf16[128,512]{1,0:T(8,128)(2,1)S(1)} %get-tuple-element.37), channel_id=1, source_target_pairs={{0,384},{128,0},{256,128},{384,256},{1,385},{129,1},{257,129},{385... | collective-permute-start | bytes 393224 | tf_op jit(solution)/shard_map/ppermute | solution.py:25
  100.8 5.1 %collective-permute-start.11 = (bf16[128,512]{1,0:T(8,128)(2,1)S(1)}, bf16[128,512]{1,0:T(8,128)(2,1)S(1)}, u32[]{:S(2)}, u32[]{:S(2)}) collective-permute-start(bf16[128,512]{1,0:T(8,128)(2,1)S(1)} %get-tuple-element.38), channel_id=1, source_target_pairs={{0,128},{128,256},{256,384},{384,0},{1,129},{129,257},{257,385},{3... | collective-permute-start | bytes 393224 | tf_op jit(solution)/shard_map/ppermute | solution.py:25
  105.9 4.1 %collective-permute-start.9 = (bf16[128,512]{1,0:T(8,128)(2,1)S(1)}, bf16[128,512]{1,0:T(8,128)(2,1)S(1)}, u32[]{:S(2)}, u32[]{:S(2)}) collective-permute-start(bf16[128,512]{1,0:T(8,128)(2,1)S(1)} %get-tuple-element.38), channel_id=1, source_target_pairs={{0,384},{128,0},{256,128},{384,256},{1,385},{129,1},{257,129},{385... | collective-permute-start | bytes 393224 | tf_op jit(solution)/shard_map/ppermute | solution.py:25
  110.0 5.1 %collective-permute-start.12 = (bf16[128,512]{1,0:T(8,128)(2,1)S(1)}, bf16[128,512]{1,0:T(8,128)(2,1)S(1)}, u32[]{:S(2)}, u32[]{:S(2)}) collective-permute-start(bf16[128,512]{1,0:T(8,128)(2,1)S(1)} %get-tuple-element.37), channel_id=1, source_target_pairs={{0,128},{128,256},{256,384},{384,0},{1,129},{129,257},{257,385},{3... | collective-permute-start | bytes 393224 | tf_op jit(solution)/shard_map/ppermute | solution.py:25
  115.1 1.2 collective-permute-done.10.after_b
  116.3 3.6 %collective-permute-start.14 = (bf16[128,512]{1,0:T(8,128)(2,1)S(1)}, bf16[128,512]{1,0:T(8,128)(2,1)S(1)}, u32[]{:S(2)}, u32[]{:S(2)}) collective-permute-start(bf16[128,512]{1,0:T(8,128)(2,1)S(1)} %collective-permute-done.10.after_b), channel_id=1, source_target_pairs={{0,384},{128,0},{256,128},{384,256},{1,385},{129,1},{257,129},{385... | collective-permute-start | bytes 393224 | tf_op jit(solution)/shard_map/ppermute | solution.py:25
  119.9 6.9 %collective-permute-start.13 = (bf16[128,512]{1,0:T(8,128)(2,1)S(1)}, bf16[128,512]{1,0:T(8,128)(2,1)S(1)}, u32[]{:S(2)}, u32[]{:S(2)}) collective-permute-start(bf16[128,512]{1,0:T(8,128)(2,1)S(1)} %collective-permute-done.11.before_a), channel_id=1, source_target_pairs={{0,128},{128,256},{256,384},{384,0},{1,129},{129,257},{257,385},{3... | collective-permute-start | bytes 393224 | tf_op jit(solution)/shard_map/ppermute | solution.py:25
  126.8 5.5 %all-to-all-done.3.rows = bf16[4,4,272,512]{3,2,1,0:T(8,128)(2,1)} async-done(((bf16[4,4,272,512]{3,2,1,0:T(8,128)(2,1)}), bf16[4,4,272,512]{3,2,1,0:T(8,128)(2,1)}, u32[]{:S(2)}, u32[]{:S(2)}) %all-to-all-start.3) | async-done | bytes 4456480 | tf_op jit(solution)/shard_map/all_to_all | solution.py:17
  132.3 3.6 %shard_map.57 = (f32[4,256,512]{2,1,0:T(8,128)S(1)}, f32[4,256,512]{2,1,0:T(8,128)S(1)}, bf16[4,256,512]{2,1,0:T(8,128)(2,1)S(1)}, bf16[4,256,512]{2,1,0:T(8,128)(2,1)S(1)}) custom-call(s32[1]{0:T(128)} %bitcast.place, bf16[4,4,272,512]{3,2,1,0:T(8,128)(2,1)} %all-to-all-done.3.rows, bf16[256,512]{1,0:T(8,128)(2,1)S(1)} %multiply_convert_fusion.1.own, ...), custom_call_target="tpu_custom_call" | custom-call | flops 1073741824 | bytes 11534336 | tf_op jit(solution)/shard_map/pallas_call | solution.py:94
  135.9 2.2 %collective-permute-done.12.before_b = bf16[128,512]{1,0:T(8,128)(2,1)S(1)} collective-permute-done((bf16[128,512]{1,0:T(8,128)(2,1)S(1)}, bf16[128,512]{1,0:T(8,128)(2,1)S(1)}, u32[]{:S(2)}, u32[]{:S(2)}) %collective-permute-start.12) | collective-permute-done | bytes 131104 | tf_op jit(solution)/shard_map/ppermute | solution.py:25
  138.1 5.9 %collective-permute-done.13.far_a = bf16[128,512]{1,0:T(8,128)(2,1)S(1)} collective-permute-done((bf16[128,512]{1,0:T(8,128)(2,1)S(1)}, bf16[128,512]{1,0:T(8,128)(2,1)S(1)}, u32[]{:S(2)}, u32[]{:S(2)}) %collective-permute-start.13) | collective-permute-done | bytes 131104 | tf_op jit(solution)/shard_map/ppermute | solution.py:25
  144.7 3.5 %collective-permute-start.15 = (bf16[4,256,512]{2,1,0:T(8,128)(2,1)S(1)}, bf16[4,256,512]{2,1,0:T(8,128)(2,1)S(1)}, u32[]{:S(2)}, u32[]{:S(2)}) collective-permute-start(bf16[4,256,512]{2,1,0:T(8,128)(2,1)S(1)} %shard_map.59), channel_id=1, source_target_pairs={{0,16},{16,0},{1,17},{17,1},{2,18},{18,2},{3,19},{19,3},{4,20},{20... | collective-permute-start | bytes 3145736 | tf_op jit(solution)/shard_map/ppermute | solution.py:37
  149.0 1.5 collective-permute-done.15
  150.5 1.4 add_convert_fusion
  151.9 6.5 %all-to-all-start.4 = ((bf16[4,256,512]{2,1,0:T(8,128)(2,1)}), bf16[4,256,512]{2,1,0:T(8,128)(2,1)S(1)}, u32[]{:S(2)}, u32[]{:S(2)}) async-start(bf16[4,256,512]{2,1,0:T(8,128)(2,1)} %add_convert_fusion), calls=%async_computation.4 | async-start | bytes 2097152 | tf_op jit(solution)/shard_map/all_to_all | solution.py:17
  159.2 13.6 %all-to-all-done.4 = bf16[4,256,512]{2,1,0:T(8,128)(2,1)S(1)} async-done(((bf16[4,256,512]{2,1,0:T(8,128)(2,1)}), bf16[4,256,512]{2,1,0:T(8,128)(2,1)S(1)}, u32[]{:S(2)}, u32[]{:S(2)}) %all-to-all-start.4) | async-done | bytes 1048608 | tf_op jit(solution)/shard_map/all_to_all | solution.py:17
  (50 shorter events, 11.8 us)
Async XLA Ops:
  1.6 32.5 %all-to-all-start = ((bf16[4,80,512]{2,1,0:T(8,128)(2,1)}), bf16[4,80,512]{2,1,0:T(8,128)(2,1)S(1)}, u32[]{:S(2)}, u32[]{:S(2)}) async-start(bf16[4,80,512]{2,1,0:T(8,128)(2,1)} %shard_map.55), calls=%async_computation | async-start | bytes 655360 | tf_op jit(solution)/shard_map/all_to_all | solution.py:17
  18.2 4.7 %collective-permute-start = (bf16[256,256]{1,0:T(8,128)(2,1)S(1)}, bf16[256,256]{1,0:T(8,128)(2,1)S(1)}, u32[]{:S(2)}, u32[]{:S(2)}) collective-permute-start(bf16[256,256]{1,0:T(8,128)(2,1)S(1)} %get-tuple-element.39), channel_id=1, source_target_pairs={{0,0},{1,32},{2,64},{3,96},{16,16},{17,48},{18,80},{19,112},{32,1}... | collective-permute-start | bytes 393224 | tf_op jit(solution)/shard_map/ppermute | solution.py:47
  18.9 4.0 %collective-permute-start.1 = (bf16[256,256]{1,0:T(8,128)(2,1)S(1)}, bf16[256,256]{1,0:T(8,128)(2,1)S(1)}, u32[]{:S(2)}, u32[]{:S(2)}) collective-permute-start(bf16[256,256]{1,0:T(8,128)(2,1)S(1)} %get-tuple-element.40), channel_id=1, source_target_pairs={{0,16},{1,48},{2,80},{3,112},{16,0},{17,32},{18,64},{19,96},{32,17... | collective-permute-start | bytes 393224 | tf_op jit(solution)/shard_map/ppermute | solution.py:47
  35.3 30.7 %all-to-all-start.1 = ((bf16[16,16,512]{2,1,0:T(8,128)(2,1)}), bf16[16,16,512]{2,1,0:T(8,128)(2,1)S(1)}, u32[]{:S(2)}, u32[]{:S(2)}) async-start(bf16[16,16,512]{2,1,0:T(8,128)(2,1)} %bitcast.6), calls=%async_computation.1 | async-start | bytes 524288 | tf_op jit(solution)/shard_map/all_to_all | solution.py:17
  46.2 19.4 %collective-permute-start.3 = (bf16[272,512]{1,0:T(8,128)(2,1)S(1)}, bf16[272,512]{1,0:T(8,128)(2,1)S(1)}, u32[]{:S(2)}, u32[]{:S(2)}) collective-permute-start(bf16[272,512]{1,0:T(8,128)(2,1)S(1)} %pad_maximum_fusion.own), channel_id=1, source_target_pairs={{0,4},{4,8},{8,12},{12,0},{1,5},{5,9},{9,13},{13,1},{2,6},{6,10},{... | collective-permute-start | bytes 835592 | tf_op jit(solution)/shard_map/ppermute | solution.py:25
  49.4 16.5 %collective-permute-start.2 = (bf16[272,512]{1,0:T(8,128)(2,1)S(1)}, bf16[272,512]{1,0:T(8,128)(2,1)S(1)}, u32[]{:S(2)}, u32[]{:S(2)}) collective-permute-start(bf16[272,512]{1,0:T(8,128)(2,1)S(1)} %pad_maximum_fusion.own), channel_id=1, source_target_pairs={{0,12},{4,0},{8,4},{12,8},{1,13},{5,1},{9,5},{13,9},{2,14},{6,2},{... | collective-permute-start | bytes 835592 | tf_op jit(solution)/shard_map/ppermute | solution.py:25
  53.3 10.1 %collective-permute-start.5 = (bf16[256,512]{1,0:T(8,128)(2,1)S(1)}, bf16[256,512]{1,0:T(8,128)(2,1)S(1)}, u32[]{:S(2)}, u32[]{:S(2)}) collective-permute-start(bf16[256,512]{1,0:T(8,128)(2,1)S(1)} %reshape.66), channel_id=1, source_target_pairs={{0,32},{32,64},{64,96},{96,0},{1,33},{33,65},{65,97},{97,1},{2,34}... | collective-permute-start | bytes 786440 | tf_op jit(solution)/shard_map/ppermute | solution.py:25
  56.5 9.0 %collective-permute-start.4 = (bf16[256,512]{1,0:T(8,128)(2,1)S(1)}, bf16[256,512]{1,0:T(8,128)(2,1)S(1)}, u32[]{:S(2)}, u32[]{:S(2)}) collective-permute-start(bf16[256,512]{1,0:T(8,128)(2,1)S(1)} %reshape.66), channel_id=1, source_target_pairs={{0,96},{32,0},{64,32},{96,64},{1,97},{33,1},{65,33},{97,65},{2,98}... | collective-permute-start | bytes 786440 | tf_op jit(solution)/shard_map/ppermute | solution.py:25
  59.8 11.5 %collective-permute-start.7 = (bf16[256,512]{1,0:T(8,128)(2,1)S(1)}, bf16[256,512]{1,0:T(8,128)(2,1)S(1)}, u32[]{:S(2)}, u32[]{:S(2)}) collective-permute-start(bf16[256,512]{1,0:T(8,128)(2,1)S(1)} %reshape.66), channel_id=1, source_target_pairs={{0,64},{32,96},{64,0},{96,32},{1,65},{33,97},{65,1},{97,33},{2,66}... | collective-permute-start | bytes 786440 | tf_op jit(solution)/shard_map/ppermute | solution.py:25
  63.4 15.3 %collective-permute-start.6 = (bf16[272,512]{1,0:T(8,128)(2,1)S(1)}, bf16[272,512]{1,0:T(8,128)(2,1)S(1)}, u32[]{:S(2)}, u32[]{:S(2)}) collective-permute-start(bf16[272,512]{1,0:T(8,128)(2,1)S(1)} %pad_maximum_fusion.own), channel_id=1, source_target_pairs={{0,8},{4,12},{8,0},{12,4},{1,9},{5,13},{9,1},{13,5},{2,10},{6,14},... | collective-permute-start | bytes 835592 | tf_op jit(solution)/shard_map/ppermute | solution.py:25
  67.0 14.2 %all-to-all-start.2 = ((bf16[4,256,512]{2,1,0:T(8,128)(2,1)}), bf16[4,256,512]{2,1,0:T(8,128)(2,1)S(1)}, u32[]{:S(2)}, u32[]{:S(2)}) async-start(bf16[4,256,512]{2,1,0:T(8,128)(2,1)} %broadcast_in_dim.39), calls=%async_computation.2 | async-start | bytes 2097152 | tf_op jit(solution)/shard_map/all_to_all | solution.py:17
  78.9 2.1 %copy-start = (bf16[4,4,272,512]{3,2,1,0:T(8,128)(2,1)}, bf16[4,4,272,512]{3,2,1,0:T(8,128)(2,1)S(1)}, u32[]{:S(2)}) copy-start(bf16[4,4,272,512]{3,2,1,0:T(8,128)(2,1)S(1)} %shard_map.56) | copy-start | bytes 13369348
  81.7 50.6 %all-to-all-start.3 = ((bf16[4,4,272,512]{3,2,1,0:T(8,128)(2,1)}), bf16[4,4,272,512]{3,2,1,0:T(8,128)(2,1)}, u32[]{:S(2)}, u32[]{:S(2)}) async-start(bf16[4,4,272,512]{3,2,1,0:T(8,128)(2,1)} %copy-done), calls=%async_computation.3 | async-start | bytes 8912896 | tf_op jit(solution)/shard_map/all_to_all | solution.py:17
  86.6 9.9 %copy-start.1 = (bf16[256,512]{1,0:T(8,128)(2,1)S(1)}, bf16[256,512]{1,0:T(8,128)(2,1)}, u32[]{:S(2)}) copy-start(bf16[256,512]{1,0:T(8,128)(2,1)} %param.7) | copy-start | bytes 786436
  87.4 9.1 %collective-permute-start.8 = (bf16[256,512]{1,0:T(8,128)(2,1)S(1)}, bf16[256,512]{1,0:T(8,128)(2,1)S(1)}, u32[]{:S(2)}, u32[]{:S(2)}) collective-permute-start(bf16[256,512]{1,0:T(8,128)(2,1)S(1)} %convolution_convert_fusion), channel_id=1, source_target_pairs={{0,16},{16,0},{1,17},{17,1},{2,18},{18,2},{3,19},{19,3},{4,20},{20... | collective-permute-start | bytes 786440 | tf_op jit(solution)/shard_map/ppermute | solution.py:37
  96.7 19.6 %collective-permute-start.10 = (bf16[128,512]{1,0:T(8,128)(2,1)S(1)}, bf16[128,512]{1,0:T(8,128)(2,1)S(1)}, u32[]{:S(2)}, u32[]{:S(2)}) collective-permute-start(bf16[128,512]{1,0:T(8,128)(2,1)S(1)} %get-tuple-element.37), channel_id=1, source_target_pairs={{0,384},{128,0},{256,128},{384,256},{1,385},{129,1},{257,129},{385... | collective-permute-start | bytes 393224 | tf_op jit(solution)/shard_map/ppermute | solution.py:25
  100.8 19.1 %collective-permute-start.11 = (bf16[128,512]{1,0:T(8,128)(2,1)S(1)}, bf16[128,512]{1,0:T(8,128)(2,1)S(1)}, u32[]{:S(2)}, u32[]{:S(2)}) collective-permute-start(bf16[128,512]{1,0:T(8,128)(2,1)S(1)} %get-tuple-element.38), channel_id=1, source_target_pairs={{0,128},{128,256},{256,384},{384,0},{1,129},{129,257},{257,385},{3... | collective-permute-start | bytes 393224 | tf_op jit(solution)/shard_map/ppermute | solution.py:25
  105.9 20.9 %collective-permute-start.9 = (bf16[128,512]{1,0:T(8,128)(2,1)S(1)}, bf16[128,512]{1,0:T(8,128)(2,1)S(1)}, u32[]{:S(2)}, u32[]{:S(2)}) collective-permute-start(bf16[128,512]{1,0:T(8,128)(2,1)S(1)} %get-tuple-element.38), channel_id=1, source_target_pairs={{0,384},{128,0},{256,128},{384,256},{1,385},{129,1},{257,129},{385... | collective-permute-start | bytes 393224 | tf_op jit(solution)/shard_map/ppermute | solution.py:25
  110.0 28.1 %collective-permute-start.12 = (bf16[128,512]{1,0:T(8,128)(2,1)S(1)}, bf16[128,512]{1,0:T(8,128)(2,1)S(1)}, u32[]{:S(2)}, u32[]{:S(2)}) collective-permute-start(bf16[128,512]{1,0:T(8,128)(2,1)S(1)} %get-tuple-element.37), channel_id=1, source_target_pairs={{0,128},{128,256},{256,384},{384,0},{1,129},{129,257},{257,385},{3... | collective-permute-start | bytes 393224 | tf_op jit(solution)/shard_map/ppermute | solution.py:25
  116.3 21.8 %collective-permute-start.14 = (bf16[128,512]{1,0:T(8,128)(2,1)S(1)}, bf16[128,512]{1,0:T(8,128)(2,1)S(1)}, u32[]{:S(2)}, u32[]{:S(2)}) collective-permute-start(bf16[128,512]{1,0:T(8,128)(2,1)S(1)} %collective-permute-done.10.after_b), channel_id=1, source_target_pairs={{0,384},{128,0},{256,128},{384,256},{1,385},{129,1},{257,129},{385... | collective-permute-start | bytes 393224 | tf_op jit(solution)/shard_map/ppermute | solution.py:25
  119.9 24.1 %collective-permute-start.13 = (bf16[128,512]{1,0:T(8,128)(2,1)S(1)}, bf16[128,512]{1,0:T(8,128)(2,1)S(1)}, u32[]{:S(2)}, u32[]{:S(2)}) collective-permute-start(bf16[128,512]{1,0:T(8,128)(2,1)S(1)} %collective-permute-done.11.before_a), channel_id=1, source_target_pairs={{0,128},{128,256},{256,384},{384,0},{1,129},{129,257},{257,385},{3... | collective-permute-start | bytes 393224 | tf_op jit(solution)/shard_map/ppermute | solution.py:25
  144.7 5.8 %collective-permute-start.15 = (bf16[4,256,512]{2,1,0:T(8,128)(2,1)S(1)}, bf16[4,256,512]{2,1,0:T(8,128)(2,1)S(1)}, u32[]{:S(2)}, u32[]{:S(2)}) collective-permute-start(bf16[4,256,512]{2,1,0:T(8,128)(2,1)S(1)} %shard_map.59), channel_id=1, source_target_pairs={{0,16},{16,0},{1,17},{17,1},{2,18},{18,2},{3,19},{19,3},{4,20},{20... | collective-permute-start | bytes 3145736 | tf_op jit(solution)/shard_map/ppermute | solution.py:37
  151.9 21.0 %all-to-all-start.4 = ((bf16[4,256,512]{2,1,0:T(8,128)(2,1)}), bf16[4,256,512]{2,1,0:T(8,128)(2,1)S(1)}, u32[]{:S(2)}, u32[]{:S(2)}) async-start(bf16[4,256,512]{2,1,0:T(8,128)(2,1)} %add_convert_fusion), calls=%async_computation.4 | async-start | bytes 2097152 | tf_op jit(solution)/shard_map/all_to_all | solution.py:17
